TPU v7x, 32 devices: a whole 2x2x4 slice. The times are simulated.
32 devices in a mesh: row: 2 (over x), col: 4 (over z), depth: 4 (over y, core).
Axes of the slice: x: 2, y: 2, z: 4, core: 2. Of those that a mesh axis runs over, the one named last changes fastest.
Arguments:
- k_parts: bfloat16 [2, 1024, 1024], P(None, 'row', 'col'), as said below
- p_parts: bfloat16 [2, 1024, 1024], P(None, 'row', 'col'), as said below
- k_mask: int32 [16, 16], P('row', 'col'), may hold values from 0 to 1, as said below
- p_mask: int32 [16, 16], P('row', 'col'), may hold values from 0 to 1, as said below
- atoms: int32 [16], replicated, may hold values from 0 to 3, as said below
- classes: int32 [4, 4], replicated, may hold values from 0 to 3
- rates: float32 [4], replicated, may hold values from 0.5 to 8
Outputs:
- derivative: float32 [2, 1024, 1024], P(None, ('row', 'depth'), 'col')
Inputs may be any that keep to these rules, and one draw needn't show every extreme that they name: k_parts[0] is symmetric and k_parts[1] antisymmetric, so the Kohn-Sham matrix is Hermitian. p_parts[0] is symmetric and p_parts[1] antisymmetric, so the density matrix is Hermitian. `k_mask`: symmetric; every diagonal tile is kept; each tile row keeps a band of tiles around the diagonal of its own half-width, from 0 to 4 tiles, besides scattered tiles further away. `p_mask`: symmetric; every diagonal tile is kept; each tile row keeps a band of tiles around the diagonal of its own half-width, from 0 to 4 tiles, besides scattered tiles further away. `atoms`: never falling along the tiles; every atom block holds at least one tile.
All inputs are finite; a program needn't handle non-finite values.
Results may differ from a plain program's by a relative error of at most 0.0003.
Values may be sent and summed in bfloat16 or wider, within the bound.
No kernel may reach another device: no remote copies, remote signals or barrier semaphores. Data moves between devices by JAX's collectives and lax.ppermute only.
A program may use at most 64 MiB of HBM per device.

v0:
```python
import functools

import jax
import jax.numpy as jnp
from jax import lax
from jax.experimental import pallas as pl
from jax.experimental.pallas import tpu as pltpu
from jax.sharding import PartitionSpec as P

TILE = 64

HBM = pl.BlockSpec(memory_space=pltpu.HBM)
SMEM = pl.BlockSpec(memory_space=pltpu.SMEM)
VMEM = pl.BlockSpec(memory_space=pltpu.VMEM)


def params(*shapes):
    total = sum(functools.reduce(lambda a, b: a * b, s) * w for s, w in shapes)
    return pltpu.CompilerParams(vmem_limit_bytes=2 * total + (4 << 20))


def tile_row(mask_ref, tile, width, dtype):
    lanes = lax.broadcasted_iota(jnp.int32, (1, width), 1) // TILE
    row = jnp.zeros((1, width), jnp.float32)
    for place in range(width // TILE):
        row = jnp.where(lanes == place, mask_ref[place, tile].astype(jnp.float32), row)
    return row.astype(dtype)


def fetch_masks(sources, masks, sems):
    copies = [
        pltpu.make_async_copy(ref, masks.at[i], sems.at[i]) for i, ref in enumerate(sources)
    ]
    for copy in copies:
        copy.start()
    return copies


def rows_kernel(places, first_mask, second_mask, first_ref, second_ref, *refs):
    out_refs = refs[:-4]
    held, masks, sems, mask_sems = refs[-4:]
    rows, width = held.shape[1:]
    each = 4 // len(out_refs)
    first = lax.rem(lax.axis_index("depth"), places) * rows
    mask_copies = fetch_masks((first_mask, second_mask), masks, mask_sems)
    span = pl.ds(pl.multiple_of(first, rows), rows)
    copies = [
        pltpu.make_async_copy(ref.at[:, span, :], held.at[pl.ds(2 * i, 2)], sems.at[i])
        for i, ref in enumerate((first_ref, second_ref))
    ]
    for copy in copies:
        copy.start()
    for copy in mask_copies:
        copy.wait()
    for i, copy in enumerate(copies):
        copy.wait()
        for tile in range(rows // TILE):
            factor = tile_row(masks.at[i], first // TILE + tile, width, held.dtype)
            at = pl.ds(tile * TILE, TILE)
            for part in (2 * i, 2 * i + 1):
                out_refs[part // each][part % each, at, :] = held[part, at, :] * factor


def mask_rows(first_mask, second_mask, first_parts, second_parts, places, arrays, name):
    here, width = first_parts.shape[1:]
    shape, dtype = (4, here // places, width), first_parts.dtype
    return pl.pallas_call(
        functools.partial(rows_kernel, places),
        in_specs=[HBM] * 4,
        out_specs=[VMEM] * arrays,
        out_shape=[jax.ShapeDtypeStruct((4 // arrays,) + shape[1:], dtype)] * arrays,
        scratch_shapes=[
            pltpu.VMEM(shape, dtype),
            pltpu.SMEM((2,) + first_mask.shape, first_mask.dtype),
            pltpu.SemaphoreType.DMA((2,)),
            pltpu.SemaphoreType.DMA((2,)),
        ],
        name=name,
    )(first_mask, second_mask, first_parts, second_parts)


def local_kernel(
    atoms,
    classes,
    rates,
    k_mask,
    p_mask,
    k_ref,
    p_ref,
    strip,
    near,
    damp,
    held,
    own,
    masks,
    sems,
    mask_sems,
):
    here, width = near.shape[1:]
    out_rows = damp.shape[1]
    row, col, layer = (lax.axis_index(a) for a in ("row", "col", "depth"))
    mask_copies = fetch_masks((k_mask, p_mask), masks, mask_sems)
    own_copy = pltpu.make_async_copy(strip.at[pl.ds(2, 2)], own, sems.at[2])
    copies = [
        pltpu.make_async_copy(ref, held.at[pl.ds(2 * i, 2)], sems.at[i])
        for i, ref in enumerate((p_ref, k_ref))
    ]
    for copy in copies + [own_copy]:
        copy.start()
    for copy in mask_copies:
        copy.wait()
    for i, copy in enumerate(copies):
        copy.wait()
        for tile in range(here // TILE):
            factor = tile_row(masks.at[1 - i], tile, width, held.dtype)
            at = pl.ds(tile * TILE, TILE)
            for part in (2 * i, 2 * i + 1):
                near[part, at, :] = held[part, at, :] * factor
    own_copy.wait()
    lanes = lax.broadcasted_iota(jnp.int32, (1, width), 1) // TILE
    row_tiles, col_tiles = out_rows // TILE, width // TILE
    first = (row * lax.axis_size("depth") + layer) * row_tiles
    for tile in range(row_tiles):
        at = pl.ds(tile * TILE, TILE)
        atom_row = atoms[first + tile]
        gamma = jnp.zeros((1, width), jnp.float32)
        for spot in range(col_tiles):
            atom_col = atoms[col * col_tiles + spot]
            rate = jnp.where(atom_row != atom_col, rates[classes[atom_row, atom_col]], 0.0)
            gamma = jnp.where(lanes == spot, rate, gamma)
        for part in range(2):
            damp[part, at, :] = gamma * own[part, at, :].astype(jnp.float32)


def local_part(k_mask, p_mask, atoms, classes, rates, k_parts, p_parts, strip):
    here, width = k_parts.shape[1:]
    out_rows, dtype = strip.shape[1], strip.dtype
    return pl.pallas_call(
        local_kernel,
        in_specs=[SMEM] * 3 + [HBM] * 5,
        out_specs=[VMEM] * 2,
        out_shape=[
            jax.ShapeDtypeStruct((4, here, width), dtype),
            jax.ShapeDtypeStruct((2, out_rows, width), jnp.float32),
        ],
        scratch_shapes=[
            pltpu.VMEM((4, here, width), dtype),
            pltpu.VMEM((2, out_rows, width), dtype),
            pltpu.SMEM((2,) + k_mask.shape, k_mask.dtype),
            pltpu.SemaphoreType.DMA((3,)),
            pltpu.SemaphoreType.DMA((2,)),
        ],
        cost_estimate=pl.CostEstimate(
            flops=8 * here * width, bytes_accessed=20 * here * width, transcendentals=0
        ),
        name="local_part",
    )(atoms, classes, rates, k_mask, p_mask, k_parts, p_parts, strip)


def place_left(left, ref, at, rows):
    k_re, k_im, p_re, p_im = ref[0], ref[1], ref[2], ref[3]
    top, low = pl.ds(0, rows), pl.ds(rows, rows)
    left[0, top, at] = k_re
    left[0, low, at] = k_im
    left[1, top, at] = -k_im
    left[1, low, at] = k_re
    left[2, top, at] = -p_re
    left[2, low, at] = -p_im
    left[3, top, at] = p_im
    left[3, low, at] = -p_re


def share_place(row, layer, index, rows_n, split, here, rows):
    other = lax.rem(row - index // split - 1 + rows_n, rows_n)
    return other * here + (lax.rem(layer, split) ^ (index % split)) * rows


def add_product(total, left, at_left, right, at_right):
    value = total[...]
    each = 4 // len(right)
    for slot in range(4):
        value += jnp.dot(
            left[slot, :, at_left],
            right[slot // each][slot % each, at_right, :],
            preferred_element_type=jnp.float32,
        )
    total[...] = value


def early_kernel(cols_n, near, own, *refs):
    blocks = refs[:-2]
    ups, downs = blocks[: cols_n // 2 - 1], blocks[cols_n // 2 - 1 :]
    left, total = refs[-2:]
    out_rows, width = own.shape[1:]
    here = near.shape[1]
    row, col = lax.axis_index("row"), lax.axis_index("col")

    def columns(shift):
        block = lax.rem(col + shift + cols_n, cols_n)
        return pl.ds(pl.multiple_of(block * width, width), width)

    place_left(left, own, columns(0), out_rows)
    for step, ref in enumerate(ups, 1):
        place_left(left, ref, columns(-step), out_rows)
    for step, ref in enumerate(downs, 1):
        place_left(left, ref, columns(step), out_rows)
    left[:, :, columns(-(cols_n // 2))] = jnp.zeros((4, 2 * out_rows, width), left.dtype)
    total[...] = jnp.zeros_like(total)
    at = pl.ds(pl.multiple_of(row * here, here), here)
    add_product(total, left, at, [near], slice(None))


def early_product(near, strip, blocks, cols_n):
    out_rows, width = strip.shape[1:]
    here = near.shape[1]
    left, total = (4, 2 * out_rows, cols_n * width), (2 * out_rows, width)
    operands = [near, strip] + blocks
    return pl.pallas_call(
        functools.partial(early_kernel, cols_n),
        in_specs=[VMEM] * len(operands),
        out_specs=[VMEM, VMEM],
        out_shape=[
            jax.ShapeDtypeStruct(left, near.dtype),
            jax.ShapeDtypeStruct(total, jnp.float32),
        ],
        compiler_params=params((near.shape, 2), (left, 4), (total, 8)),
        cost_estimate=pl.CostEstimate(
            flops=2 * 8 * out_rows * here * width * 40,
            bytes_accessed=left[0] * left[1] * left[2] * 4,
            transcendentals=0,
        ),
        name="early_product",
    )(*operands)


def product_kernel(rows_n, cols_n, split, damp, near, left, early, last, *refs):
    shares = refs[:-3]
    out_ref, left_last, total = refs[-3:]
    out_rows, width = last.shape[1:]
    here = near.shape[1]
    row, layer = lax.axis_index("row"), lax.axis_index("depth")
    place_left(left_last, last, pl.ds(0, width), out_rows)
    total[...] = early[...]
    rights = [(row * here, here, [near])]
    for index in range(len(shares) // 2):
        pair = shares[2 * index : 2 * index + 2]
        rows = pair[0].shape[1]
        first = share_place(row, layer, index, rows_n, split, here, rows)
        rights.append((first, rows, pair))
        at = pl.ds(pl.multiple_of(first, rows), rows)
        add_product(total, left, at, pair, slice(None))
    start = lax.rem(lax.axis_index("col") + cols_n - cols_n // 2, cols_n) * width
    for first, rows, right in rights:

        @pl.when((start >= first) & (start < first + rows))
        def _():
            at = pl.ds(pl.multiple_of(start - first, width), width)
            add_product(total, left_last, slice(None), right, at)

    out_ref[0] = total[pl.ds(out_rows, out_rows), :] - damp[0]
    out_ref[1] = -total[pl.ds(0, out_rows), :] - damp[1]


def body(k_parts, p_parts, k_mask, p_mask, atoms, classes, rates):
    rows_n, cols_n, depth = (lax.axis_size(a) for a in ("row", "col", "depth"))
    here, width = k_parts.shape[1:]
    out_rows = here // depth
    split = 2 if depth % 2 == 0 else 1
    k_mask, p_mask = k_mask.T, p_mask.T
    (strip,) = mask_rows(k_mask, p_mask, k_parts, p_parts, depth, 1, "mask_strip")
    share = mask_rows(p_mask, k_mask, p_parts, k_parts, split, 2, "mask_share")
    near, damp = local_part(k_mask, p_mask, atoms, classes, rates, k_parts, p_parts, strip)
    ups, downs = [strip], [strip]
    for step in range(1, cols_n // 2 + 1):
        ups.append(lax.ppermute(ups[-1], "col", [(i, (i + 1) % cols_n) for i in range(cols_n)]))
    for step in range(1, cols_n - cols_n // 2):
        downs.append(lax.ppermute(downs[-1], "col", [(i, (i - 1) % cols_n) for i in range(cols_n)]))
    shares = []
    for shift in range(1, rows_n):
        perm = [(i, (i + shift) % rows_n) for i in range(rows_n)]
        got = [lax.ppermute(part, "row", perm) for part in share]
        shares += got
        if split == 2:
            swap = [(i, i ^ 1) for i in range(depth)]
            shares += [lax.ppermute(part, "depth", swap) for part in got]
    blocks = ups[1:-1] + downs[1:]
    left, early = early_product(near, strip, blocks, cols_n)
    operands = [damp, near, left, early, ups[-1]] + shares
    block, total = (4, 2 * out_rows, width), (2 * out_rows, width)
    return pl.pallas_call(
        functools.partial(product_kernel, rows_n, cols_n, split),
        in_specs=[VMEM] * len(operands),
        out_specs=VMEM,
        out_shape=jax.ShapeDtypeStruct((2, out_rows, width), jnp.float32),
        scratch_shapes=[pltpu.VMEM(block, strip.dtype), pltpu.VMEM(total, jnp.float32)],
        compiler_params=params((near.shape, 2 * rows_n), (left.shape, 2), (block, 4), (total, 16)),
        name="commutator",
    )(*operands)


def solution(mesh):
    return jax.shard_map(
        body,
        mesh=mesh,
        in_specs=(
            P(None, "row", "col"),
            P(None, "row", "col"),
            P("row", "col"),
            P("row", "col"),
            P(),
            P(),
            P(),
        ),
        out_specs=P(None, ("row", "depth"), "col"),
        check_vma=False,
    )
```

profile of v0, /device:TPU:0, one launch (start us, length us, event | category | flops | bytes accessed | tf_op | source)
XLA Modules:
  0.0 26.1 jit_solution(17939296196851068658)
XLA Ops:
  0.0 1.7 %mask_strip.1.strip.own = bf16[4,128,256]{2,1,0:T(8,128)(2,1)} custom-call(s32[4,8]{1,0:T(4,128)} %bitcast.2, s32[4,8]{1,0:T(4,128)} %bitcast.5, bf16[2,512,256]{2,1,0:T(8,128)(2,1)} %second_ref.3, bf16[2,512,256]{2,1,0:T(8,128)(2,1)} %first_ref.3), custom_call_target="tpu_custom_call" | custom-call | tf_op jit(solution)/shard_map/mask_strip/pallas_call | solution.py:67
  1.7 0.0 copy-start.2
  1.7 3.1 %collective-permute-start = (bf16[4,128,256]{2,1,0:T(8,128)(2,1)}, bf16[4,128,256]{2,1,0:T(8,128)(2,1)S(1)}, u32[]{:S(2)}, u32[]{:S(2)}) collective-permute-start(bf16[4,128,256]{2,1,0:T(8,128)(2,1)} %mask_strip.1.strip.own), channel_id=1, source_target_pairs={{0,4},{4,8},{8,12},{12,0},{1,5},{5,9},{9,13},{13,1},{2,6},{6,10},{... | collective-permute-start | bytes 786440 | tf_op jit(solution)/shard_map/ppermute | solution.py:275
  4.8 1.9 %mask_share.1 = (bf16[2,256,256]{2,1,0:T(8,128)(2,1)}, bf16[2,256,256]{2,1,0:T(8,128)(2,1)}) custom-call(s32[4,8]{1,0:T(4,128)} %bitcast.6, s32[4,8]{1,0:T(4,128)} %bitcast.3, bf16[2,512,256]{2,1,0:T(8,128)(2,1)} %first_ref.3, bf16[2,512,256]{2,1,0:T(8,128)(2,1)} %second_ref.3), custom_call_target="tpu_custom_call" | custom-call | tf_op jit(solution)/shard_map/mask_share/pallas_call | solution.py:67
  6.7 1.6 %collective-permute-start.3 = (bf16[2,256,256]{2,1,0:T(8,128)(2,1)}, bf16[2,256,256]{2,1,0:T(8,128)(2,1)S(1)}, u32[]{:S(2)}, u32[]{:S(2)}) collective-permute-start(bf16[2,256,256]{2,1,0:T(8,128)(2,1)} %get-tuple-element.15), channel_id=1, source_target_pairs={{0,16},{16,0},{1,17},{17,1},{2,18},{18,2},{3,19},{19,3},{4,20},{20... | collective-permute-start | bytes 786440 | tf_op jit(solution)/shard_map/ppermute | solution.py:281
  8.3 0.5 %collective-permute-start.4 = (bf16[2,256,256]{2,1,0:T(8,128)(2,1)}, bf16[2,256,256]{2,1,0:T(8,128)(2,1)S(1)}, u32[]{:S(2)}, u32[]{:S(2)}) collective-permute-start(bf16[2,256,256]{2,1,0:T(8,128)(2,1)} %get-tuple-element.16), channel_id=1, source_target_pairs={{0,16},{16,0},{1,17},{17,1},{2,18},{18,2},{3,19},{19,3},{4,20},{20... | collective-permute-start | bytes 786440 | tf_op jit(solution)/shard_map/ppermute | solution.py:281
  8.8 2.1 %collective-permute-start.1 = (bf16[4,128,256]{2,1,0:T(8,128)(2,1)}, bf16[4,128,256]{2,1,0:T(8,128)(2,1)S(1)}, u32[]{:S(2)}, u32[]{:S(2)}) collective-permute-start(bf16[4,128,256]{2,1,0:T(8,128)(2,1)} %mask_strip.1.strip.own), channel_id=1, source_target_pairs={{0,12},{4,0},{8,4},{12,8},{1,13},{5,1},{9,5},{13,9},{2,14},{6,2},{... | collective-permute-start | bytes 786440 | tf_op jit(solution)/shard_map/ppermute | solution.py:277
  10.9 3.1 %local_part.1 = (bf16[4,512,256]{2,1,0:T(8,128)(2,1)}, f32[2,128,256]{2,1,0:T(8,128)}) custom-call(s32[16]{0:T(128)} %atoms.1, s32[4,4]{1,0:T(4,128)} %classes.1, f32[4]{0:T(128)} %rates.1, s32[4,8]{1,0:T(4,128)} %bitcast.4, s32[4,8]{1,0:T(4,128)} %bitcast.7, bf16[2,512,256]{2,1,0:T(8,128)(2,1)} %second_ref.3, bf16[2,512,256]{2,1,0:T(8,128)(2,1)} %first_ref.3, ...), custom_call_target="tpu_custom_call" | custom-call | flops 1048576 | bytes 2621440 | tf_op jit(solution)/shard_map/local_part/pallas_call | solution.py:138
  14.0 0.1 collective-permute-done.refs_0_
  14.0 0.0 collective-permute-start.2
  14.0 2.2 %collective-permute-done.3.refs_0_ = bf16[2,256,256]{2,1,0:T(8,128)(2,1)S(1)} collective-permute-done((bf16[2,256,256]{2,1,0:T(8,128)(2,1)}, bf16[2,256,256]{2,1,0:T(8,128)(2,1)S(1)}, u32[]{:S(2)}, u32[]{:S(2)}) %collective-permute-start.3) | collective-permute-done | bytes 262176 | tf_op jit(solution)/shard_map/ppermute | solution.py:281
  16.2 0.0 collective-permute-start.5
  16.2 4.1 %collective-permute-done.4.refs_1_ = bf16[2,256,256]{2,1,0:T(8,128)(2,1)S(1)} collective-permute-done((bf16[2,256,256]{2,1,0:T(8,128)(2,1)}, bf16[2,256,256]{2,1,0:T(8,128)(2,1)S(1)}, u32[]{:S(2)}, u32[]{:S(2)}) %collective-permute-start.4) | collective-permute-done | bytes 262176 | tf_op jit(solution)/shard_map/ppermute | solution.py:281
  20.4 0.0 collective-permute-start.6
  20.4 0.0 collective-permute-done.1.refs_1_
  20.4 0.0 copy-done.2
  20.4 0.0 copy-start
  20.4 1.2 %copy-done = bf16[4,512,256]{2,1,0:T(8,128)(2,1)S(1)} copy-done((bf16[4,512,256]{2,1,0:T(8,128)(2,1)S(1)}, bf16[4,512,256]{2,1,0:T(8,128)(2,1)}, u32[]{:S(2)}) %copy-start) | copy-done | bytes 1048600
  21.6 0.0 copy-start.1
  21.6 0.0 copy-start.3
  21.6 0.7 %early_product.1 = (bf16[4,256,1024]{2,1,0:T(8,128)(2,1)S(1)}, f32[256,256]{1,0:T(8,128)S(1)}) custom-call(bf16[4,512,256]{2,1,0:T(8,128)(2,1)S(1)} %copy-done, bf16[4,128,256]{2,1,0:T(8,128)(2,1)S(1)} %copy-done.2, bf16[4,128,256]{2,1,0:T(8,128)(2,1)S(1)} %collective-permute-done.refs_0_, bf16[4,128,256]{2,1,0:T(8,128)(2,1)S(1)} %collective-permute-done.1.refs_1_), custom_call_target="tpu_custom_call" | custom-call | flops 10737418240 | bytes 4194304 | tf_op jit(solution)/shard_map/early_product/pallas_call | solution.py:218
  22.3 2.3 %collective-permute-done.2.last = bf16[4,128,256]{2,1,0:T(8,128)(2,1)S(1)} collective-permute-done((bf16[4,128,256]{2,1,0:T(8,128)(2,1)S(1)}, bf16[4,128,256]{2,1,0:T(8,128)(2,1)S(1)}, u32[]{:S(2)}, u32[]{:S(2)}) %collective-permute-start.2) | collective-permute-done | bytes 262176 | tf_op jit(solution)/shard_map/ppermute | solution.py:275
  24.6 0.0 collective-permute-done.5.refs_2_
  24.6 0.0 collective-permute-done.6.refs_3_
  24.6 0.0 copy-done.1
  24.6 0.0 copy-done.3
  24.6 1.5 %commutator.1 = f32[2,128,256]{2,1,0:T(8,128)} custom-call(f32[2,128,256]{2,1,0:T(8,128)S(1)} %copy-done.3, bf16[4,512,256]{2,1,0:T(8,128)(2,1)S(1)} %copy-done.1, bf16[4,256,1024]{2,1,0:T(8,128)(2,1)S(1)} %get-tuple-element.13.left, f32[256,256]{1,0:T(8,128)S(1)} %get-tuple-element.14.early, bf16[4,128,256]{2,1,0:T(8,128)(2,1)S(1)} %collective-permute-done.2.last, ...), custom_call_target="tpu_custom_call" | custom-call | tf_op jit(solution)/shard_map/commutator/pallas_call | solution.py:290
Async XLA Ops:
  1.7 18.6 %copy-start.2 = (bf16[4,128,256]{2,1,0:T(8,128)(2,1)S(1)}, bf16[4,128,256]{2,1,0:T(8,128)(2,1)}, u32[]{:S(2)}) copy-start(bf16[4,128,256]{2,1,0:T(8,128)(2,1)} %mask_strip.1.strip.own) | copy-start | bytes 786436
  1.7 12.3 %collective-permute-start = (bf16[4,128,256]{2,1,0:T(8,128)(2,1)}, bf16[4,128,256]{2,1,0:T(8,128)(2,1)S(1)}, u32[]{:S(2)}, u32[]{:S(2)}) collective-permute-start(bf16[4,128,256]{2,1,0:T(8,128)(2,1)} %mask_strip.1.strip.own), channel_id=1, source_target_pairs={{0,4},{4,8},{8,12},{12,0},{1,5},{5,9},{9,13},{13,1},{2,6},{6,10},{... | collective-permute-start | bytes 786440 | tf_op jit(solution)/shard_map/ppermute | solution.py:275
  6.7 9.5 %collective-permute-start.3 = (bf16[2,256,256]{2,1,0:T(8,128)(2,1)}, bf16[2,256,256]{2,1,0:T(8,128)(2,1)S(1)}, u32[]{:S(2)}, u32[]{:S(2)}) collective-permute-start(bf16[2,256,256]{2,1,0:T(8,128)(2,1)} %get-tuple-element.15), channel_id=1, source_target_pairs={{0,16},{16,0},{1,17},{17,1},{2,18},{18,2},{3,19},{19,3},{4,20},{20... | collective-permute-start | bytes 786440 | tf_op jit(solution)/shard_map/ppermute | solution.py:281
  8.3 12.1 %collective-permute-start.4 = (bf16[2,256,256]{2,1,0:T(8,128)(2,1)}, bf16[2,256,256]{2,1,0:T(8,128)(2,1)S(1)}, u32[]{:S(2)}, u32[]{:S(2)}) collective-permute-start(bf16[2,256,256]{2,1,0:T(8,128)(2,1)} %get-tuple-element.16), channel_id=1, source_target_pairs={{0,16},{16,0},{1,17},{17,1},{2,18},{18,2},{3,19},{19,3},{4,20},{20... | collective-permute-start | bytes 786440 | tf_op jit(solution)/shard_map/ppermute | solution.py:281
  8.8 11.6 %collective-permute-start.1 = (bf16[4,128,256]{2,1,0:T(8,128)(2,1)}, bf16[4,128,256]{2,1,0:T(8,128)(2,1)S(1)}, u32[]{:S(2)}, u32[]{:S(2)}) collective-permute-start(bf16[4,128,256]{2,1,0:T(8,128)(2,1)} %mask_strip.1.strip.own), channel_id=1, source_target_pairs={{0,12},{4,0},{8,4},{12,8},{1,13},{5,1},{9,5},{13,9},{2,14},{6,2},{... | collective-permute-start | bytes 786440 | tf_op jit(solution)/shard_map/ppermute | solution.py:277
  14.0 10.6 %collective-permute-start.2 = (bf16[4,128,256]{2,1,0:T(8,128)(2,1)S(1)}, bf16[4,128,256]{2,1,0:T(8,128)(2,1)S(1)}, u32[]{:S(2)}, u32[]{:S(2)}) collective-permute-start(bf16[4,128,256]{2,1,0:T(8,128)(2,1)S(1)} %collective-permute-done.refs_0_), channel_id=1, source_target_pairs={{0,4},{4,8},{8,12},{12,0},{1,5},{5,9},{9,13},{13,1},{2,6},{6,10},{... | collective-permute-start | bytes 786440 | tf_op jit(solution)/shard_map/ppermute | solution.py:275
  16.2 8.4 %collective-permute-start.5 = (bf16[2,256,256]{2,1,0:T(8,128)(2,1)S(1)}, bf16[2,256,256]{2,1,0:T(8,128)(2,1)S(1)}, u32[]{:S(2)}, u32[]{:S(2)}) collective-permute-start(bf16[2,256,256]{2,1,0:T(8,128)(2,1)S(1)} %collective-permute-done.3.refs_0_), channel_id=1, source_target_pairs={{0,1},{1,0},{2,3},{3,2},{4,5},{5,4},{6,7},{7,6},{8,9},{9,8},{10,11... | collective-permute-start | bytes 786440 | tf_op jit(solution)/shard_map/ppermute | solution.py:285
  20.4 4.2 %collective-permute-start.6 = (bf16[2,256,256]{2,1,0:T(8,128)(2,1)S(1)}, bf16[2,256,256]{2,1,0:T(8,128)(2,1)S(1)}, u32[]{:S(2)}, u32[]{:S(2)}) collective-permute-start(bf16[2,256,256]{2,1,0:T(8,128)(2,1)S(1)} %collective-permute-done.4.refs_1_), channel_id=1, source_target_pairs={{0,1},{1,0},{2,3},{3,2},{4,5},{5,4},{6,7},{7,6},{8,9},{9,8},{10,11... | collective-permute-start | bytes 786440 | tf_op jit(solution)/shard_map/ppermute | solution.py:285
  20.4 1.2 %copy-start = (bf16[4,512,256]{2,1,0:T(8,128)(2,1)S(1)}, bf16[4,512,256]{2,1,0:T(8,128)(2,1)}, u32[]{:S(2)}) copy-start(bf16[4,512,256]{2,1,0:T(8,128)(2,1)} %get-tuple-element.12.near) | copy-start | bytes 3145732
  21.6 3.0 %copy-start.1 = (bf16[4,512,256]{2,1,0:T(8,128)(2,1)S(1)}, bf16[4,512,256]{2,1,0:T(8,128)(2,1)}, u32[]{:S(2)}) copy-start(bf16[4,512,256]{2,1,0:T(8,128)(2,1)} %get-tuple-element.12.near) | copy-start | bytes 3145732
  21.6 3.0 %copy-start.3 = (f32[2,128,256]{2,1,0:T(8,128)S(1)}, f32[2,128,256]{2,1,0:T(8,128)}, u32[]{:S(2)}) copy-start(f32[2,128,256]{2,1,0:T(8,128)} %get-tuple-element.11.damp) | copy-start | bytes 786436
where the time goes:
time: 26.4 us; the launch traced here: 26.1 us
  Pallas kernels  8.92 us (34%)
  waiting for transfers between devices  8.69 us (33%)
  starting transfers between devices  7.23 us (27%)
  local copies, waits for them, and re-layouts  1.23 us (5%)
    ppermute x2, waiting for transfers between devices, body(): got = [lax.ppermute(part, 'row', perm) for part in share]  6.32 us
    pallas_call x2, Pallas kernels, mask_rows(): pl.pallas_call(functools.partial(rows_kernel, places), in_specs=[HBM] * 4...  3.6 us
    pallas_call x1, Pallas kernels, local_part(): pl.pallas_call(local_kernel, in_specs=[SMEM] * 3 + [HBM] * 5, out_specs=[...  3.09 us
    ppermute x2, starting transfers between devices, body(): lax.ppermute(ups[-1], 'col', [(i, (i + 1) % cols_n) for i in range(cols_n)])  3.08 us
    ppermute x2, waiting for transfers between devices, body(): lax.ppermute(ups[-1], 'col', [(i, (i + 1) % cols_n) for i in range(cols_n)])  2.37 us
    ppermute x2, starting transfers between devices, body(): got = [lax.ppermute(part, 'row', perm) for part in share]  2.09 us
    ppermute x1, starting transfers between devices, body(): lax.ppermute(downs[-1], 'col', [(i, (i - 1) % cols_n) for i in range(cols...  2.05 us
    pallas_call x1, Pallas kernels, body(): pl.pallas_call(functools.partial(product_kernel, rows_n, cols_n, split),...  1.52 us
  transfers between devices with their start and end apart: 7, of which 4 were waited for; matrix products, arithmetic and copies ran while one was open for 0% of the time, Pallas kernels for 22%

commit v1 on v0

v1 whole, which is shorter than its diff:
```python
import functools

import jax
import jax.numpy as jnp
from jax import lax
from jax.experimental import pallas as pl
from jax.experimental.pallas import tpu as pltpu
from jax.sharding import PartitionSpec as P

TILE = 64

HBM = pl.BlockSpec(memory_space=pltpu.HBM)
SMEM = pl.BlockSpec(memory_space=pltpu.SMEM)
VMEM = pl.BlockSpec(memory_space=pltpu.VMEM)


def params(*shapes):
    total = sum(functools.reduce(lambda a, b: a * b, s) * w for s, w in shapes)
    return pltpu.CompilerParams(vmem_limit_bytes=2 * total + (4 << 20))


def tile_row(mask_ref, tile, width, dtype):
    lanes = lax.broadcasted_iota(jnp.int32, (1, width), 1) // TILE
    row = jnp.zeros((1, width), jnp.float32)
    for place in range(width // TILE):
        row = jnp.where(lanes == place, mask_ref[place, tile].astype(jnp.float32), row)
    return row.astype(dtype)


def fetch_masks(sources, masks, sems):
    copies = [
        pltpu.make_async_copy(ref, masks.at[i], sems.at[i]) for i, ref in enumerate(sources)
    ]
    for copy in copies:
        copy.start()
    return copies


def rows_kernel(places, first_mask, second_mask, first_ref, second_ref, *refs):
    out_refs = refs[:-6]
    held, masked, masks, sems, out_sems, mask_sems = refs[-6:]
    rows, width = held.shape[1:]
    each = 4 // len(out_refs)
    unit = masked.shape[1]
    first = lax.rem(lax.axis_index("depth"), places) * rows
    span = pl.ds(pl.multiple_of(first, rows), rows)
    mask_copies = fetch_masks((first_mask, second_mask), masks, mask_sems)
    copies = [
        pltpu.make_async_copy(ref.at[:, span, :], held.at[pl.ds(2 * i, 2)], sems.at[i])
        for i, ref in enumerate((first_ref, second_ref))
    ]
    for copy in copies:
        copy.start()
    for copy in mask_copies:
        copy.wait()
    out_copies = []
    for i, copy in enumerate(copies):
        copy.wait()
        for tile in range(rows // TILE):
            factor = tile_row(masks.at[i], first // TILE + tile, width, held.dtype)
            at = pl.ds(tile * TILE, TILE)
            block, within = divmod(tile * TILE, unit)
            for part in range(2):
                spot = 2 * (i * (rows // unit) + block) + part
                masked[spot, pl.ds(within, TILE), :] = held[2 * i + part, at, :] * factor
        size = 2 * (rows // unit)
        target = out_refs[i] if each == 2 else out_refs[0].at[pl.ds(i * size, size)]
        out_copies.append(
            pltpu.make_async_copy(masked.at[pl.ds(i * size, size)], target, out_sems.at[i])
        )
        out_copies[-1].start()
    for copy in out_copies:
        copy.wait()


def mask_rows(first_mask, second_mask, first_parts, second_parts, places, arrays, name):
    here, width = first_parts.shape[1:]
    rows, dtype = here // places, first_parts.dtype
    unit = min(rows, width)
    count = 4 * (rows // unit)
    return pl.pallas_call(
        functools.partial(rows_kernel, places),
        in_specs=[HBM] * 4,
        out_specs=[HBM] * arrays,
        out_shape=[jax.ShapeDtypeStruct((count // arrays, unit, width), dtype)] * arrays,
        scratch_shapes=[
            pltpu.VMEM((4, rows, width), dtype),
            pltpu.VMEM((count, unit, width), dtype),
            pltpu.SMEM((2,) + first_mask.shape, first_mask.dtype),
            pltpu.SemaphoreType.DMA((2,)),
            pltpu.SemaphoreType.DMA((2,)),
            pltpu.SemaphoreType.DMA((2,)),
        ],
        name=name,
    )(first_mask, second_mask, first_parts, second_parts)


def local_kernel(
    k_mask,
    p_mask,
    atoms_ref,
    classes_ref,
    rates_ref,
    k_ref,
    p_ref,
    strip,
    near_ref,
    damp,
    held,
    near,
    own,
    masks,
    atoms,
    classes,
    rates,
    sems,
    out_sems,
    small_sems,
):
    here, width = held.shape[1:]
    out_rows = damp.shape[1]
    row, col, layer = (lax.axis_index(a) for a in ("row", "col", "depth"))
    small = fetch_masks((k_mask, p_mask), masks, small_sems)
    copies = [
        pltpu.make_async_copy(ref, held.at[pl.ds(2 * i, 2)], sems.at[i])
        for i, ref in enumerate((p_ref, k_ref))
    ]
    own_copy = pltpu.make_async_copy(strip.at[pl.ds(2, 2)], own, sems.at[2])
    tables = [
        pltpu.make_async_copy(source, target, small_sems.at[2 + i])
        for i, (source, target) in enumerate(
            ((atoms_ref, atoms), (classes_ref, classes), (rates_ref, rates))
        )
    ]
    for copy in copies + [own_copy] + tables:
        copy.start()
    for copy in small + copies:
        copy.wait()
    out_copies = []
    for block in range(here // width):
        for tile in range(block * width // TILE, (block + 1) * width // TILE):
            at, spot = pl.ds(tile * TILE, TILE), pl.ds(tile * TILE - block * width, TILE)
            for i in range(2):
                factor = tile_row(masks.at[1 - i], tile, width, held.dtype)
                for part in (2 * i, 2 * i + 1):
                    near[4 * block + part, spot, :] = held[part, at, :] * factor
        span = pl.ds(4 * block, 4)
        out_copies.append(
            pltpu.make_async_copy(near.at[span], near_ref.at[span], out_sems.at[block])
        )
        out_copies[-1].start()
    for copy in [own_copy] + tables:
        copy.wait()
    lanes = lax.broadcasted_iota(jnp.int32, (1, width), 1) // TILE
    row_tiles, col_tiles = out_rows // TILE, width // TILE
    first = (row * lax.axis_size("depth") + layer) * row_tiles
    for tile in range(row_tiles):
        at = pl.ds(tile * TILE, TILE)
        atom_row = atoms[first + tile]
        gamma = jnp.zeros((1, width), jnp.float32)
        for spot in range(col_tiles):
            atom_col = atoms[col * col_tiles + spot]
            rate = jnp.where(atom_row != atom_col, rates[classes[atom_row, atom_col]], 0.0)
            gamma = jnp.where(lanes == spot, rate, gamma)
        for part in range(2):
            damp[part, at, :] = gamma * own[part, at, :].astype(jnp.float32)
    for copy in out_copies:
        copy.wait()


def local_part(k_mask, p_mask, atoms, classes, rates, k_parts, p_parts, strip):
    here, width = k_parts.shape[1:]
    out_rows, dtype = strip.shape[1], strip.dtype
    blocks = here // width
    near = (4 * blocks, width, width)
    return pl.pallas_call(
        local_kernel,
        in_specs=[HBM] * 8,
        out_specs=[HBM, VMEM],
        out_shape=[
            jax.ShapeDtypeStruct(near, dtype),
            jax.ShapeDtypeStruct((2, out_rows, width), jnp.float32),
        ],
        scratch_shapes=[
            pltpu.VMEM((4, here, width), dtype),
            pltpu.VMEM(near, dtype),
            pltpu.VMEM((2, out_rows, width), dtype),
            pltpu.SMEM((2,) + k_mask.shape, k_mask.dtype),
            pltpu.SMEM(atoms.shape, atoms.dtype),
            pltpu.SMEM(classes.shape, classes.dtype),
            pltpu.SMEM(rates.shape, rates.dtype),
            pltpu.SemaphoreType.DMA((3,)),
            pltpu.SemaphoreType.DMA((blocks,)),
            pltpu.SemaphoreType.DMA((5,)),
        ],
        cost_estimate=pl.CostEstimate(
            flops=8 * here * width, bytes_accessed=20 * here * width, transcendentals=0
        ),
        name="local_part",
    )(k_mask, p_mask, atoms, classes, rates, k_parts, p_parts, strip)


def place_left(left, ref, block):
    rows, width = ref.shape[1:]
    k_re, k_im, p_re, p_im = ref[0], ref[1], ref[2], ref[3]
    for half, parts in enumerate(((k_re, -k_im, -p_re, p_im), (k_im, k_re, -p_im, -p_re))):
        for slot, part in enumerate(parts):
            at = pl.multiple_of((4 * block + slot) * width, width)
            left[pl.ds(half * rows, rows), pl.ds(at, width)] = part


def share_block(row, layer, index, rows_n, split, here, size):
    other = lax.rem(row - index // split - 1 + rows_n, rows_n)
    return other * here + (lax.rem(layer, split) ^ (index % split)) * size


def products(left, block, right, first, count):
    each = 4 // len(right)
    width = right[0].shape[1]
    steps = [(0, count)] if each == 4 else [(step, 1) for step in range(count)]
    found = []
    for step, size in steps:
        for half, ref in enumerate(right):
            at = pl.multiple_of((4 * (block + step) + half * each) * width, width)
            value = ref[pl.ds((first + step) * each, size * each)]
            found.append(
                jnp.dot(
                    left[:, pl.ds(at, size * each * width)],
                    value.reshape(size * each * width, width),
                    preferred_element_type=jnp.float32,
                )
            )
    return sum(found[1:], found[0])


def early_kernel(cols_n, near, own, *refs):
    blocks = refs[:-2]
    ups, downs = blocks[: cols_n // 2 - 1], blocks[cols_n // 2 - 1 :]
    left, total = refs[-2:]
    width = own.shape[2]
    row, col = lax.axis_index("row"), lax.axis_index("col")
    place_left(left, own, col)
    for step, ref in enumerate(ups, 1):
        place_left(left, ref, lax.rem(col - step + cols_n, cols_n))
    for step, ref in enumerate(downs, 1):
        place_left(left, ref, lax.rem(col + step, cols_n))
    last = pl.multiple_of(lax.rem(col + cols_n - cols_n // 2, cols_n) * 4 * width, width)
    left[:, pl.ds(last, 4 * width)] = jnp.zeros((left.shape[0], 4 * width), left.dtype)
    count = near.shape[0] // 4
    total[...] = products(left, row * count, [near], 0, count)


def early_product(near, strip, blocks, cols_n):
    out_rows, width = strip.shape[1:]
    left, total = (2 * out_rows, cols_n * 4 * width), (2 * out_rows, width)
    operands = [near, strip] + blocks
    return pl.pallas_call(
        functools.partial(early_kernel, cols_n),
        in_specs=[VMEM] * len(operands),
        out_specs=[VMEM, VMEM],
        out_shape=[
            jax.ShapeDtypeStruct(left, near.dtype),
            jax.ShapeDtypeStruct(total, jnp.float32),
        ],
        compiler_params=params((near.shape, 2), (left, 4), (total, 8)),
        cost_estimate=pl.CostEstimate(
            flops=4 * out_rows * near.shape[0] * width * width * 40,
            bytes_accessed=left[0] * left[1] * 4,
            transcendentals=0,
        ),
        name="early_product",
    )(*operands)


def product_kernel(rows_n, cols_n, split, damp, near, left, early, last, *refs):
    shares = refs[:-3]
    out_ref, left_last, total = refs[-3:]
    out_rows = last.shape[1]
    row, layer = lax.axis_index("row"), lax.axis_index("depth")
    place_left(left_last, last, 0)
    here = near.shape[0] // 4
    rights = [(row * here, here, [near])]
    value = early[...]
    for index in range(len(shares) // 2):
        pair = shares[2 * index : 2 * index + 2]
        size = pair[0].shape[0] // 2
        block = share_block(row, layer, index, rows_n, split, here, size)
        rights.append((block, size, pair))
        value += products(left, block, pair, 0, size)
    total[...] = value
    wanted = lax.rem(lax.axis_index("col") + cols_n - cols_n // 2, cols_n)
    for block, size, right in rights:

        @pl.when((wanted >= block) & (wanted < block + size))
        def _():
            total[...] += products(left_last, 0, right, wanted - block, 1)

    out_ref[0] = total[pl.ds(out_rows, out_rows), :] - damp[0]
    out_ref[1] = -total[pl.ds(0, out_rows), :] - damp[1]


def body(k_parts, p_parts, k_mask, p_mask, atoms, classes, rates):
    rows_n, cols_n, depth = (lax.axis_size(a) for a in ("row", "col", "depth"))
    here, width = k_parts.shape[1:]
    out_rows = here // depth
    split = 2 if depth % 2 == 0 else 1
    k_mask, p_mask = k_mask.T, p_mask.T
    (strip,) = mask_rows(k_mask, p_mask, k_parts, p_parts, depth, 1, "mask_strip")
    share = mask_rows(p_mask, k_mask, p_parts, k_parts, split, 2, "mask_share")
    ups, downs = [strip], [strip]
    for step in range(1, cols_n // 2 + 1):
        ups.append(lax.ppermute(ups[-1], "col", [(i, (i + 1) % cols_n) for i in range(cols_n)]))
    for step in range(1, cols_n - cols_n // 2):
        downs.append(lax.ppermute(downs[-1], "col", [(i, (i - 1) % cols_n) for i in range(cols_n)]))
    near, damp = local_part(
        k_mask, p_mask, atoms, classes, rates, k_parts, p_parts, strip
    )
    shares = []
    for shift in range(1, rows_n):
        perm = [(i, (i + shift) % rows_n) for i in range(rows_n)]
        got = [lax.ppermute(part, "row", perm) for part in share]
        shares += got
        if split == 2:
            swap = [(i, i ^ 1) for i in range(depth)]
            shares += [lax.ppermute(part, "depth", swap) for part in got]
    blocks = ups[1:-1] + downs[1:]
    left, early = early_product(near, strip, blocks, cols_n)
    operands = [damp, near, left, early, ups[-1]] + shares
    block, total = (2 * out_rows, 4 * width), (2 * out_rows, width)
    return pl.pallas_call(
        functools.partial(product_kernel, rows_n, cols_n, split),
        in_specs=[VMEM] * len(operands),
        out_specs=VMEM,
        out_shape=jax.ShapeDtypeStruct((2, out_rows, width), jnp.float32),
        scratch_shapes=[pltpu.VMEM(block, strip.dtype), pltpu.VMEM(total, jnp.float32)],
        compiler_params=params((near.shape, 2 * rows_n), (left.shape, 2), (block, 4), (total, 16)),
        name="commutator",
    )(*operands)


def solution(mesh):
    return jax.shard_map(
        body,
        mesh=mesh,
        in_specs=(
            P(None, "row", "col"),
            P(None, "row", "col"),
            P("row", "col"),
            P("row", "col"),
            P(),
            P(),
            P(),
        ),
        out_specs=P(None, ("row", "depth"), "col"),
        check_vma=False,
    )
```

time: 26.4 us -> 26.3 us (level)
  transfers between devices with their start and end apart: 7 -> 7, of which waited for: 4 -> 4; matrix products, arithmetic and copies ran while one was open for 0% -> 0% of each run, Pallas kernels for 22% -> 21%
where the time goes in v1:
time: 26.3 us; the launch traced here: 26.1 us
  waiting for transfers between devices  8.85 us (34%)
  Pallas kernels  8.75 us (33%)
  starting transfers between devices  7.23 us (27%)
  local copies, waits for them, and re-layouts  1.23 us (5%)
    ppermute x2, waiting for transfers between devices, body(): got = [lax.ppermute(part, 'row', perm) for part in share]  6.22 us
    pallas_call x2, Pallas kernels, mask_rows(): pl.pallas_call(functools.partial(rows_kernel, places), in_specs=[HBM] * 4...  3.53 us
    ppermute x2, starting transfers between devices, body(): lax.ppermute(ups[-1], 'col', [(i, (i + 1) % cols_n) for i in range(cols_n)])  3.08 us
    pallas_call x1, Pallas kernels, local_part(): pl.pallas_call(local_kernel, in_specs=[HBM] * 8, out_specs=[HBM, VMEM], o...  3.02 us
    ppermute x2, waiting for transfers between devices, body(): lax.ppermute(ups[-1], 'col', [(i, (i + 1) % cols_n) for i in range(cols_n)])  2.62 us
    ppermute x2, starting transfers between devices, body(): got = [lax.ppermute(part, 'row', perm) for part in share]  2.09 us
    ppermute x1, starting transfers between devices, body(): lax.ppermute(downs[-1], 'col', [(i, (i - 1) % cols_n) for i in range(cols...  2.05 us
    pallas_call x1, Pallas kernels, body(): pl.pallas_call(functools.partial(product_kernel, rows_n, cols_n, split),...  1.54 us
  transfers between devices with their start and end apart: 7, of which 4 were waited for; matrix products, arithmetic and copies ran while one was open for 0% of the time, Pallas kernels for 21%

profile of v1, /device:TPU:0, one launch (start us, length us, event | category | flops | bytes accessed | tf_op | source)
XLA Modules:
  0.0 26.1 jit_solution(17917690988498572004)
XLA Ops:
  0.0 1.7 %mask_strip.1.strip.own = bf16[4,128,256]{2,1,0:T(8,128)(2,1)} custom-call(s32[4,8]{1,0:T(4,128)} %bitcast.2, s32[4,8]{1,0:T(4,128)} %bitcast.5, bf16[2,512,256]{2,1,0:T(8,128)(2,1)} %second_ref.3, bf16[2,512,256]{2,1,0:T(8,128)(2,1)} %first_ref.3), custom_call_target="tpu_custom_call" | custom-call | tf_op jit(solution)/shard_map/mask_strip/pallas_call | solution.py:81
  1.7 0.0 copy-start.2
  1.7 3.1 %collective-permute-start = (bf16[4,128,256]{2,1,0:T(8,128)(2,1)}, bf16[4,128,256]{2,1,0:T(8,128)(2,1)S(1)}, u32[]{:S(2)}, u32[]{:S(2)}) collective-permute-start(bf16[4,128,256]{2,1,0:T(8,128)(2,1)} %mask_strip.1.strip.own), channel_id=1, source_target_pairs={{0,4},{4,8},{8,12},{12,0},{1,5},{5,9},{9,13},{13,1},{2,6},{6,10},{... | collective-permute-start | bytes 786440 | tf_op jit(solution)/shard_map/ppermute | solution.py:312
  4.8 1.8 %mask_share.1 = (bf16[2,256,256]{2,1,0:T(8,128)(2,1)}, bf16[2,256,256]{2,1,0:T(8,128)(2,1)}) custom-call(s32[4,8]{1,0:T(4,128)} %bitcast.6, s32[4,8]{1,0:T(4,128)} %bitcast.3, bf16[2,512,256]{2,1,0:T(8,128)(2,1)} %first_ref.3, bf16[2,512,256]{2,1,0:T(8,128)(2,1)} %second_ref.3), custom_call_target="tpu_custom_call" | custom-call | tf_op jit(solution)/shard_map/mask_share/pallas_call | solution.py:81
  6.6 1.6 %collective-permute-start.3 = (bf16[2,256,256]{2,1,0:T(8,128)(2,1)}, bf16[2,256,256]{2,1,0:T(8,128)(2,1)S(1)}, u32[]{:S(2)}, u32[]{:S(2)}) collective-permute-start(bf16[2,256,256]{2,1,0:T(8,128)(2,1)} %get-tuple-element.15), channel_id=1, source_target_pairs={{0,16},{16,0},{1,17},{17,1},{2,18},{18,2},{3,19},{19,3},{4,20},{20... | collective-permute-start | bytes 786440 | tf_op jit(solution)/shard_map/ppermute | solution.py:321
  8.2 0.5 %collective-permute-start.4 = (bf16[2,256,256]{2,1,0:T(8,128)(2,1)}, bf16[2,256,256]{2,1,0:T(8,128)(2,1)S(1)}, u32[]{:S(2)}, u32[]{:S(2)}) collective-permute-start(bf16[2,256,256]{2,1,0:T(8,128)(2,1)} %get-tuple-element.16), channel_id=1, source_target_pairs={{0,16},{16,0},{1,17},{17,1},{2,18},{18,2},{3,19},{19,3},{4,20},{20... | collective-permute-start | bytes 786440 | tf_op jit(solution)/shard_map/ppermute | solution.py:321
  8.7 2.1 %collective-permute-start.1 = (bf16[4,128,256]{2,1,0:T(8,128)(2,1)}, bf16[4,128,256]{2,1,0:T(8,128)(2,1)S(1)}, u32[]{:S(2)}, u32[]{:S(2)}) collective-permute-start(bf16[4,128,256]{2,1,0:T(8,128)(2,1)} %mask_strip.1.strip.own), channel_id=1, source_target_pairs={{0,12},{4,0},{8,4},{12,8},{1,13},{5,1},{9,5},{13,9},{2,14},{6,2},{... | collective-permute-start | bytes 786440 | tf_op jit(solution)/shard_map/ppermute | solution.py:314
  10.8 3.0 %local_part.1 = (bf16[8,256,256]{2,1,0:T(8,128)(2,1)}, f32[2,128,256]{2,1,0:T(8,128)}) custom-call(s32[4,8]{1,0:T(4,128)} %bitcast.4, s32[4,8]{1,0:T(4,128)} %bitcast.7, s32[16]{0:T(128)} %atoms_ref.1, s32[4,4]{1,0:T(4,128)} %classes_ref.1, f32[4]{0:T(128)} %rates_ref.1, bf16[2,512,256]{2,1,0:T(8,128)(2,1)} %second_ref.3, bf16[2,512,256]{2,1,0:T(8,128)(2,1)} %first_ref.3, ...), custom_call_target="tpu_custom_call" | custom-call | flops 1048576 | bytes 2621440 | tf_op jit(solution)/shard_map/local_part/pallas_call | solution.py:176
  13.8 0.3 collective-permute-done.refs_0_
  14.1 0.0 collective-permute-start.2
  14.1 2.1 %collective-permute-done.3.refs_0_ = bf16[2,256,256]{2,1,0:T(8,128)(2,1)S(1)} collective-permute-done((bf16[2,256,256]{2,1,0:T(8,128)(2,1)}, bf16[2,256,256]{2,1,0:T(8,128)(2,1)S(1)}, u32[]{:S(2)}, u32[]{:S(2)}) %collective-permute-start.3) | collective-permute-done | bytes 262176 | tf_op jit(solution)/shard_map/ppermute | solution.py:321
  16.1 0.0 collective-permute-start.5
  16.1 4.1 %collective-permute-done.4.refs_1_ = bf16[2,256,256]{2,1,0:T(8,128)(2,1)S(1)} collective-permute-done((bf16[2,256,256]{2,1,0:T(8,128)(2,1)}, bf16[2,256,256]{2,1,0:T(8,128)(2,1)S(1)}, u32[]{:S(2)}, u32[]{:S(2)}) %collective-permute-start.4) | collective-permute-done | bytes 262176 | tf_op jit(solution)/shard_map/ppermute | solution.py:321
  20.3 0.0 collective-permute-start.6
  20.3 0.0 collective-permute-done.1.refs_1_
  20.3 0.0 copy-done.2
  20.3 0.0 copy-start
  20.3 1.2 %copy-done = bf16[8,256,256]{2,1,0:T(8,128)(2,1)S(1)} copy-done((bf16[8,256,256]{2,1,0:T(8,128)(2,1)S(1)}, bf16[8,256,256]{2,1,0:T(8,128)(2,1)}, u32[]{:S(2)}) %copy-start) | copy-done | bytes 1048600
  21.5 0.0 copy-start.1
  21.5 0.0 copy-start.3
  21.5 0.7 %early_product.1 = (bf16[256,4096]{1,0:T(8,128)(2,1)S(1)}, f32[256,256]{1,0:T(8,128)S(1)}) custom-call(bf16[8,256,256]{2,1,0:T(8,128)(2,1)S(1)} %copy-done, bf16[4,128,256]{2,1,0:T(8,128)(2,1)S(1)} %copy-done.2, bf16[4,128,256]{2,1,0:T(8,128)(2,1)S(1)} %collective-permute-done.refs_0_, bf16[4,128,256]{2,1,0:T(8,128)(2,1)S(1)} %collective-permute-done.1.refs_1_), custom_call_target="tpu_custom_call" | custom-call | flops 10737418240 | bytes 4194304 | tf_op jit(solution)/shard_map/early_product/pallas_call | solution.py:257
  22.2 2.4 %collective-permute-done.2.last = bf16[4,128,256]{2,1,0:T(8,128)(2,1)S(1)} collective-permute-done((bf16[4,128,256]{2,1,0:T(8,128)(2,1)S(1)}, bf16[4,128,256]{2,1,0:T(8,128)(2,1)S(1)}, u32[]{:S(2)}, u32[]{:S(2)}) %collective-permute-start.2) | collective-permute-done | bytes 262176 | tf_op jit(solution)/shard_map/ppermute | solution.py:312
  24.6 0.0 collective-permute-done.5.refs_2_
  24.6 0.0 collective-permute-done.6.refs_3_
  24.6 0.0 copy-done.1
  24.6 0.0 copy-done.3
  24.6 1.5 %commutator.1 = f32[2,128,256]{2,1,0:T(8,128)} custom-call(f32[2,128,256]{2,1,0:T(8,128)S(1)} %copy-done.3, bf16[8,256,256]{2,1,0:T(8,128)(2,1)S(1)} %copy-done.1, bf16[256,4096]{1,0:T(8,128)(2,1)S(1)} %get-tuple-element.13.left, f32[256,256]{1,0:T(8,128)S(1)} %get-tuple-element.14.early, bf16[4,128,256]{2,1,0:T(8,128)(2,1)S(1)} %collective-permute-done.2.last, ...), custom_call_target="tpu_custom_call" | custom-call | tf_op jit(solution)/shard_map/commutator/pallas_call | solution.py:330
Async XLA Ops:
  1.7 18.6 %copy-start.2 = (bf16[4,128,256]{2,1,0:T(8,128)(2,1)S(1)}, bf16[4,128,256]{2,1,0:T(8,128)(2,1)}, u32[]{:S(2)}) copy-start(bf16[4,128,256]{2,1,0:T(8,128)(2,1)} %mask_strip.1.strip.own) | copy-start | bytes 786436
  1.7 12.4 %collective-permute-start = (bf16[4,128,256]{2,1,0:T(8,128)(2,1)}, bf16[4,128,256]{2,1,0:T(8,128)(2,1)S(1)}, u32[]{:S(2)}, u32[]{:S(2)}) collective-permute-start(bf16[4,128,256]{2,1,0:T(8,128)(2,1)} %mask_strip.1.strip.own), channel_id=1, source_target_pairs={{0,4},{4,8},{8,12},{12,0},{1,5},{5,9},{9,13},{13,1},{2,6},{6,10},{... | collective-permute-start | bytes 786440 | tf_op jit(solution)/shard_map/ppermute | solution.py:312
  6.6 9.5 %collective-permute-start.3 = (bf16[2,256,256]{2,1,0:T(8,128)(2,1)}, bf16[2,256,256]{2,1,0:T(8,128)(2,1)S(1)}, u32[]{:S(2)}, u32[]{:S(2)}) collective-permute-start(bf16[2,256,256]{2,1,0:T(8,128)(2,1)} %get-tuple-element.15), channel_id=1, source_target_pairs={{0,16},{16,0},{1,17},{17,1},{2,18},{18,2},{3,19},{19,3},{4,20},{20... | collective-permute-start | bytes 786440 | tf_op jit(solution)/shard_map/ppermute | solution.py:321
  8.2 12.1 %collective-permute-start.4 = (bf16[2,256,256]{2,1,0:T(8,128)(2,1)}, bf16[2,256,256]{2,1,0:T(8,128)(2,1)S(1)}, u32[]{:S(2)}, u32[]{:S(2)}) collective-permute-start(bf16[2,256,256]{2,1,0:T(8,128)(2,1)} %get-tuple-element.16), channel_id=1, source_target_pairs={{0,16},{16,0},{1,17},{17,1},{2,18},{18,2},{3,19},{19,3},{4,20},{20... | collective-permute-start | bytes 786440 | tf_op jit(solution)/shard_map/ppermute | solution.py:321
  8.7 11.6 %collective-permute-start.1 = (bf16[4,128,256]{2,1,0:T(8,128)(2,1)}, bf16[4,128,256]{2,1,0:T(8,128)(2,1)S(1)}, u32[]{:S(2)}, u32[]{:S(2)}) collective-permute-start(bf16[4,128,256]{2,1,0:T(8,128)(2,1)} %mask_strip.1.strip.own), channel_id=1, source_target_pairs={{0,12},{4,0},{8,4},{12,8},{1,13},{5,1},{9,5},{13,9},{2,14},{6,2},{... | collective-permute-start | bytes 786440 | tf_op jit(solution)/shard_map/ppermute | solution.py:314
  14.1 10.5 %collective-permute-start.2 = (bf16[4,128,256]{2,1,0:T(8,128)(2,1)S(1)}, bf16[4,128,256]{2,1,0:T(8,128)(2,1)S(1)}, u32[]{:S(2)}, u32[]{:S(2)}) collective-permute-start(bf16[4,128,256]{2,1,0:T(8,128)(2,1)S(1)} %collective-permute-done.refs_0_), channel_id=1, source_target_pairs={{0,4},{4,8},{8,12},{12,0},{1,5},{5,9},{9,13},{13,1},{2,6},{6,10},{... | collective-permute-start | bytes 786440 | tf_op jit(solution)/shard_map/ppermute | solution.py:312
  16.1 8.4 %collective-permute-start.5 = (bf16[2,256,256]{2,1,0:T(8,128)(2,1)S(1)}, bf16[2,256,256]{2,1,0:T(8,128)(2,1)S(1)}, u32[]{:S(2)}, u32[]{:S(2)}) collective-permute-start(bf16[2,256,256]{2,1,0:T(8,128)(2,1)S(1)} %collective-permute-done.3.refs_0_), channel_id=1, source_target_pairs={{0,1},{1,0},{2,3},{3,2},{4,5},{5,4},{6,7},{7,6},{8,9},{9,8},{10,11... | collective-permute-start | bytes 786440 | tf_op jit(solution)/shard_map/ppermute | solution.py:325
  20.3 4.3 %collective-permute-start.6 = (bf16[2,256,256]{2,1,0:T(8,128)(2,1)S(1)}, bf16[2,256,256]{2,1,0:T(8,128)(2,1)S(1)}, u32[]{:S(2)}, u32[]{:S(2)}) collective-permute-start(bf16[2,256,256]{2,1,0:T(8,128)(2,1)S(1)} %collective-permute-done.4.refs_1_), channel_id=1, source_target_pairs={{0,1},{1,0},{2,3},{3,2},{4,5},{5,4},{6,7},{7,6},{8,9},{9,8},{10,11... | collective-permute-start | bytes 786440 | tf_op jit(solution)/shard_map/ppermute | solution.py:325
  20.3 1.2 %copy-start = (bf16[8,256,256]{2,1,0:T(8,128)(2,1)S(1)}, bf16[8,256,256]{2,1,0:T(8,128)(2,1)}, u32[]{:S(2)}) copy-start(bf16[8,256,256]{2,1,0:T(8,128)(2,1)} %get-tuple-element.12.near) | copy-start | bytes 3145732
  21.5 3.1 %copy-start.1 = (bf16[8,256,256]{2,1,0:T(8,128)(2,1)S(1)}, bf16[8,256,256]{2,1,0:T(8,128)(2,1)}, u32[]{:S(2)}) copy-start(bf16[8,256,256]{2,1,0:T(8,128)(2,1)} %get-tuple-element.12.near) | copy-start | bytes 3145732
  21.5 3.1 %copy-start.3 = (f32[2,128,256]{2,1,0:T(8,128)S(1)}, f32[2,128,256]{2,1,0:T(8,128)}, u32[]{:S(2)}) copy-start(f32[2,128,256]{2,1,0:T(8,128)} %get-tuple-element.11.damp) | copy-start | bytes 786436

commit v2 on v1

--- a/solution.py
+++ b/solution.py
@@ -209,6 +209,24 @@
             left[pl.ds(half * rows, rows), pl.ds(at, width)] = part
 
 
+def relay_kernel(block, out):
+    out[...] = block[...]
+
+
+def relay(block):
+    return pl.pallas_call(
+        relay_kernel,
+        in_specs=[VMEM],
+        out_specs=VMEM,
+        out_shape=jax.ShapeDtypeStruct(block.shape, block.dtype),
+        compiler_params=params((block.shape, 4)),
+        cost_estimate=pl.CostEstimate(
+            flops=100000000, bytes_accessed=4 * block.size, transcendentals=0
+        ),
+        name="relay",
+    )(block)
+
+
 def share_block(row, layer, index, rows_n, split, here, size):
     other = lax.rem(row - index // split - 1 + rows_n, rows_n)
     return other * here + (lax.rem(layer, split) ^ (index % split)) * size
@@ -272,7 +290,32 @@
     )(*operands)
 
 
-def product_kernel(rows_n, cols_n, split, damp, near, left, early, last, *refs):
+def shares_kernel(rows_n, split, here, left, early, *refs):
+    shares, total = refs[:-1], refs[-1]
+    row, layer = lax.axis_index("row"), lax.axis_index("depth")
+    value = early[...]
+    for index in range(len(shares) // 2):
+        pair = shares[2 * index : 2 * index + 2]
+        size = pair[0].shape[0] // 2
+        block = share_block(row, layer, index, rows_n, split, here, size)
+        value += products(left, block, pair, 0, size)
+    total[...] = value
+
+
+def shares_product(left, early, shares, rows_n, split, here):
+    operands = [left, early] + shares
+    return pl.pallas_call(
+        functools.partial(shares_kernel, rows_n, split, here),
+        in_specs=[VMEM] * len(operands),
+        out_specs=VMEM,
+        out_shape=jax.ShapeDtypeStruct(early.shape, early.dtype),
+        compiler_params=params((left.shape, 4), (early.shape, 12)),
+        cost_estimate=pl.CostEstimate(flops=1000000, bytes_accessed=1000000, transcendentals=0),
+        name="shares_product",
+    )(*operands)
+
+
+def product_kernel(rows_n, cols_n, split, damp, near, middle, last, *refs):
     shares = refs[:-3]
     out_ref, left_last, total = refs[-3:]
     out_rows = last.shape[1]
@@ -280,20 +323,17 @@
     place_left(left_last, last, 0)
     here = near.shape[0] // 4
     rights = [(row * here, here, [near])]
-    value = early[...]
     for index in range(len(shares) // 2):
         pair = shares[2 * index : 2 * index + 2]
         size = pair[0].shape[0] // 2
         block = share_block(row, layer, index, rows_n, split, here, size)
         rights.append((block, size, pair))
-        value += products(left, block, pair, 0, size)
-    total[...] = value
     wanted = lax.rem(lax.axis_index("col") + cols_n - cols_n // 2, cols_n)
     for block, size, right in rights:
 
         @pl.when((wanted >= block) & (wanted < block + size))
         def _():
-            total[...] += products(left_last, 0, right, wanted - block, 1)
+            total[...] = middle[...] + products(left_last, 0, right, wanted - block, 1)
 
     out_ref[0] = total[pl.ds(out_rows, out_rows), :] - damp[0]
     out_ref[1] = -total[pl.ds(0, out_rows), :] - damp[1]
@@ -309,7 +349,8 @@
     share = mask_rows(p_mask, k_mask, p_parts, k_parts, split, 2, "mask_share")
     ups, downs = [strip], [strip]
     for step in range(1, cols_n // 2 + 1):
-        ups.append(lax.ppermute(ups[-1], "col", [(i, (i + 1) % cols_n) for i in range(cols_n)]))
+        block = ups[-1] if step == 1 else relay(ups[-1])
+        ups.append(lax.ppermute(block, "col", [(i, (i + 1) % cols_n) for i in range(cols_n)]))
     for step in range(1, cols_n - cols_n // 2):
         downs.append(lax.ppermute(downs[-1], "col", [(i, (i - 1) % cols_n) for i in range(cols_n)]))
     near, damp = local_part(
@@ -325,7 +366,8 @@
             shares += [lax.ppermute(part, "depth", swap) for part in got]
     blocks = ups[1:-1] + downs[1:]
     left, early = early_product(near, strip, blocks, cols_n)
-    operands = [damp, near, left, early, ups[-1]] + shares
+    middle = shares_product(left, early, shares, rows_n, split, here // width)
+    operands = [damp, near, middle, ups[-1]] + shares
     block, total = (2 * out_rows, 4 * width), (2 * out_rows, width)
     return pl.pallas_call(
         functools.partial(product_kernel, rows_n, cols_n, split),

time: 26.3 us -> 25.9 us (0.985)
  waiting for transfers between devices: 8.85 us -> 8.27 us
    ppermute x2, waiting for transfers between devices: 2.62 us -> 2.12 us  [body(): lax.ppermute(block, 'col', [(i, (i + 1) % cols_n) for i in range(cols_n)])]
    pallas_call x0 -> x2, Pallas kernels: none -> 0.47 us  [the longest x1 0.45 us: shares_product(): pl.pallas_call(functools.partial(shares_kernel, rows_n, split, here), in_...]
    pallas_call x1, Pallas kernels: 1.54 us -> 1.09 us  [body(): pl.pallas_call(functools.partial(product_kernel, rows_n, cols_n, split),...]
  transfers between devices with their start and end apart: 7 -> 7, of which waited for: 4 -> 4; matrix products, arithmetic and copies ran while one was open for 0% -> 0% of each run, Pallas kernels for 21% -> 23%
where the time goes in v2:
time: 25.9 us; the launch traced here: 25.7 us
  Pallas kernels  8.77 us (34%)
  waiting for transfers between devices  8.27 us (32%)
  starting transfers between devices  7.29 us (28%)
  local copies, waits for them, and re-layouts  1.23 us (5%)
    ppermute x2, waiting for transfers between devices, body(): got = [lax.ppermute(part, 'row', perm) for part in share]  6.14 us
    pallas_call x2, Pallas kernels, mask_rows(): pl.pallas_call(functools.partial(rows_kernel, places), in_specs=[HBM] * 4...  3.53 us
    ppermute x2, starting transfers between devices, body(): lax.ppermute(block, 'col', [(i, (i + 1) % cols_n) for i in range(cols_n)])  3.13 us
    pallas_call x1, Pallas kernels, local_part(): pl.pallas_call(local_kernel, in_specs=[HBM] * 8, out_specs=[HBM, VMEM], o...  3.02 us
    ppermute x2, waiting for transfers between devices, body(): lax.ppermute(block, 'col', [(i, (i + 1) % cols_n) for i in range(cols_n)])  2.12 us
    ppermute x2, starting transfers between devices, body(): got = [lax.ppermute(part, 'row', perm) for part in share]  2.09 us
    ppermute x1, starting transfers between devices, body(): lax.ppermute(downs[-1], 'col', [(i, (i - 1) % cols_n) for i in range(cols...  2.05 us
    unnamed x8, local copies, waits for them, and re-layouts  1.23 us
  transfers between devices with their start and end apart: 7, of which 4 were waited for; matrix products, arithmetic and copies ran while one was open for 0% of the time, Pallas kernels for 23%

profile of v2, /device:TPU:0, one launch (start us, length us, event | category | flops | bytes accessed | tf_op | source)
XLA Modules:
  0.0 25.7 jit_solution(1354874077536044327)
XLA Ops:
  0.0 1.7 %mask_strip.1.strip.own = bf16[4,128,256]{2,1,0:T(8,128)(2,1)} custom-call(s32[4,8]{1,0:T(4,128)} %bitcast.2, s32[4,8]{1,0:T(4,128)} %bitcast.5, bf16[2,512,256]{2,1,0:T(8,128)(2,1)} %second_ref.3, bf16[2,512,256]{2,1,0:T(8,128)(2,1)} %first_ref.3), custom_call_target="tpu_custom_call" | custom-call | tf_op jit(solution)/shard_map/mask_strip/pallas_call | solution.py:81
  1.7 0.0 copy-start.2
  1.7 3.1 %collective-permute-start = (bf16[4,128,256]{2,1,0:T(8,128)(2,1)}, bf16[4,128,256]{2,1,0:T(8,128)(2,1)S(1)}, u32[]{:S(2)}, u32[]{:S(2)}) collective-permute-start(bf16[4,128,256]{2,1,0:T(8,128)(2,1)} %mask_strip.1.strip.own), channel_id=1, source_target_pairs={{0,4},{4,8},{8,12},{12,0},{1,5},{5,9},{9,13},{13,1},{2,6},{6,10},{... | collective-permute-start | bytes 786440 | tf_op jit(solution)/shard_map/ppermute | solution.py:353
  4.8 1.8 %mask_share.1 = (bf16[2,256,256]{2,1,0:T(8,128)(2,1)}, bf16[2,256,256]{2,1,0:T(8,128)(2,1)}) custom-call(s32[4,8]{1,0:T(4,128)} %bitcast.6, s32[4,8]{1,0:T(4,128)} %bitcast.3, bf16[2,512,256]{2,1,0:T(8,128)(2,1)} %first_ref.3, bf16[2,512,256]{2,1,0:T(8,128)(2,1)} %second_ref.3), custom_call_target="tpu_custom_call" | custom-call | tf_op jit(solution)/shard_map/mask_share/pallas_call | solution.py:81
  6.6 1.6 %collective-permute-start.2 = (bf16[2,256,256]{2,1,0:T(8,128)(2,1)}, bf16[2,256,256]{2,1,0:T(8,128)(2,1)S(1)}, u32[]{:S(2)}, u32[]{:S(2)}) collective-permute-start(bf16[2,256,256]{2,1,0:T(8,128)(2,1)} %get-tuple-element.15), channel_id=1, source_target_pairs={{0,16},{16,0},{1,17},{17,1},{2,18},{18,2},{3,19},{19,3},{4,20},{20... | collective-permute-start | bytes 786440 | tf_op jit(solution)/shard_map/ppermute | solution.py:362
  8.2 0.5 %collective-permute-start.3 = (bf16[2,256,256]{2,1,0:T(8,128)(2,1)}, bf16[2,256,256]{2,1,0:T(8,128)(2,1)S(1)}, u32[]{:S(2)}, u32[]{:S(2)}) collective-permute-start(bf16[2,256,256]{2,1,0:T(8,128)(2,1)} %get-tuple-element.16), channel_id=1, source_target_pairs={{0,16},{16,0},{1,17},{17,1},{2,18},{18,2},{3,19},{19,3},{4,20},{20... | collective-permute-start | bytes 786440 | tf_op jit(solution)/shard_map/ppermute | solution.py:362
  8.7 2.1 %collective-permute-start.1 = (bf16[4,128,256]{2,1,0:T(8,128)(2,1)}, bf16[4,128,256]{2,1,0:T(8,128)(2,1)S(1)}, u32[]{:S(2)}, u32[]{:S(2)}) collective-permute-start(bf16[4,128,256]{2,1,0:T(8,128)(2,1)} %mask_strip.1.strip.own), channel_id=1, source_target_pairs={{0,12},{4,0},{8,4},{12,8},{1,13},{5,1},{9,5},{13,9},{2,14},{6,2},{... | collective-permute-start | bytes 786440 | tf_op jit(solution)/shard_map/ppermute | solution.py:355
  10.8 3.0 %local_part.1 = (bf16[8,256,256]{2,1,0:T(8,128)(2,1)}, f32[2,128,256]{2,1,0:T(8,128)}) custom-call(s32[4,8]{1,0:T(4,128)} %bitcast.4, s32[4,8]{1,0:T(4,128)} %bitcast.7, s32[16]{0:T(128)} %atoms_ref.1, s32[4,4]{1,0:T(4,128)} %classes_ref.1, f32[4]{0:T(128)} %rates_ref.1, bf16[2,512,256]{2,1,0:T(8,128)(2,1)} %second_ref.3, bf16[2,512,256]{2,1,0:T(8,128)(2,1)} %first_ref.3, ...), custom_call_target="tpu_custom_call" | custom-call | flops 1048576 | bytes 2621440 | tf_op jit(solution)/shard_map/local_part/pallas_call | solution.py:176
  13.8 0.3 %collective-permute-done.refs_0_.block = bf16[4,128,256]{2,1,0:T(8,128)(2,1)S(1)} collective-permute-done((bf16[4,128,256]{2,1,0:T(8,128)(2,1)}, bf16[4,128,256]{2,1,0:T(8,128)(2,1)S(1)}, u32[]{:S(2)}, u32[]{:S(2)}) %collective-permute-start) | collective-permute-done | bytes 262176 | tf_op jit(solution)/shard_map/ppermute | solution.py:353
  14.1 0.1 collective-permute-start.6
  14.2 2.0 %collective-permute-done.2.refs_0_ = bf16[2,256,256]{2,1,0:T(8,128)(2,1)S(1)} collective-permute-done((bf16[2,256,256]{2,1,0:T(8,128)(2,1)}, bf16[2,256,256]{2,1,0:T(8,128)(2,1)S(1)}, u32[]{:S(2)}, u32[]{:S(2)}) %collective-permute-start.2) | collective-permute-done | bytes 262176 | tf_op jit(solution)/shard_map/ppermute | solution.py:362
  16.1 0.0 collective-permute-start.4
  16.1 4.1 %collective-permute-done.3.refs_1_ = bf16[2,256,256]{2,1,0:T(8,128)(2,1)S(1)} collective-permute-done((bf16[2,256,256]{2,1,0:T(8,128)(2,1)}, bf16[2,256,256]{2,1,0:T(8,128)(2,1)S(1)}, u32[]{:S(2)}, u32[]{:S(2)}) %collective-permute-start.3) | collective-permute-done | bytes 262176 | tf_op jit(solution)/shard_map/ppermute | solution.py:362
  20.3 0.0 collective-permute-start.5
  20.3 0.0 collective-permute-done.1.refs_1_
  20.3 0.0 copy-done.2
  20.3 0.0 copy-start
  20.3 1.2 %copy-done = bf16[8,256,256]{2,1,0:T(8,128)(2,1)S(1)} copy-done((bf16[8,256,256]{2,1,0:T(8,128)(2,1)S(1)}, bf16[8,256,256]{2,1,0:T(8,128)(2,1)}, u32[]{:S(2)}) %copy-start) | copy-done | bytes 1048600
  21.5 0.7 %early_product.1 = (bf16[256,4096]{1,0:T(8,128)(2,1)S(1)}, f32[256,256]{1,0:T(8,128)S(1)}) custom-call(bf16[8,256,256]{2,1,0:T(8,128)(2,1)S(1)} %copy-done, bf16[4,128,256]{2,1,0:T(8,128)(2,1)S(1)} %copy-done.2, bf16[4,128,256]{2,1,0:T(8,128)(2,1)S(1)} %collective-permute-done.refs_0_.block, bf16[4,128,256]{2,1,0:T(8,128)(2,1)S(1)} %collective-permute-done.1.refs_1_), custom_call_target="tpu_custom_call" | custom-call | flops 10737418240 | bytes 4194304 | tf_op jit(solution)/shard_map/early_product/pallas_call | solution.py:275
  22.2 0.0 copy-start.1
  22.2 0.0 copy-start.3
  22.2 0.0 collective-permute-done.4.refs_2_
  22.2 0.0 collective-permute-done.5.refs_3_
  22.2 0.5 %shares_product.1.middle = f32[256,256]{1,0:T(8,128)S(1)} custom-call(bf16[256,4096]{1,0:T(8,128)(2,1)S(1)} %get-tuple-element.13.left, f32[256,256]{1,0:T(8,128)S(1)} %get-tuple-element.14.early, bf16[2,256,256]{2,1,0:T(8,128)(2,1)S(1)} %collective-permute-done.2.refs_0_, bf16[2,256,256]{2,1,0:T(8,128)(2,1)S(1)} %collective-permute-done.3.refs_1_, ...), custom_call_target="tpu_custom_call" | custom-call | flops 1000000 | bytes 1000000 | tf_op jit(solution)/shard_map/shares_product/pallas_call | solution.py:307
  22.7 1.9 %collective-permute-done.6.last = bf16[4,128,256]{2,1,0:T(8,128)(2,1)S(1)} collective-permute-done((bf16[4,128,256]{2,1,0:T(8,128)(2,1)S(1)}, bf16[4,128,256]{2,1,0:T(8,128)(2,1)S(1)}, u32[]{:S(2)}, u32[]{:S(2)}) %collective-permute-start.6) | collective-permute-done | bytes 262176 | tf_op jit(solution)/shard_map/ppermute | solution.py:353
  24.6 0.0 copy-done.1
  24.6 0.0 copy-done.3
  24.6 1.1 %commutator.1 = f32[2,128,256]{2,1,0:T(8,128)} custom-call(f32[2,128,256]{2,1,0:T(8,128)S(1)} %copy-done.3, bf16[8,256,256]{2,1,0:T(8,128)(2,1)S(1)} %copy-done.1, f32[256,256]{1,0:T(8,128)S(1)} %shares_product.1.middle, bf16[4,128,256]{2,1,0:T(8,128)(2,1)S(1)} %collective-permute-done.6.last, bf16[2,256,256]{2,1,0:T(8,128)(2,1)S(1)} %collective-permute-done.2.refs_0_, ...), custom_call_target="tpu_custom_call" | custom-call | tf_op jit(solution)/shard_map/commutator/pallas_call | solution.py:372
  (1 shorter events, 0.0 us)
Async XLA Ops:
  1.7 18.6 %copy-start.2 = (bf16[4,128,256]{2,1,0:T(8,128)(2,1)S(1)}, bf16[4,128,256]{2,1,0:T(8,128)(2,1)}, u32[]{:S(2)}) copy-start(bf16[4,128,256]{2,1,0:T(8,128)(2,1)} %mask_strip.1.strip.own) | copy-start | bytes 786436
  1.7 12.4 %collective-permute-start = (bf16[4,128,256]{2,1,0:T(8,128)(2,1)}, bf16[4,128,256]{2,1,0:T(8,128)(2,1)S(1)}, u32[]{:S(2)}, u32[]{:S(2)}) collective-permute-start(bf16[4,128,256]{2,1,0:T(8,128)(2,1)} %mask_strip.1.strip.own), channel_id=1, source_target_pairs={{0,4},{4,8},{8,12},{12,0},{1,5},{5,9},{9,13},{13,1},{2,6},{6,10},{... | collective-permute-start | bytes 786440 | tf_op jit(solution)/shard_map/ppermute | solution.py:353
  6.6 9.5 %collective-permute-start.2 = (bf16[2,256,256]{2,1,0:T(8,128)(2,1)}, bf16[2,256,256]{2,1,0:T(8,128)(2,1)S(1)}, u32[]{:S(2)}, u32[]{:S(2)}) collective-permute-start(bf16[2,256,256]{2,1,0:T(8,128)(2,1)} %get-tuple-element.15), channel_id=1, source_target_pairs={{0,16},{16,0},{1,17},{17,1},{2,18},{18,2},{3,19},{19,3},{4,20},{20... | collective-permute-start | bytes 786440 | tf_op jit(solution)/shard_map/ppermute | solution.py:362
  8.2 12.1 %collective-permute-start.3 = (bf16[2,256,256]{2,1,0:T(8,128)(2,1)}, bf16[2,256,256]{2,1,0:T(8,128)(2,1)S(1)}, u32[]{:S(2)}, u32[]{:S(2)}) collective-permute-start(bf16[2,256,256]{2,1,0:T(8,128)(2,1)} %get-tuple-element.16), channel_id=1, source_target_pairs={{0,16},{16,0},{1,17},{17,1},{2,18},{18,2},{3,19},{19,3},{4,20},{20... | collective-permute-start | bytes 786440 | tf_op jit(solution)/shard_map/ppermute | solution.py:362
  8.7 11.6 %collective-permute-start.1 = (bf16[4,128,256]{2,1,0:T(8,128)(2,1)}, bf16[4,128,256]{2,1,0:T(8,128)(2,1)S(1)}, u32[]{:S(2)}, u32[]{:S(2)}) collective-permute-start(bf16[4,128,256]{2,1,0:T(8,128)(2,1)} %mask_strip.1.strip.own), channel_id=1, source_target_pairs={{0,12},{4,0},{8,4},{12,8},{1,13},{5,1},{9,5},{13,9},{2,14},{6,2},{... | collective-permute-start | bytes 786440 | tf_op jit(solution)/shard_map/ppermute | solution.py:355
  14.1 10.5 %collective-permute-start.6 = (bf16[4,128,256]{2,1,0:T(8,128)(2,1)S(1)}, bf16[4,128,256]{2,1,0:T(8,128)(2,1)S(1)}, u32[]{:S(2)}, u32[]{:S(2)}) collective-permute-start(bf16[4,128,256]{2,1,0:T(8,128)(2,1)S(1)} %relay.1), channel_id=1, source_target_pairs={{0,4},{4,8},{8,12},{12,0},{1,5},{5,9},{9,13},{13,1},{2,6},{6,10},{... | collective-permute-start | bytes 786440 | tf_op jit(solution)/shard_map/ppermute | solution.py:353
  16.1 6.1 %collective-permute-start.4 = (bf16[2,256,256]{2,1,0:T(8,128)(2,1)S(1)}, bf16[2,256,256]{2,1,0:T(8,128)(2,1)S(1)}, u32[]{:S(2)}, u32[]{:S(2)}) collective-permute-start(bf16[2,256,256]{2,1,0:T(8,128)(2,1)S(1)} %collective-permute-done.2.refs_0_), channel_id=1, source_target_pairs={{0,1},{1,0},{2,3},{3,2},{4,5},{5,4},{6,7},{7,6},{8,9},{9,8},{10,11... | collective-permute-start | bytes 786440 | tf_op jit(solution)/shard_map/ppermute | solution.py:366
  20.3 1.9 %collective-permute-start.5 = (bf16[2,256,256]{2,1,0:T(8,128)(2,1)S(1)}, bf16[2,256,256]{2,1,0:T(8,128)(2,1)S(1)}, u32[]{:S(2)}, u32[]{:S(2)}) collective-permute-start(bf16[2,256,256]{2,1,0:T(8,128)(2,1)S(1)} %collective-permute-done.3.refs_1_), channel_id=1, source_target_pairs={{0,1},{1,0},{2,3},{3,2},{4,5},{5,4},{6,7},{7,6},{8,9},{9,8},{10,11... | collective-permute-start | bytes 786440 | tf_op jit(solution)/shard_map/ppermute | solution.py:366
  20.3 1.2 %copy-start = (bf16[8,256,256]{2,1,0:T(8,128)(2,1)S(1)}, bf16[8,256,256]{2,1,0:T(8,128)(2,1)}, u32[]{:S(2)}) copy-start(bf16[8,256,256]{2,1,0:T(8,128)(2,1)} %get-tuple-element.12.near) | copy-start | bytes 3145732
  22.2 2.4 %copy-start.1 = (bf16[8,256,256]{2,1,0:T(8,128)(2,1)S(1)}, bf16[8,256,256]{2,1,0:T(8,128)(2,1)}, u32[]{:S(2)}) copy-start(bf16[8,256,256]{2,1,0:T(8,128)(2,1)} %get-tuple-element.12.near) | copy-start | bytes 3145732
  22.2 2.4 %copy-start.3 = (f32[2,128,256]{2,1,0:T(8,128)S(1)}, f32[2,128,256]{2,1,0:T(8,128)}, u32[]{:S(2)}) copy-start(f32[2,128,256]{2,1,0:T(8,128)} %get-tuple-element.11.damp) | copy-start | bytes 786436

commit v3 on v2

--- a/solution.py
+++ b/solution.py
@@ -40,35 +40,42 @@
     out_refs = refs[:-6]
     held, masked, masks, sems, out_sems, mask_sems = refs[-6:]
     rows, width = held.shape[1:]
-    each = 4 // len(out_refs)
+    count = out_refs[0].shape[0]
     unit = masked.shape[1]
     first = lax.rem(lax.axis_index("depth"), places) * rows
-    span = pl.ds(pl.multiple_of(first, rows), rows)
     mask_copies = fetch_masks((first_mask, second_mask), masks, mask_sems)
-    copies = [
-        pltpu.make_async_copy(ref.at[:, span, :], held.at[pl.ds(2 * i, 2)], sems.at[i])
-        for i, ref in enumerate((first_ref, second_ref))
-    ]
-    for copy in copies:
-        copy.start()
+    copies = []
+    for i, ref in enumerate((first_ref, second_ref)):
+        for tile in range(rows // TILE):
+            for part in range(2):
+                slot, to = 2 * i + part, pl.ds(tile * TILE, TILE)
+                at = pl.ds(pl.multiple_of(first + tile * TILE, TILE), TILE)
+                copies.append(
+                    pltpu.make_async_copy(
+                        ref.at[part, at], held.at[slot, to], sems.at[len(copies)]
+                    )
+                )
+                copies[-1].start()
     for copy in mask_copies:
         copy.wait()
     out_copies = []
-    for i, copy in enumerate(copies):
-        copy.wait()
+    for i in range(2):
         for tile in range(rows // TILE):
             factor = tile_row(masks.at[i], first // TILE + tile, width, held.dtype)
             at = pl.ds(tile * TILE, TILE)
             block, within = divmod(tile * TILE, unit)
+            to = pl.ds(within, TILE)
             for part in range(2):
+                copies[len(out_copies)].wait()
                 spot = 2 * (i * (rows // unit) + block) + part
-                masked[spot, pl.ds(within, TILE), :] = held[2 * i + part, at, :] * factor
-        size = 2 * (rows // unit)
-        target = out_refs[i] if each == 2 else out_refs[0].at[pl.ds(i * size, size)]
-        out_copies.append(
-            pltpu.make_async_copy(masked.at[pl.ds(i * size, size)], target, out_sems.at[i])
-        )
-        out_copies[-1].start()
+                masked[spot, to, :] = held[2 * i + part, at, :] * factor
+                target = out_refs[spot // count].at[spot % count, to]
+                out_copies.append(
+                    pltpu.make_async_copy(
+                        masked.at[spot, to], target, out_sems.at[len(out_copies)]
+                    )
+                )
+                out_copies[-1].start()
     for copy in out_copies:
         copy.wait()
 
@@ -87,8 +94,8 @@
             pltpu.VMEM((4, rows, width), dtype),
             pltpu.VMEM((count, unit, width), dtype),
             pltpu.SMEM((2,) + first_mask.shape, first_mask.dtype),
-            pltpu.SemaphoreType.DMA((2,)),
-            pltpu.SemaphoreType.DMA((2,)),
+            pltpu.SemaphoreType.DMA((4 * (rows // TILE),)),
+            pltpu.SemaphoreType.DMA((4 * (rows // TILE),)),
             pltpu.SemaphoreType.DMA((2,)),
         ],
         name=name,
@@ -121,11 +128,18 @@
     out_rows = damp.shape[1]
     row, col, layer = (lax.axis_index(a) for a in ("row", "col", "depth"))
     small = fetch_masks((k_mask, p_mask), masks, small_sems)
+    half = width // 2
     copies = [
-        pltpu.make_async_copy(ref, held.at[pl.ds(2 * i, 2)], sems.at[i])
+        pltpu.make_async_copy(
+            ref.at[part, pl.ds(start, half)],
+            held.at[2 * i + part, pl.ds(start, half)],
+            sems.at[1 + 4 * (start // half) + 2 * i + part],
+        )
+        for start in range(0, here, half)
         for i, ref in enumerate((p_ref, k_ref))
+        for part in range(2)
     ]
-    own_copy = pltpu.make_async_copy(strip.at[pl.ds(2, 2)], own, sems.at[2])
+    own_copy = pltpu.make_async_copy(strip.at[pl.ds(2, 2)], own, sems.at[0])
     tables = [
         pltpu.make_async_copy(source, target, small_sems.at[2 + i])
         for i, (source, target) in enumerate(
@@ -134,21 +148,27 @@
     ]
     for copy in copies + [own_copy] + tables:
         copy.start()
-    for copy in small + copies:
+    for copy in small:
         copy.wait()
     out_copies = []
-    for block in range(here // width):
-        for tile in range(block * width // TILE, (block + 1) * width // TILE):
+    for step in range(here // half):
+        for copy in copies[4 * step : 4 * step + 4]:
+            copy.wait()
+        block, within = divmod(step * half, width)
+        for tile in range(step * half // TILE, (step + 1) * half // TILE):
             at, spot = pl.ds(tile * TILE, TILE), pl.ds(tile * TILE - block * width, TILE)
             for i in range(2):
                 factor = tile_row(masks.at[1 - i], tile, width, held.dtype)
                 for part in (2 * i, 2 * i + 1):
                     near[4 * block + part, spot, :] = held[part, at, :] * factor
-        span = pl.ds(4 * block, 4)
-        out_copies.append(
-            pltpu.make_async_copy(near.at[span], near_ref.at[span], out_sems.at[block])
-        )
-        out_copies[-1].start()
+        for part in range(4):
+            place = (4 * block + part, pl.ds(within, half))
+            out_copies.append(
+                pltpu.make_async_copy(
+                    near.at[place], near_ref.at[place], out_sems.at[len(out_copies)]
+                )
+            )
+            out_copies[-1].start()
     for copy in [own_copy] + tables:
         copy.wait()
     lanes = lax.broadcasted_iota(jnp.int32, (1, width), 1) // TILE
@@ -189,8 +209,8 @@
             pltpu.SMEM(atoms.shape, atoms.dtype),
             pltpu.SMEM(classes.shape, classes.dtype),
             pltpu.SMEM(rates.shape, rates.dtype),
-            pltpu.SemaphoreType.DMA((3,)),
-            pltpu.SemaphoreType.DMA((blocks,)),
+            pltpu.SemaphoreType.DMA((1 + 8 * blocks,)),
+            pltpu.SemaphoreType.DMA((8 * blocks,)),
             pltpu.SemaphoreType.DMA((5,)),
         ],
         cost_estimate=pl.CostEstimate(
@@ -316,8 +336,8 @@
 
 
 def product_kernel(rows_n, cols_n, split, damp, near, middle, last, *refs):
-    shares = refs[:-3]
-    out_ref, left_last, total = refs[-3:]
+    shares = refs[:-5]
+    out_ref, left_last, total, result, sems = refs[-5:]
     out_rows = last.shape[1]
     row, layer = lax.axis_index("row"), lax.axis_index("depth")
     place_left(left_last, last, 0)
@@ -335,8 +355,23 @@
         def _():
             total[...] = middle[...] + products(left_last, 0, right, wanted - block, 1)
 
-    out_ref[0] = total[pl.ds(out_rows, out_rows), :] - damp[0]
-    out_ref[1] = -total[pl.ds(0, out_rows), :] - damp[1]
+    copies = []
+    rows = out_rows // 4
+    for part in range(2):
+        for start in range(0, out_rows, rows):
+            at = pl.ds(start, rows)
+            if part == 0:
+                result[0, at, :] = total[pl.ds(out_rows + start, rows), :] - damp[0, at, :]
+            else:
+                result[1, at, :] = -total[at, :] - damp[1, at, :]
+            copies.append(
+                pltpu.make_async_copy(
+                    result.at[part, at], out_ref.at[part, at], sems.at[len(copies)]
+                )
+            )
+            copies[-1].start()
+    for copy in copies:
+        copy.wait()
 
 
 def body(k_parts, p_parts, k_mask, p_mask, atoms, classes, rates):
@@ -372,9 +407,14 @@
     return pl.pallas_call(
         functools.partial(product_kernel, rows_n, cols_n, split),
         in_specs=[VMEM] * len(operands),
-        out_specs=VMEM,
+        out_specs=HBM,
         out_shape=jax.ShapeDtypeStruct((2, out_rows, width), jnp.float32),
-        scratch_shapes=[pltpu.VMEM(block, strip.dtype), pltpu.VMEM(total, jnp.float32)],
+        scratch_shapes=[
+            pltpu.VMEM(block, strip.dtype),
+            pltpu.VMEM(total, jnp.float32),
+            pltpu.VMEM((2, out_rows, width), jnp.float32),
+            pltpu.SemaphoreType.DMA((8,)),
+        ],
         compiler_params=params((near.shape, 2 * rows_n), (left.shape, 2), (block, 4), (total, 16)),
         name="commutator",
     )(*operands)

time: 25.9 us -> 26.1 us (level)
    ppermute x2, waiting for transfers between devices: 2.12 us -> 1.72 us  [body(): lax.ppermute(block, 'col', [(i, (i + 1) % cols_n) for i in range(cols_n)])]
  transfers between devices with their start and end apart: 7 -> 7, of which waited for: 4 -> 3; matrix products, arithmetic and copies ran while one was open for 0% -> 0% of each run, Pallas kernels for 23% -> 24%
where the time goes in v3:
time: 26.1 us; the launch traced here: 25.7 us
  Pallas kernels  8.99 us (34%)
  waiting for transfers between devices  8.09 us (31%)
  starting transfers between devices  7.29 us (28%)
  local copies, waits for them, and re-layouts  1.23 us (5%)
    ppermute x2, waiting for transfers between devices, body(): got = [lax.ppermute(part, 'row', perm) for part in share]  6.36 us
    pallas_call x2, Pallas kernels, mask_rows(): pl.pallas_call(functools.partial(rows_kernel, places), in_specs=[HBM] * 4...  3.7 us
    ppermute x2, starting transfers between devices, body(): lax.ppermute(block, 'col', [(i, (i + 1) % cols_n) for i in range(cols_n)])  3.13 us
    pallas_call x1, Pallas kernels, local_part(): pl.pallas_call(local_kernel, in_specs=[HBM] * 8, out_specs=[HBM, VMEM], o...  3.03 us
    ppermute x2, starting transfers between devices, body(): got = [lax.ppermute(part, 'row', perm) for part in share]  2.09 us
    ppermute x1, starting transfers between devices, body(): lax.ppermute(downs[-1], 'col', [(i, (i - 1) % cols_n) for i in range(cols...  2.06 us
    ppermute x2, waiting for transfers between devices, body(): lax.ppermute(block, 'col', [(i, (i + 1) % cols_n) for i in range(cols_n)])  1.72 us
    unnamed x8, local copies, waits for them, and re-layouts  1.23 us
  transfers between devices with their start and end apart: 7, of which 3 were waited for; matrix products, arithmetic and copies ran while one was open for 0% of the time, Pallas kernels for 24%

profile of v3, /device:TPU:0, one launch (start us, length us, event | category | flops | bytes accessed | tf_op | source)
XLA Modules:
  0.0 25.7 jit_solution(17697874725700008971)
XLA Ops:
  0.0 1.7 %mask_strip.1.strip.own = bf16[4,128,256]{2,1,0:T(8,128)(2,1)} custom-call(s32[4,8]{1,0:T(4,128)} %bitcast.2, s32[4,8]{1,0:T(4,128)} %bitcast.5, bf16[2,512,256]{2,1,0:T(8,128)(2,1)} %second_ref.3, bf16[2,512,256]{2,1,0:T(8,128)(2,1)} %first_ref.3), custom_call_target="tpu_custom_call" | custom-call | tf_op jit(solution)/shard_map/mask_strip/pallas_call | solution.py:88
  1.7 0.0 copy-start.2
  1.7 3.1 %collective-permute-start = (bf16[4,128,256]{2,1,0:T(8,128)(2,1)}, bf16[4,128,256]{2,1,0:T(8,128)(2,1)S(1)}, u32[]{:S(2)}, u32[]{:S(2)}) collective-permute-start(bf16[4,128,256]{2,1,0:T(8,128)(2,1)} %mask_strip.1.strip.own), channel_id=1, source_target_pairs={{0,4},{4,8},{8,12},{12,0},{1,5},{5,9},{9,13},{13,1},{2,6},{6,10},{... | collective-permute-start | bytes 786440 | tf_op jit(solution)/shard_map/ppermute | solution.py:388
  4.8 2.0 %mask_share.1 = (bf16[2,256,256]{2,1,0:T(8,128)(2,1)}, bf16[2,256,256]{2,1,0:T(8,128)(2,1)}) custom-call(s32[4,8]{1,0:T(4,128)} %bitcast.6, s32[4,8]{1,0:T(4,128)} %bitcast.3, bf16[2,512,256]{2,1,0:T(8,128)(2,1)} %first_ref.3, bf16[2,512,256]{2,1,0:T(8,128)(2,1)} %second_ref.3), custom_call_target="tpu_custom_call" | custom-call | tf_op jit(solution)/shard_map/mask_share/pallas_call | solution.py:88
  6.8 1.6 %collective-permute-start.2 = (bf16[2,256,256]{2,1,0:T(8,128)(2,1)}, bf16[2,256,256]{2,1,0:T(8,128)(2,1)S(1)}, u32[]{:S(2)}, u32[]{:S(2)}) collective-permute-start(bf16[2,256,256]{2,1,0:T(8,128)(2,1)} %get-tuple-element.15), channel_id=1, source_target_pairs={{0,16},{16,0},{1,17},{17,1},{2,18},{18,2},{3,19},{19,3},{4,20},{20... | collective-permute-start | bytes 786440 | tf_op jit(solution)/shard_map/ppermute | solution.py:397
  8.4 0.5 %collective-permute-start.3 = (bf16[2,256,256]{2,1,0:T(8,128)(2,1)}, bf16[2,256,256]{2,1,0:T(8,128)(2,1)S(1)}, u32[]{:S(2)}, u32[]{:S(2)}) collective-permute-start(bf16[2,256,256]{2,1,0:T(8,128)(2,1)} %get-tuple-element.16), channel_id=1, source_target_pairs={{0,16},{16,0},{1,17},{17,1},{2,18},{18,2},{3,19},{19,3},{4,20},{20... | collective-permute-start | bytes 786440 | tf_op jit(solution)/shard_map/ppermute | solution.py:397
  8.9 2.1 %collective-permute-start.1 = (bf16[4,128,256]{2,1,0:T(8,128)(2,1)}, bf16[4,128,256]{2,1,0:T(8,128)(2,1)S(1)}, u32[]{:S(2)}, u32[]{:S(2)}) collective-permute-start(bf16[4,128,256]{2,1,0:T(8,128)(2,1)} %mask_strip.1.strip.own), channel_id=1, source_target_pairs={{0,12},{4,0},{8,4},{12,8},{1,13},{5,1},{9,5},{13,9},{2,14},{6,2},{... | collective-permute-start | bytes 786440 | tf_op jit(solution)/shard_map/ppermute | solution.py:390
  11.0 3.0 %local_part.1 = (bf16[8,256,256]{2,1,0:T(8,128)(2,1)}, f32[2,128,256]{2,1,0:T(8,128)}) custom-call(s32[4,8]{1,0:T(4,128)} %bitcast.4, s32[4,8]{1,0:T(4,128)} %bitcast.7, s32[16]{0:T(128)} %atoms_ref.1, s32[4,4]{1,0:T(4,128)} %classes_ref.1, f32[4]{0:T(128)} %rates_ref.1, bf16[2,512,256]{2,1,0:T(8,128)(2,1)} %second_ref.3, bf16[2,512,256]{2,1,0:T(8,128)(2,1)} %first_ref.3, ...), custom_call_target="tpu_custom_call" | custom-call | flops 1048576 | bytes 2621440 | tf_op jit(solution)/shard_map/local_part/pallas_call | solution.py:196
  14.0 0.0 collective-permute-done.refs_0_.block
  14.0 0.1 collective-permute-start.6
  14.1 2.2 %collective-permute-done.2.refs_0_ = bf16[2,256,256]{2,1,0:T(8,128)(2,1)S(1)} collective-permute-done((bf16[2,256,256]{2,1,0:T(8,128)(2,1)}, bf16[2,256,256]{2,1,0:T(8,128)(2,1)S(1)}, u32[]{:S(2)}, u32[]{:S(2)}) %collective-permute-start.2) | collective-permute-done | bytes 262176 | tf_op jit(solution)/shard_map/ppermute | solution.py:397
  16.3 0.0 collective-permute-start.4
  16.3 4.1 %collective-permute-done.3.refs_1_ = bf16[2,256,256]{2,1,0:T(8,128)(2,1)S(1)} collective-permute-done((bf16[2,256,256]{2,1,0:T(8,128)(2,1)}, bf16[2,256,256]{2,1,0:T(8,128)(2,1)S(1)}, u32[]{:S(2)}, u32[]{:S(2)}) %collective-permute-start.3) | collective-permute-done | bytes 262176 | tf_op jit(solution)/shard_map/ppermute | solution.py:397
  20.5 0.0 collective-permute-start.5
  20.5 0.0 collective-permute-done.1.refs_1_
  20.5 0.0 copy-done.2
  20.5 0.0 copy-start
  20.5 1.2 %copy-done = bf16[8,256,256]{2,1,0:T(8,128)(2,1)S(1)} copy-done((bf16[8,256,256]{2,1,0:T(8,128)(2,1)S(1)}, bf16[8,256,256]{2,1,0:T(8,128)(2,1)}, u32[]{:S(2)}) %copy-start) | copy-done | bytes 1048600
  21.7 0.7 %early_product.1 = (bf16[256,4096]{1,0:T(8,128)(2,1)S(1)}, f32[256,256]{1,0:T(8,128)S(1)}) custom-call(bf16[8,256,256]{2,1,0:T(8,128)(2,1)S(1)} %copy-done, bf16[4,128,256]{2,1,0:T(8,128)(2,1)S(1)} %copy-done.2, bf16[4,128,256]{2,1,0:T(8,128)(2,1)S(1)} %collective-permute-done.refs_0_.block, bf16[4,128,256]{2,1,0:T(8,128)(2,1)S(1)} %collective-permute-done.1.refs_1_), custom_call_target="tpu_custom_call" | custom-call | flops 10737418240 | bytes 4194304 | tf_op jit(solution)/shard_map/early_product/pallas_call | solution.py:295
  22.4 0.0 copy-start.1
  22.4 0.0 copy-start.3
  22.4 0.0 collective-permute-done.4.refs_2_
  22.4 0.0 collective-permute-done.5.refs_3_
  22.4 0.5 %shares_product.1.middle = f32[256,256]{1,0:T(8,128)S(1)} custom-call(bf16[256,4096]{1,0:T(8,128)(2,1)S(1)} %get-tuple-element.13.left, f32[256,256]{1,0:T(8,128)S(1)} %get-tuple-element.14.early, bf16[2,256,256]{2,1,0:T(8,128)(2,1)S(1)} %collective-permute-done.2.refs_0_, bf16[2,256,256]{2,1,0:T(8,128)(2,1)S(1)} %collective-permute-done.3.refs_1_, ...), custom_call_target="tpu_custom_call" | custom-call | flops 1000000 | bytes 1000000 | tf_op jit(solution)/shard_map/shares_product/pallas_call | solution.py:327
  22.9 1.7 %collective-permute-done.6.last = bf16[4,128,256]{2,1,0:T(8,128)(2,1)S(1)} collective-permute-done((bf16[4,128,256]{2,1,0:T(8,128)(2,1)S(1)}, bf16[4,128,256]{2,1,0:T(8,128)(2,1)S(1)}, u32[]{:S(2)}, u32[]{:S(2)}) %collective-permute-start.6) | collective-permute-done | bytes 262176 | tf_op jit(solution)/shard_map/ppermute | solution.py:388
  24.6 0.0 copy-done.1
  24.6 0.0 copy-done.3
  24.6 1.1 %commutator.1 = f32[2,128,256]{2,1,0:T(8,128)} custom-call(f32[2,128,256]{2,1,0:T(8,128)S(1)} %copy-done.3, bf16[8,256,256]{2,1,0:T(8,128)(2,1)S(1)} %copy-done.1, f32[256,256]{1,0:T(8,128)S(1)} %shares_product.1.middle, bf16[4,128,256]{2,1,0:T(8,128)(2,1)S(1)} %collective-permute-done.6.last, bf16[2,256,256]{2,1,0:T(8,128)(2,1)S(1)} %collective-permute-done.2.refs_0_, ...), custom_call_target="tpu_custom_call" | custom-call | tf_op jit(solution)/shard_map/commutator/pallas_call | solution.py:407
  (1 shorter events, 0.0 us)
Async XLA Ops:
  1.7 18.8 %copy-start.2 = (bf16[4,128,256]{2,1,0:T(8,128)(2,1)S(1)}, bf16[4,128,256]{2,1,0:T(8,128)(2,1)}, u32[]{:S(2)}) copy-start(bf16[4,128,256]{2,1,0:T(8,128)(2,1)} %mask_strip.1.strip.own) | copy-start | bytes 786436
  1.7 12.3 %collective-permute-start = (bf16[4,128,256]{2,1,0:T(8,128)(2,1)}, bf16[4,128,256]{2,1,0:T(8,128)(2,1)S(1)}, u32[]{:S(2)}, u32[]{:S(2)}) collective-permute-start(bf16[4,128,256]{2,1,0:T(8,128)(2,1)} %mask_strip.1.strip.own), channel_id=1, source_target_pairs={{0,4},{4,8},{8,12},{12,0},{1,5},{5,9},{9,13},{13,1},{2,6},{6,10},{... | collective-permute-start | bytes 786440 | tf_op jit(solution)/shard_map/ppermute | solution.py:388
  6.8 9.5 %collective-permute-start.2 = (bf16[2,256,256]{2,1,0:T(8,128)(2,1)}, bf16[2,256,256]{2,1,0:T(8,128)(2,1)S(1)}, u32[]{:S(2)}, u32[]{:S(2)}) collective-permute-start(bf16[2,256,256]{2,1,0:T(8,128)(2,1)} %get-tuple-element.15), channel_id=1, source_target_pairs={{0,16},{16,0},{1,17},{17,1},{2,18},{18,2},{3,19},{19,3},{4,20},{20... | collective-permute-start | bytes 786440 | tf_op jit(solution)/shard_map/ppermute | solution.py:397
  8.4 12.1 %collective-permute-start.3 = (bf16[2,256,256]{2,1,0:T(8,128)(2,1)}, bf16[2,256,256]{2,1,0:T(8,128)(2,1)S(1)}, u32[]{:S(2)}, u32[]{:S(2)}) collective-permute-start(bf16[2,256,256]{2,1,0:T(8,128)(2,1)} %get-tuple-element.16), channel_id=1, source_target_pairs={{0,16},{16,0},{1,17},{17,1},{2,18},{18,2},{3,19},{19,3},{4,20},{20... | collective-permute-start | bytes 786440 | tf_op jit(solution)/shard_map/ppermute | solution.py:397
  8.9 11.6 %collective-permute-start.1 = (bf16[4,128,256]{2,1,0:T(8,128)(2,1)}, bf16[4,128,256]{2,1,0:T(8,128)(2,1)S(1)}, u32[]{:S(2)}, u32[]{:S(2)}) collective-permute-start(bf16[4,128,256]{2,1,0:T(8,128)(2,1)} %mask_strip.1.strip.own), channel_id=1, source_target_pairs={{0,12},{4,0},{8,4},{12,8},{1,13},{5,1},{9,5},{13,9},{2,14},{6,2},{... | collective-permute-start | bytes 786440 | tf_op jit(solution)/shard_map/ppermute | solution.py:390
  14.0 10.6 %collective-permute-start.6 = (bf16[4,128,256]{2,1,0:T(8,128)(2,1)S(1)}, bf16[4,128,256]{2,1,0:T(8,128)(2,1)S(1)}, u32[]{:S(2)}, u32[]{:S(2)}) collective-permute-start(bf16[4,128,256]{2,1,0:T(8,128)(2,1)S(1)} %relay.1), channel_id=1, source_target_pairs={{0,4},{4,8},{8,12},{12,0},{1,5},{5,9},{9,13},{13,1},{2,6},{6,10},{... | collective-permute-start | bytes 786440 | tf_op jit(solution)/shard_map/ppermute | solution.py:388
  16.3 6.1 %collective-permute-start.4 = (bf16[2,256,256]{2,1,0:T(8,128)(2,1)S(1)}, bf16[2,256,256]{2,1,0:T(8,128)(2,1)S(1)}, u32[]{:S(2)}, u32[]{:S(2)}) collective-permute-start(bf16[2,256,256]{2,1,0:T(8,128)(2,1)S(1)} %collective-permute-done.2.refs_0_), channel_id=1, source_target_pairs={{0,1},{1,0},{2,3},{3,2},{4,5},{5,4},{6,7},{7,6},{8,9},{9,8},{10,11... | collective-permute-start | bytes 786440 | tf_op jit(solution)/shard_map/ppermute | solution.py:401
  20.5 1.9 %collective-permute-start.5 = (bf16[2,256,256]{2,1,0:T(8,128)(2,1)S(1)}, bf16[2,256,256]{2,1,0:T(8,128)(2,1)S(1)}, u32[]{:S(2)}, u32[]{:S(2)}) collective-permute-start(bf16[2,256,256]{2,1,0:T(8,128)(2,1)S(1)} %collective-permute-done.3.refs_1_), channel_id=1, source_target_pairs={{0,1},{1,0},{2,3},{3,2},{4,5},{5,4},{6,7},{7,6},{8,9},{9,8},{10,11... | collective-permute-start | bytes 786440 | tf_op jit(solution)/shard_map/ppermute | solution.py:401
  20.5 1.2 %copy-start = (bf16[8,256,256]{2,1,0:T(8,128)(2,1)S(1)}, bf16[8,256,256]{2,1,0:T(8,128)(2,1)}, u32[]{:S(2)}) copy-start(bf16[8,256,256]{2,1,0:T(8,128)(2,1)} %get-tuple-element.12.near) | copy-start | bytes 3145732
  22.4 2.2 %copy-start.1 = (bf16[8,256,256]{2,1,0:T(8,128)(2,1)S(1)}, bf16[8,256,256]{2,1,0:T(8,128)(2,1)}, u32[]{:S(2)}) copy-start(bf16[8,256,256]{2,1,0:T(8,128)(2,1)} %get-tuple-element.12.near) | copy-start | bytes 3145732
  22.4 2.2 %copy-start.3 = (f32[2,128,256]{2,1,0:T(8,128)S(1)}, f32[2,128,256]{2,1,0:T(8,128)}, u32[]{:S(2)}) copy-start(f32[2,128,256]{2,1,0:T(8,128)} %get-tuple-element.11.damp) | copy-start | bytes 786436

commit v4 on v2

--- a/solution.py
+++ b/solution.py
@@ -95,6 +95,56 @@
     )(first_mask, second_mask, first_parts, second_parts)
 
 
+def strip_kernel(k_ref, p_ref, strip_ref, sems):
+    rows = strip_ref.shape[1]
+    at = pl.ds(pl.multiple_of(lax.axis_index("depth") * rows, rows), rows)
+    copies = [
+        pltpu.make_async_copy(ref.at[:, at, :], strip_ref.at[pl.ds(2 * i, 2)], sems.at[i])
+        for i, ref in enumerate((k_ref, p_ref))
+    ]
+    for copy in copies:
+        copy.start()
+    for copy in copies:
+        copy.wait()
+
+
+def cut_strip(k_parts, p_parts, out_rows):
+    return pl.pallas_call(
+        strip_kernel,
+        in_specs=[HBM] * 2,
+        out_specs=HBM,
+        out_shape=jax.ShapeDtypeStruct((4, out_rows, k_parts.shape[2]), k_parts.dtype),
+        scratch_shapes=[pltpu.SemaphoreType.DMA((2,))],
+        name="cut_strip",
+    )(k_parts, p_parts)
+
+
+def factors_kernel(*refs):
+    masks, out_ref = refs[:-1], refs[-1]
+    rows, width = out_ref.shape[2:]
+    tiles = rows // TILE
+    first = lax.axis_index("depth") * tiles
+    for index, mask in enumerate(masks):
+        for i in range(2):
+            for tile in range(tiles):
+                factor = tile_row(mask.at[i], first + tile, width, out_ref.dtype)
+                out_ref[index, i, pl.ds(tile * TILE, TILE), :] = jnp.broadcast_to(
+                    factor, (TILE, width)
+                )
+
+
+def expand_factors(masks, out_rows, width, dtype):
+    shape = (len(masks), 2, out_rows, width)
+    return pl.pallas_call(
+        factors_kernel,
+        in_specs=[SMEM] * len(masks),
+        out_specs=VMEM,
+        out_shape=jax.ShapeDtypeStruct(shape, dtype),
+        compiler_params=params((shape, 2)),
+        name="expand_factors",
+    )(*masks)
+
+
 def local_kernel(
     k_mask,
     p_mask,
@@ -103,12 +153,10 @@
     rates_ref,
     k_ref,
     p_ref,
-    strip,
     near_ref,
     damp,
     held,
     near,
-    own,
     masks,
     atoms,
     classes,
@@ -125,14 +173,13 @@
         pltpu.make_async_copy(ref, held.at[pl.ds(2 * i, 2)], sems.at[i])
         for i, ref in enumerate((p_ref, k_ref))
     ]
-    own_copy = pltpu.make_async_copy(strip.at[pl.ds(2, 2)], own, sems.at[2])
     tables = [
         pltpu.make_async_copy(source, target, small_sems.at[2 + i])
         for i, (source, target) in enumerate(
             ((atoms_ref, atoms), (classes_ref, classes), (rates_ref, rates))
         )
     ]
-    for copy in copies + [own_copy] + tables:
+    for copy in copies + tables:
         copy.start()
     for copy in small + copies:
         copy.wait()
@@ -149,7 +196,7 @@
             pltpu.make_async_copy(near.at[span], near_ref.at[span], out_sems.at[block])
         )
         out_copies[-1].start()
-    for copy in [own_copy] + tables:
+    for copy in tables:
         copy.wait()
     lanes = lax.broadcasted_iota(jnp.int32, (1, width), 1) // TILE
     row_tiles, col_tiles = out_rows // TILE, width // TILE
@@ -163,19 +210,22 @@
             rate = jnp.where(atom_row != atom_col, rates[classes[atom_row, atom_col]], 0.0)
             gamma = jnp.where(lanes == spot, rate, gamma)
         for part in range(2):
-            damp[part, at, :] = gamma * own[part, at, :].astype(jnp.float32)
+            start = layer * out_rows + tile * TILE
+            within = pl.ds(pl.multiple_of(lax.rem(start, width), TILE), TILE)
+            own = near[4 * (start // width) + part, within, :]
+            damp[part, at, :] = gamma * own.astype(jnp.float32)
     for copy in out_copies:
         copy.wait()
 
 
-def local_part(k_mask, p_mask, atoms, classes, rates, k_parts, p_parts, strip):
+def local_part(k_mask, p_mask, atoms, classes, rates, k_parts, p_parts, out_rows):
     here, width = k_parts.shape[1:]
-    out_rows, dtype = strip.shape[1], strip.dtype
+    dtype = k_parts.dtype
     blocks = here // width
     near = (4 * blocks, width, width)
     return pl.pallas_call(
         local_kernel,
-        in_specs=[HBM] * 8,
+        in_specs=[HBM] * 7,
         out_specs=[HBM, VMEM],
         out_shape=[
             jax.ShapeDtypeStruct(near, dtype),
@@ -184,12 +234,11 @@
         scratch_shapes=[
             pltpu.VMEM((4, here, width), dtype),
             pltpu.VMEM(near, dtype),
-            pltpu.VMEM((2, out_rows, width), dtype),
             pltpu.SMEM((2,) + k_mask.shape, k_mask.dtype),
             pltpu.SMEM(atoms.shape, atoms.dtype),
             pltpu.SMEM(classes.shape, classes.dtype),
             pltpu.SMEM(rates.shape, rates.dtype),
-            pltpu.SemaphoreType.DMA((3,)),
+            pltpu.SemaphoreType.DMA((2,)),
             pltpu.SemaphoreType.DMA((blocks,)),
             pltpu.SemaphoreType.DMA((5,)),
         ],
@@ -197,12 +246,14 @@
             flops=8 * here * width, bytes_accessed=20 * here * width, transcendentals=0
         ),
         name="local_part",
-    )(k_mask, p_mask, atoms, classes, rates, k_parts, p_parts, strip)
-
-
-def place_left(left, ref, block):
+    )(k_mask, p_mask, atoms, classes, rates, k_parts, p_parts)
+
+
+def place_left(left, ref, block, factors, index):
     rows, width = ref.shape[1:]
-    k_re, k_im, p_re, p_im = ref[0], ref[1], ref[2], ref[3]
+    k_factor, p_factor = factors[index, 0], factors[index, 1]
+    k_re, k_im = ref[0] * k_factor, ref[1] * k_factor
+    p_re, p_im = ref[2] * p_factor, ref[3] * p_factor
     for half, parts in enumerate(((k_re, -k_im, -p_re, p_im), (k_im, k_re, -p_im, -p_re))):
         for slot, part in enumerate(parts):
             at = pl.multiple_of((4 * block + slot) * width, width)
@@ -251,27 +302,27 @@
     return sum(found[1:], found[0])
 
 
-def early_kernel(cols_n, near, own, *refs):
+def early_kernel(cols_n, near, factors, own, *refs):
     blocks = refs[:-2]
     ups, downs = blocks[: cols_n // 2 - 1], blocks[cols_n // 2 - 1 :]
     left, total = refs[-2:]
     width = own.shape[2]
     row, col = lax.axis_index("row"), lax.axis_index("col")
-    place_left(left, own, col)
+    place_left(left, own, col, factors, 0)
     for step, ref in enumerate(ups, 1):
-        place_left(left, ref, lax.rem(col - step + cols_n, cols_n))
+        place_left(left, ref, lax.rem(col - step + cols_n, cols_n), factors, step)
     for step, ref in enumerate(downs, 1):
-        place_left(left, ref, lax.rem(col + step, cols_n))
+        place_left(left, ref, lax.rem(col + step, cols_n), factors, cols_n - step)
     last = pl.multiple_of(lax.rem(col + cols_n - cols_n // 2, cols_n) * 4 * width, width)
     left[:, pl.ds(last, 4 * width)] = jnp.zeros((left.shape[0], 4 * width), left.dtype)
     count = near.shape[0] // 4
     total[...] = products(left, row * count, [near], 0, count)
 
 
-def early_product(near, strip, blocks, cols_n):
+def early_product(near, factors, strip, blocks, cols_n):
     out_rows, width = strip.shape[1:]
     left, total = (2 * out_rows, cols_n * 4 * width), (2 * out_rows, width)
-    operands = [near, strip] + blocks
+    operands = [near, factors, strip] + blocks
     return pl.pallas_call(
         functools.partial(early_kernel, cols_n),
         in_specs=[VMEM] * len(operands),
@@ -315,12 +366,12 @@
     )(*operands)
 
 
-def product_kernel(rows_n, cols_n, split, damp, near, middle, last, *refs):
+def product_kernel(rows_n, cols_n, split, damp, near, factors, middle, last, *refs):
     shares = refs[:-3]
     out_ref, left_last, total = refs[-3:]
     out_rows = last.shape[1]
     row, layer = lax.axis_index("row"), lax.axis_index("depth")
-    place_left(left_last, last, 0)
+    place_left(left_last, last, 0, factors, cols_n // 2)
     here = near.shape[0] // 4
     rights = [(row * here, here, [near])]
     for index in range(len(shares) // 2):
@@ -345,7 +396,7 @@
     out_rows = here // depth
     split = 2 if depth % 2 == 0 else 1
     k_mask, p_mask = k_mask.T, p_mask.T
-    (strip,) = mask_rows(k_mask, p_mask, k_parts, p_parts, depth, 1, "mask_strip")
+    strip = cut_strip(k_parts, p_parts, out_rows)
     share = mask_rows(p_mask, k_mask, p_parts, k_parts, split, 2, "mask_share")
     ups, downs = [strip], [strip]
     for step in range(1, cols_n // 2 + 1):
@@ -353,8 +404,13 @@
         ups.append(lax.ppermute(block, "col", [(i, (i + 1) % cols_n) for i in range(cols_n)]))
     for step in range(1, cols_n - cols_n // 2):
         downs.append(lax.ppermute(downs[-1], "col", [(i, (i - 1) % cols_n) for i in range(cols_n)]))
+    masks = [jnp.stack((k_mask, p_mask))]
+    for shift in range(1, cols_n):
+        perm = [(i, (i + shift) % cols_n) for i in range(cols_n)]
+        masks.append(lax.ppermute(masks[0], "col", perm))
+    factors = expand_factors(masks, out_rows, width, strip.dtype)
     near, damp = local_part(
-        k_mask, p_mask, atoms, classes, rates, k_parts, p_parts, strip
+        k_mask, p_mask, atoms, classes, rates, k_parts, p_parts, out_rows
     )
     shares = []
     for shift in range(1, rows_n):
@@ -365,9 +421,9 @@
             swap = [(i, i ^ 1) for i in range(depth)]
             shares += [lax.ppermute(part, "depth", swap) for part in got]
     blocks = ups[1:-1] + downs[1:]
-    left, early = early_product(near, strip, blocks, cols_n)
+    left, early = early_product(near, factors, strip, blocks, cols_n)
     middle = shares_product(left, early, shares, rows_n, split, here // width)
-    operands = [damp, near, middle, ups[-1]] + shares
+    operands = [damp, near, factors, middle, ups[-1]] + shares
     block, total = (2 * out_rows, 4 * width), (2 * out_rows, width)
     return pl.pallas_call(
         functools.partial(product_kernel, rows_n, cols_n, split),

time: 25.9 us -> 46.1 us (1.78)
  waiting for transfers between devices: 8.27 us -> 16.9 us
  Pallas kernels: 8.77 us -> 17 us
  starting transfers between devices: 7.29 us -> 10.6 us
    ppermute x0 -> x3, waiting for transfers between devices: none -> 12 us  [body(): masks.append(lax.ppermute(masks[0], 'col', perm))]
    pallas_call x1 -> x3, Pallas kernels: 3.02 us -> 12.9 us  [the longest x1 9.06 us: cut_strip(): pl.pallas_call(strip_kernel, in_specs=[HBM] * 2, out_specs=HBM, out_shape...]
    ppermute x2, waiting for transfers between devices: 6.14 us -> 0.01 us  [body(): got = [lax.ppermute(part, 'row', perm) for part in share]]
    ppermute x2, waiting for transfers between devices: 2.12 us -> 4.93 us  [body(): lax.ppermute(block, 'col', [(i, (i + 1) % cols_n) for i in range(cols_n)])]
    ppermute x0 -> x3, starting transfers between devices: none -> 2.51 us  [body(): masks.append(lax.ppermute(masks[0], 'col', perm))]
    pallas_call x2 -> x1, Pallas kernels: 3.53 us -> 1.83 us  [mask_rows(): pl.pallas_call(functools.partial(rows_kernel, places), in_specs=[HBM] * 4...]
    ppermute x2, starting transfers between devices: 0.01 us -> 0.51 us  [body(): shares += [lax.ppermute(part, 'depth', swap) for part in got]]
    unnamed x8 -> x12, local copies, waits for them, and re-layouts: 1.23 us -> 1.25 us
  transfers between devices with their start and end apart: 7 -> 10, of which waited for: 4 -> 3; matrix products, arithmetic and copies ran while one was open for 0% -> 0% of each run, Pallas kernels for 23% -> 15%
where the time goes in v4:
time: 46.1 us; the launch traced here: 45.9 us
  Pallas kernels  17 us (37%)
  waiting for transfers between devices  16.9 us (37%)
  starting transfers between devices  10.6 us (23%)
  local copies, waits for them, and re-layouts  1.25 us (3%)
    ppermute x3, waiting for transfers between devices, body(): masks.append(lax.ppermute(masks[0], 'col', perm))  12 us
    pallas_call x1, Pallas kernels, cut_strip(): pl.pallas_call(strip_kernel, in_specs=[HBM] * 2, out_specs=HBM, out_shape...  9.06 us
    ppermute x2, waiting for transfers between devices, body(): lax.ppermute(block, 'col', [(i, (i + 1) % cols_n) for i in range(cols_n)])  4.93 us
    ppermute x2, starting transfers between devices, body(): lax.ppermute(block, 'col', [(i, (i + 1) % cols_n) for i in range(cols_n)])  3.42 us
    pallas_call x1, Pallas kernels, local_part(): pl.pallas_call(local_kernel, in_specs=[HBM] * 7, out_specs=[HBM, VMEM], o...  3 us
    ppermute x3, starting transfers between devices, body(): masks.append(lax.ppermute(masks[0], 'col', perm))  2.51 us
    ppermute x2, starting transfers between devices, body(): got = [lax.ppermute(part, 'row', perm) for part in share]  2.09 us
    ppermute x1, starting transfers between devices, body(): lax.ppermute(downs[-1], 'col', [(i, (i - 1) % cols_n) for i in range(cols...  2.05 us
  transfers between devices with their start and end apart: 10, of which 3 were waited for; matrix products, arithmetic and copies ran while one was open for 0% of the time, Pallas kernels for 15%

profile of v4, /device:TPU:0, one launch (start us, length us, event | category | flops | bytes accessed | tf_op | source)
XLA Modules:
  0.0 45.9 jit_solution(13810517820725991645)
XLA Ops:
  0.0 0.0 copy-start.4
  0.0 0.0 copy-start.5
  0.0 9.1 %cut_strip.1.own = bf16[4,128,256]{2,1,0:T(8,128)(2,1)} custom-call(bf16[2,512,256]{2,1,0:T(8,128)(2,1)} %second_ref.1, bf16[2,512,256]{2,1,0:T(8,128)(2,1)} %first_ref.1), custom_call_target="tpu_custom_call" | custom-call | tf_op jit(solution)/shard_map/cut_strip/pallas_call | solution.py:112
  9.1 0.0 copy-start.3
  9.1 3.1 %collective-permute-start.3 = (bf16[4,128,256]{2,1,0:T(8,128)(2,1)}, bf16[4,128,256]{2,1,0:T(8,128)(2,1)S(1)}, u32[]{:S(2)}, u32[]{:S(2)}) collective-permute-start(bf16[4,128,256]{2,1,0:T(8,128)(2,1)} %cut_strip.1.own), channel_id=1, source_target_pairs={{0,4},{4,8},{8,12},{12,0},{1,5},{5,9},{9,13},{13,1},{2,6},{6,10},{... | collective-permute-start | bytes 786440 | tf_op jit(solution)/shard_map/ppermute | solution.py:404
  12.2 1.8 %mask_share.1 = (bf16[2,256,256]{2,1,0:T(8,128)(2,1)}, bf16[2,256,256]{2,1,0:T(8,128)(2,1)}) custom-call(s32[4,8]{1,0:T(4,128)} %bitcast.9, s32[4,8]{1,0:T(4,128)} %bitcast.6, bf16[2,512,256]{2,1,0:T(8,128)(2,1)} %first_ref.1, bf16[2,512,256]{2,1,0:T(8,128)(2,1)} %second_ref.1), custom_call_target="tpu_custom_call" | custom-call | tf_op jit(solution)/shard_map/mask_share/pallas_call | solution.py:81
  14.0 1.6 %collective-permute-start.5 = (bf16[2,256,256]{2,1,0:T(8,128)(2,1)}, bf16[2,256,256]{2,1,0:T(8,128)(2,1)S(1)}, u32[]{:S(2)}, u32[]{:S(2)}) collective-permute-start(bf16[2,256,256]{2,1,0:T(8,128)(2,1)} %get-tuple-element.15), channel_id=1, source_target_pairs={{0,16},{16,0},{1,17},{17,1},{2,18},{18,2},{3,19},{19,3},{4,20},{20... | collective-permute-start | bytes 786440 | tf_op jit(solution)/shard_map/ppermute | solution.py:418
  15.6 0.5 %collective-permute-start.6 = (bf16[2,256,256]{2,1,0:T(8,128)(2,1)}, bf16[2,256,256]{2,1,0:T(8,128)(2,1)S(1)}, u32[]{:S(2)}, u32[]{:S(2)}) collective-permute-start(bf16[2,256,256]{2,1,0:T(8,128)(2,1)} %get-tuple-element.16), channel_id=1, source_target_pairs={{0,16},{16,0},{1,17},{17,1},{2,18},{18,2},{3,19},{19,3},{4,20},{20... | collective-permute-start | bytes 786440 | tf_op jit(solution)/shard_map/ppermute | solution.py:418
  16.1 2.1 %collective-permute-start.4 = (bf16[4,128,256]{2,1,0:T(8,128)(2,1)}, bf16[4,128,256]{2,1,0:T(8,128)(2,1)S(1)}, u32[]{:S(2)}, u32[]{:S(2)}) collective-permute-start(bf16[4,128,256]{2,1,0:T(8,128)(2,1)} %cut_strip.1.own), channel_id=1, source_target_pairs={{0,12},{4,0},{8,4},{12,8},{1,13},{5,1},{9,5},{13,9},{2,14},{6,2},{... | collective-permute-start | bytes 786440 | tf_op jit(solution)/shard_map/ppermute | solution.py:406
  18.1 0.0 copy-done.4
  18.1 0.0 copy-done.5
  18.2 0.1 collective-permute-start
  18.2 8.2 %collective-permute-done.refs_1_ = s32[2,4,8]{2,1,0:T(4,128)S(1)} collective-permute-done((s32[2,4,8]{2,1,0:T(4,128)S(1)}, s32[2,4,8]{2,1,0:T(4,128)S(1)}, u32[]{:S(2)}, u32[]{:S(2)}) %collective-permute-start) | collective-permute-done | bytes 288 | tf_op jit(solution)/shard_map/ppermute | solution.py:410
  26.4 0.7 %collective-permute-start.1 = (s32[2,4,8]{2,1,0:T(4,128)S(1)}, s32[2,4,8]{2,1,0:T(4,128)S(1)}, u32[]{:S(2)}, u32[]{:S(2)}) collective-permute-start(s32[2,4,8]{2,1,0:T(4,128)S(1)} %pad_add_fusion.refs_0_), channel_id=1, source_target_pairs={{0,8},{4,12},{8,0},{12,4},{1,9},{5,13},{9,1},{13,5},{2,10},{6,14},... | collective-permute-start | bytes 776 | tf_op jit(solution)/shard_map/ppermute | solution.py:410
  27.1 3.8 %collective-permute-done.1.refs_2_ = s32[2,4,8]{2,1,0:T(4,128)S(1)} collective-permute-done((s32[2,4,8]{2,1,0:T(4,128)S(1)}, s32[2,4,8]{2,1,0:T(4,128)S(1)}, u32[]{:S(2)}, u32[]{:S(2)}) %collective-permute-start.1) | collective-permute-done | bytes 288 | tf_op jit(solution)/shard_map/ppermute | solution.py:410
  30.9 1.7 %collective-permute-start.2 = (s32[2,4,8]{2,1,0:T(4,128)S(1)}, s32[2,4,8]{2,1,0:T(4,128)S(1)}, u32[]{:S(2)}, u32[]{:S(2)}) collective-permute-start(s32[2,4,8]{2,1,0:T(4,128)S(1)} %pad_add_fusion.refs_0_), channel_id=1, source_target_pairs={{0,12},{4,0},{8,4},{12,8},{1,13},{5,1},{9,5},{13,9},{2,14},{6,2},{... | collective-permute-start | bytes 776 | tf_op jit(solution)/shard_map/ppermute | solution.py:410
  32.7 3.0 %local_part.1 = (bf16[8,256,256]{2,1,0:T(8,128)(2,1)}, f32[2,128,256]{2,1,0:T(8,128)}) custom-call(s32[4,8]{1,0:T(4,128)} %bitcast.7, s32[4,8]{1,0:T(4,128)} %bitcast.10, s32[16]{0:T(128)} %atoms_ref.1, s32[4,4]{1,0:T(4,128)} %classes_ref.1, f32[4]{0:T(128)} %rates_ref.1, bf16[2,512,256]{2,1,0:T(8,128)(2,1)} %second_ref.1, bf16[2,512,256]{2,1,0:T(8,128)(2,1)} %first_ref.1), custom_call_target="tpu_custom_call" | custom-call | flops 1048576 | bytes 2621440 | tf_op jit(solution)/shard_map/local_part/pallas_call | solution.py:226
  35.7 0.0 collective-permute-done.2.refs_3_
  35.7 0.9 %expand_factors.1.factors = bf16[4,2,128,256]{3,2,1,0:T(8,128)(2,1)S(1)} custom-call(s32[2,4,8]{2,1,0:T(4,128)S(1)} %pad_add_fusion.refs_0_, s32[2,4,8]{2,1,0:T(4,128)S(1)} %collective-permute-done.refs_1_, s32[2,4,8]{2,1,0:T(4,128)S(1)} %collective-permute-done.1.refs_2_, s32[2,4,8]{2,1,0:T(4,128)S(1)} %collective-permute-done.2.refs_3_), custom_call_target="tpu_custom_call" | custom-call | tf_op jit(solution)/shard_map/expand_factors/pallas_call | solution.py:138
  36.5 0.0 collective-permute-done.3.refs_0_.block
  36.6 0.3 collective-permute-start.9
  36.9 0.0 collective-permute-done.5.refs_0_
  36.9 0.0 collective-permute-start.7
  36.9 0.0 collective-permute-done.6.refs_1_
  36.9 0.5 %collective-permute-start.8 = (bf16[2,256,256]{2,1,0:T(8,128)(2,1)S(1)}, bf16[2,256,256]{2,1,0:T(8,128)(2,1)S(1)}, u32[]{:S(2)}, u32[]{:S(2)}) collective-permute-start(bf16[2,256,256]{2,1,0:T(8,128)(2,1)S(1)} %collective-permute-done.6.refs_1_), channel_id=1, source_target_pairs={{0,1},{1,0},{2,3},{3,2},{4,5},{5,4},{6,7},{7,6},{8,9},{9,8},{10,11... | collective-permute-start | bytes 786440 | tf_op jit(solution)/shard_map/ppermute | solution.py:422
  37.4 0.0 collective-permute-done.4.refs_1_
  37.4 0.0 copy-done.3
  37.4 0.0 copy-start
  37.4 1.2 %copy-done = bf16[8,256,256]{2,1,0:T(8,128)(2,1)S(1)} copy-done((bf16[8,256,256]{2,1,0:T(8,128)(2,1)S(1)}, bf16[8,256,256]{2,1,0:T(8,128)(2,1)}, u32[]{:S(2)}) %copy-start) | copy-done | bytes 1048600
  38.7 0.7 %early_product.1 = (bf16[256,4096]{1,0:T(8,128)(2,1)S(1)}, f32[256,256]{1,0:T(8,128)S(1)}) custom-call(bf16[8,256,256]{2,1,0:T(8,128)(2,1)S(1)} %copy-done, bf16[4,2,128,256]{3,2,1,0:T(8,128)(2,1)S(1)} %expand_factors.1.factors, bf16[4,128,256]{2,1,0:T(8,128)(2,1)S(1)} %copy-done.3, bf16[4,128,256]{2,1,0:T(8,128)(2,1)S(1)} %collective-permute-done.3.refs_0_.block, ...), custom_call_target="tpu_custom_call" | custom-call | flops 10737418240 | bytes 4194304 | tf_op jit(solution)/shard_map/early_product/pallas_call | solution.py:326
  39.4 0.0 copy-start.1
  39.4 0.0 copy-start.2
  39.4 0.0 collective-permute-done.7.refs_2_
  39.4 0.0 collective-permute-done.8.refs_3_
  39.4 0.5 shares_product.1.middle
  39.9 4.9 %collective-permute-done.9.last = bf16[4,128,256]{2,1,0:T(8,128)(2,1)S(1)} collective-permute-done((bf16[4,128,256]{2,1,0:T(8,128)(2,1)S(1)}, bf16[4,128,256]{2,1,0:T(8,128)(2,1)S(1)}, u32[]{:S(2)}, u32[]{:S(2)}) %collective-permute-start.9) | collective-permute-done | bytes 262176 | tf_op jit(solution)/shard_map/ppermute | solution.py:404
  44.8 0.0 copy-done.1
  44.8 0.0 copy-done.2
  44.8 1.1 %commutator.1 = f32[2,128,256]{2,1,0:T(8,128)} custom-call(f32[2,128,256]{2,1,0:T(8,128)S(1)} %copy-done.2, bf16[8,256,256]{2,1,0:T(8,128)(2,1)S(1)} %copy-done.1, bf16[4,2,128,256]{3,2,1,0:T(8,128)(2,1)S(1)} %expand_factors.1.factors, f32[256,256]{1,0:T(8,128)S(1)} %shares_product.1.middle, bf16[4,128,256]{2,1,0:T(8,128)(2,1)S(1)} %collective-permute-done.9.last, ...), custom_call_target="tpu_custom_call" | custom-call | tf_op jit(solution)/shard_map/commutator/pallas_call | solution.py:428
  (2 shorter events, 0.0 us)
Async XLA Ops:
  0.0 18.1 %copy-start.4 = (s32[8,4]{0,1:T(4,128)S(1)}, s32[8,4]{0,1:T(4,128)}, u32[]{:S(2)}) copy-start(s32[8,4]{0,1:T(4,128)} %param.9) | copy-start | bytes 388
  0.0 18.1 %copy-start.5 = (s32[8,4]{0,1:T(4,128)S(1)}, s32[8,4]{0,1:T(4,128)}, u32[]{:S(2)}) copy-start(s32[8,4]{0,1:T(4,128)} %param.10) | copy-start | bytes 388
  9.1 28.4 %copy-start.3 = (bf16[4,128,256]{2,1,0:T(8,128)(2,1)S(1)}, bf16[4,128,256]{2,1,0:T(8,128)(2,1)}, u32[]{:S(2)}) copy-start(bf16[4,128,256]{2,1,0:T(8,128)(2,1)} %cut_strip.1.own) | copy-start | bytes 786436
  9.1 27.5 %collective-permute-start.3 = (bf16[4,128,256]{2,1,0:T(8,128)(2,1)}, bf16[4,128,256]{2,1,0:T(8,128)(2,1)S(1)}, u32[]{:S(2)}, u32[]{:S(2)}) collective-permute-start(bf16[4,128,256]{2,1,0:T(8,128)(2,1)} %cut_strip.1.own), channel_id=1, source_target_pairs={{0,4},{4,8},{8,12},{12,0},{1,5},{5,9},{9,13},{13,1},{2,6},{6,10},{... | collective-permute-start | bytes 786440 | tf_op jit(solution)/shard_map/ppermute | solution.py:404
  14.0 22.9 %collective-permute-start.5 = (bf16[2,256,256]{2,1,0:T(8,128)(2,1)}, bf16[2,256,256]{2,1,0:T(8,128)(2,1)S(1)}, u32[]{:S(2)}, u32[]{:S(2)}) collective-permute-start(bf16[2,256,256]{2,1,0:T(8,128)(2,1)} %get-tuple-element.15), channel_id=1, source_target_pairs={{0,16},{16,0},{1,17},{17,1},{2,18},{18,2},{3,19},{19,3},{4,20},{20... | collective-permute-start | bytes 786440 | tf_op jit(solution)/shard_map/ppermute | solution.py:418
  15.6 21.4 %collective-permute-start.6 = (bf16[2,256,256]{2,1,0:T(8,128)(2,1)}, bf16[2,256,256]{2,1,0:T(8,128)(2,1)S(1)}, u32[]{:S(2)}, u32[]{:S(2)}) collective-permute-start(bf16[2,256,256]{2,1,0:T(8,128)(2,1)} %get-tuple-element.16), channel_id=1, source_target_pairs={{0,16},{16,0},{1,17},{17,1},{2,18},{18,2},{3,19},{19,3},{4,20},{20... | collective-permute-start | bytes 786440 | tf_op jit(solution)/shard_map/ppermute | solution.py:418
  16.1 21.4 %collective-permute-start.4 = (bf16[4,128,256]{2,1,0:T(8,128)(2,1)}, bf16[4,128,256]{2,1,0:T(8,128)(2,1)S(1)}, u32[]{:S(2)}, u32[]{:S(2)}) collective-permute-start(bf16[4,128,256]{2,1,0:T(8,128)(2,1)} %cut_strip.1.own), channel_id=1, source_target_pairs={{0,12},{4,0},{8,4},{12,8},{1,13},{5,1},{9,5},{13,9},{2,14},{6,2},{... | collective-permute-start | bytes 786440 | tf_op jit(solution)/shard_map/ppermute | solution.py:406
  18.2 8.3 %collective-permute-start = (s32[2,4,8]{2,1,0:T(4,128)S(1)}, s32[2,4,8]{2,1,0:T(4,128)S(1)}, u32[]{:S(2)}, u32[]{:S(2)}) collective-permute-start(s32[2,4,8]{2,1,0:T(4,128)S(1)} %pad_add_fusion.refs_0_), channel_id=1, source_target_pairs={{0,4},{4,8},{8,12},{12,0},{1,5},{5,9},{9,13},{13,1},{2,6},{6,10},{... | collective-permute-start | bytes 776 | tf_op jit(solution)/shard_map/ppermute | solution.py:410
  26.4 4.5 %collective-permute-start.1 = (s32[2,4,8]{2,1,0:T(4,128)S(1)}, s32[2,4,8]{2,1,0:T(4,128)S(1)}, u32[]{:S(2)}, u32[]{:S(2)}) collective-permute-start(s32[2,4,8]{2,1,0:T(4,128)S(1)} %pad_add_fusion.refs_0_), channel_id=1, source_target_pairs={{0,8},{4,12},{8,0},{12,4},{1,9},{5,13},{9,1},{13,5},{2,10},{6,14},... | collective-permute-start | bytes 776 | tf_op jit(solution)/shard_map/ppermute | solution.py:410
  30.9 4.7 %collective-permute-start.2 = (s32[2,4,8]{2,1,0:T(4,128)S(1)}, s32[2,4,8]{2,1,0:T(4,128)S(1)}, u32[]{:S(2)}, u32[]{:S(2)}) collective-permute-start(s32[2,4,8]{2,1,0:T(4,128)S(1)} %pad_add_fusion.refs_0_), channel_id=1, source_target_pairs={{0,12},{4,0},{8,4},{12,8},{1,13},{5,1},{9,5},{13,9},{2,14},{6,2},{... | collective-permute-start | bytes 776 | tf_op jit(solution)/shard_map/ppermute | solution.py:410
  36.6 8.2 %collective-permute-start.9 = (bf16[4,128,256]{2,1,0:T(8,128)(2,1)S(1)}, bf16[4,128,256]{2,1,0:T(8,128)(2,1)S(1)}, u32[]{:S(2)}, u32[]{:S(2)}) collective-permute-start(bf16[4,128,256]{2,1,0:T(8,128)(2,1)S(1)} %relay.1), channel_id=1, source_target_pairs={{0,4},{4,8},{8,12},{12,0},{1,5},{5,9},{9,13},{13,1},{2,6},{6,10},{... | collective-permute-start | bytes 786440 | tf_op jit(solution)/shard_map/ppermute | solution.py:404
  36.9 2.5 %collective-permute-start.7 = (bf16[2,256,256]{2,1,0:T(8,128)(2,1)S(1)}, bf16[2,256,256]{2,1,0:T(8,128)(2,1)S(1)}, u32[]{:S(2)}, u32[]{:S(2)}) collective-permute-start(bf16[2,256,256]{2,1,0:T(8,128)(2,1)S(1)} %collective-permute-done.5.refs_0_), channel_id=1, source_target_pairs={{0,1},{1,0},{2,3},{3,2},{4,5},{5,4},{6,7},{7,6},{8,9},{9,8},{10,11... | collective-permute-start | bytes 786440 | tf_op jit(solution)/shard_map/ppermute | solution.py:422
  36.9 2.5 %collective-permute-start.8 = (bf16[2,256,256]{2,1,0:T(8,128)(2,1)S(1)}, bf16[2,256,256]{2,1,0:T(8,128)(2,1)S(1)}, u32[]{:S(2)}, u32[]{:S(2)}) collective-permute-start(bf16[2,256,256]{2,1,0:T(8,128)(2,1)S(1)} %collective-permute-done.6.refs_1_), channel_id=1, source_target_pairs={{0,1},{1,0},{2,3},{3,2},{4,5},{5,4},{6,7},{7,6},{8,9},{9,8},{10,11... | collective-permute-start | bytes 786440 | tf_op jit(solution)/shard_map/ppermute | solution.py:422
  37.4 1.2 %copy-start = (bf16[8,256,256]{2,1,0:T(8,128)(2,1)S(1)}, bf16[8,256,256]{2,1,0:T(8,128)(2,1)}, u32[]{:S(2)}) copy-start(bf16[8,256,256]{2,1,0:T(8,128)(2,1)} %get-tuple-element.12.near) | copy-start | bytes 3145732
  39.4 5.4 %copy-start.1 = (bf16[8,256,256]{2,1,0:T(8,128)(2,1)S(1)}, bf16[8,256,256]{2,1,0:T(8,128)(2,1)}, u32[]{:S(2)}) copy-start(bf16[8,256,256]{2,1,0:T(8,128)(2,1)} %get-tuple-element.12.near) | copy-start | bytes 3145732
  39.4 5.4 %copy-start.2 = (f32[2,128,256]{2,1,0:T(8,128)S(1)}, f32[2,128,256]{2,1,0:T(8,128)}, u32[]{:S(2)}) copy-start(f32[2,128,256]{2,1,0:T(8,128)} %get-tuple-element.11.damp) | copy-start | bytes 786436

commit v5 on v2

--- a/solution.py
+++ b/solution.py
@@ -221,15 +221,10 @@
         out_shape=jax.ShapeDtypeStruct(block.shape, block.dtype),
         compiler_params=params((block.shape, 4)),
         cost_estimate=pl.CostEstimate(
-            flops=100000000, bytes_accessed=4 * block.size, transcendentals=0
+            flops=40000000000, bytes_accessed=4 * block.size, transcendentals=0
         ),
         name="relay",
     )(block)
-
-
-def share_block(row, layer, index, rows_n, split, here, size):
-    other = lax.rem(row - index // split - 1 + rows_n, rows_n)
-    return other * here + (lax.rem(layer, split) ^ (index % split)) * size
 
 
 def products(left, block, right, first, count):
@@ -290,50 +285,58 @@
     )(*operands)
 
 
-def shares_kernel(rows_n, split, here, left, early, *refs):
-    shares, total = refs[:-1], refs[-1]
+def shares_kernel(rows_n, depth, left, early, *refs):
+    strips, total, far = refs[:-2], refs[-2], refs[-1]
+    rows, width = strips[0].shape[1:]
     row, layer = lax.axis_index("row"), lax.axis_index("depth")
+    count = far.shape[0] // (4 * (rows_n - 1))
+    for index, ref in enumerate(strips):
+        start = (layer ^ (index % depth)) * rows
+        block = (index // depth) * count + start // width
+        at = pl.ds(pl.multiple_of(lax.rem(start, width), rows), rows)
+        for slot in range(4):
+            far[4 * block + slot, at, :] = ref[(slot + 2) % 4]
     value = early[...]
-    for index in range(len(shares) // 2):
-        pair = shares[2 * index : 2 * index + 2]
-        size = pair[0].shape[0] // 2
-        block = share_block(row, layer, index, rows_n, split, here, size)
-        value += products(left, block, pair, 0, size)
+    for shift in range(rows_n - 1):
+        block = lax.rem(row - shift - 1 + rows_n, rows_n) * count
+        value += products(left, block, [far], shift * count, count)
     total[...] = value
 
 
-def shares_product(left, early, shares, rows_n, split, here):
-    operands = [left, early] + shares
-    return pl.pallas_call(
-        functools.partial(shares_kernel, rows_n, split, here),
+def shares_product(left, early, strips, rows_n, depth):
+    operands = [left, early] + strips
+    rows, width = strips[0].shape[1:]
+    far = (4 * len(strips) * rows // width, width, width)
+    return pl.pallas_call(
+        functools.partial(shares_kernel, rows_n, depth),
         in_specs=[VMEM] * len(operands),
-        out_specs=VMEM,
-        out_shape=jax.ShapeDtypeStruct(early.shape, early.dtype),
-        compiler_params=params((left.shape, 4), (early.shape, 12)),
+        out_specs=[VMEM, VMEM],
+        out_shape=[
+            jax.ShapeDtypeStruct(early.shape, early.dtype),
+            jax.ShapeDtypeStruct(far, left.dtype),
+        ],
+        compiler_params=params((left.shape, 4), (far, 4), (early.shape, 12)),
         cost_estimate=pl.CostEstimate(flops=1000000, bytes_accessed=1000000, transcendentals=0),
         name="shares_product",
     )(*operands)
 
 
-def product_kernel(rows_n, cols_n, split, damp, near, middle, last, *refs):
-    shares = refs[:-3]
-    out_ref, left_last, total = refs[-3:]
+def product_kernel(rows_n, cols_n, damp, near, far, middle, last, *refs):
+    out_ref, left_last, total = refs
     out_rows = last.shape[1]
-    row, layer = lax.axis_index("row"), lax.axis_index("depth")
+    row = lax.axis_index("row")
     place_left(left_last, last, 0)
-    here = near.shape[0] // 4
-    rights = [(row * here, here, [near])]
-    for index in range(len(shares) // 2):
-        pair = shares[2 * index : 2 * index + 2]
-        size = pair[0].shape[0] // 2
-        block = share_block(row, layer, index, rows_n, split, here, size)
-        rights.append((block, size, pair))
+    count = near.shape[0] // 4
+    rights = [(row * count, count, near, 0)]
+    for shift in range(rows_n - 1):
+        other = lax.rem(row - shift - 1 + rows_n, rows_n)
+        rights.append((other * count, count, far, shift * count))
     wanted = lax.rem(lax.axis_index("col") + cols_n - cols_n // 2, cols_n)
-    for block, size, right in rights:
+    for block, size, right, base in rights:
 
         @pl.when((wanted >= block) & (wanted < block + size))
         def _():
-            total[...] = middle[...] + products(left_last, 0, right, wanted - block, 1)
+            total[...] = middle[...] + products(left_last, 0, [right], base + wanted - block, 1)
 
     out_ref[0] = total[pl.ds(out_rows, out_rows), :] - damp[0]
     out_ref[1] = -total[pl.ds(0, out_rows), :] - damp[1]
@@ -343,10 +346,8 @@
     rows_n, cols_n, depth = (lax.axis_size(a) for a in ("row", "col", "depth"))
     here, width = k_parts.shape[1:]
     out_rows = here // depth
-    split = 2 if depth % 2 == 0 else 1
     k_mask, p_mask = k_mask.T, p_mask.T
     (strip,) = mask_rows(k_mask, p_mask, k_parts, p_parts, depth, 1, "mask_strip")
-    share = mask_rows(p_mask, k_mask, p_parts, k_parts, split, 2, "mask_share")
     ups, downs = [strip], [strip]
     for step in range(1, cols_n // 2 + 1):
         block = ups[-1] if step == 1 else relay(ups[-1])
@@ -356,21 +357,24 @@
     near, damp = local_part(
         k_mask, p_mask, atoms, classes, rates, k_parts, p_parts, strip
     )
-    shares = []
+    strips = []
     for shift in range(1, rows_n):
         perm = [(i, (i + shift) % rows_n) for i in range(rows_n)]
-        got = [lax.ppermute(part, "row", perm) for part in share]
-        shares += got
-        if split == 2:
-            swap = [(i, i ^ 1) for i in range(depth)]
-            shares += [lax.ppermute(part, "depth", swap) for part in got]
+        got = {0: lax.ppermute(strip, "row", perm)}
+        stride = depth // 2
+        while stride:
+            perm = [(i, i ^ stride) for i in range(depth)]
+            for flip in list(got):
+                got[flip ^ stride] = lax.ppermute(got[flip], "depth", perm)
+            stride //= 2
+        strips += [got[flip] for flip in range(depth)]
     blocks = ups[1:-1] + downs[1:]
     left, early = early_product(near, strip, blocks, cols_n)
-    middle = shares_product(left, early, shares, rows_n, split, here // width)
-    operands = [damp, near, middle, ups[-1]] + shares
+    middle, far = shares_product(left, early, strips, rows_n, depth)
+    operands = [damp, near, far, middle, ups[-1]]
     block, total = (2 * out_rows, 4 * width), (2 * out_rows, width)
     return pl.pallas_call(
-        functools.partial(product_kernel, rows_n, cols_n, split),
+        functools.partial(product_kernel, rows_n, cols_n),
         in_specs=[VMEM] * len(operands),
         out_specs=VMEM,
         out_shape=jax.ShapeDtypeStruct((2, out_rows, width), jnp.float32),

time: 25.9 us -> 27.1 us (1.046)
  waiting for transfers between devices: 8.27 us -> 11.3 us
  Pallas kernels: 8.77 us -> 7 us
  starting transfers between devices: 7.29 us -> 8.54 us
  local copies, waits for them, and re-layouts: 1.23 us -> 0.01 us
    ppermute x2, waiting for transfers between devices: 2.12 us -> 7.1 us  [body(): lax.ppermute(block, 'col', [(i, (i + 1) % cols_n) for i in range(cols_n)])]
    ppermute x4, waiting for transfers between devices: 6.14 us -> 2.78 us  [the longest x3 2.78 us: body(): got[flip ^ stride] = lax.ppermute(got[flip], 'depth', perm)]
    ppermute x4, starting transfers between devices: 2.1 us -> 4.66 us  [the longest x1 3 us: body(): got = {0: lax.ppermute(strip, 'row', perm)}]
    pallas_call x2 -> x1, Pallas kernels: 3.53 us -> 1.69 us  [mask_rows(): pl.pallas_call(functools.partial(rows_kernel, places), in_specs=[HBM] * 4...]
    ppermute x2, starting transfers between devices: 3.13 us -> 1.63 us  [body(): lax.ppermute(block, 'col', [(i, (i + 1) % cols_n) for i in range(cols_n)])]
    ppermute x1, waiting for transfers between devices: 0.01 us -> 1.39 us  [body(): lax.ppermute(downs[-1], 'col', [(i, (i - 1) % cols_n) for i in range(cols...]
    unnamed x8 -> x6, local copies, waits for them, and re-layouts: 1.23 us -> 0.01 us
  transfers between devices with their start and end apart: 7 -> 7, of which waited for: 4 -> 4; matrix products, arithmetic and copies ran while one was open for 0% -> 0% of each run, Pallas kernels for 23% -> 16%
where the time goes in v5:
time: 27.1 us; the launch traced here: 26.9 us
  waiting for transfers between devices  11.3 us (42%)
  starting transfers between devices  8.54 us (32%)
  Pallas kernels  7 us (26%)
    ppermute x2, waiting for transfers between devices, body(): lax.ppermute(block, 'col', [(i, (i + 1) % cols_n) for i in range(cols_n)])  7.1 us
    pallas_call x1, Pallas kernels, local_part(): pl.pallas_call(local_kernel, in_specs=[HBM] * 8, out_specs=[HBM, VMEM], o...  3.02 us
    ppermute x1, starting transfers between devices, body(): got = {0: lax.ppermute(strip, 'row', perm)}  3 us
    ppermute x3, waiting for transfers between devices, body(): got[flip ^ stride] = lax.ppermute(got[flip], 'depth', perm)  2.78 us
    ppermute x1, starting transfers between devices, body(): lax.ppermute(downs[-1], 'col', [(i, (i - 1) % cols_n) for i in range(cols...  2.25 us
    pallas_call x1, Pallas kernels, mask_rows(): pl.pallas_call(functools.partial(rows_kernel, places), in_specs=[HBM] * 4...  1.69 us
    ppermute x3, starting transfers between devices, body(): got[flip ^ stride] = lax.ppermute(got[flip], 'depth', perm)  1.66 us
    ppermute x2, starting transfers between devices, body(): lax.ppermute(block, 'col', [(i, (i + 1) % cols_n) for i in range(cols_n)])  1.63 us
  transfers between devices with their start and end apart: 7, of which 4 were waited for; matrix products, arithmetic and copies ran while one was open for 0% of the time, Pallas kernels for 16%

profile of v5, /device:TPU:0, one launch (start us, length us, event | category | flops | bytes accessed | tf_op | source)
XLA Modules:
  0.0 26.9 jit_solution(17524567435072275188)
XLA Ops:
  0.0 1.7 %mask_strip.1.strip.own = bf16[4,128,256]{2,1,0:T(8,128)(2,1)} custom-call(s32[4,8]{1,0:T(4,128)} %bitcast.2, s32[4,8]{1,0:T(4,128)} %bitcast.4, bf16[2,512,256]{2,1,0:T(8,128)(2,1)} %k_ref.1, bf16[2,512,256]{2,1,0:T(8,128)(2,1)} %p_ref.1), custom_call_target="tpu_custom_call" | custom-call | tf_op jit(solution)/shard_map/mask_strip/pallas_call | solution.py:81
  1.7 3.0 %collective-permute-start.2 = (bf16[4,128,256]{2,1,0:T(8,128)(2,1)}, bf16[4,128,256]{2,1,0:T(8,128)(2,1)S(1)}, u32[]{:S(2)}, u32[]{:S(2)}) collective-permute-start(bf16[4,128,256]{2,1,0:T(8,128)(2,1)} %mask_strip.1.strip.own), channel_id=1, source_target_pairs={{0,16},{16,0},{1,17},{17,1},{2,18},{18,2},{3,19},{19,3},{4,20},{20... | collective-permute-start | bytes 786440 | tf_op jit(solution)/shard_map/ppermute | solution.py:363
  4.7 1.6 %collective-permute-start = (bf16[4,128,256]{2,1,0:T(8,128)(2,1)}, bf16[4,128,256]{2,1,0:T(8,128)(2,1)S(1)}, u32[]{:S(2)}, u32[]{:S(2)}) collective-permute-start(bf16[4,128,256]{2,1,0:T(8,128)(2,1)} %mask_strip.1.strip.own), channel_id=1, source_target_pairs={{0,4},{4,8},{8,12},{12,0},{1,5},{5,9},{9,13},{13,1},{2,6},{6,10},{... | collective-permute-start | bytes 786440 | tf_op jit(solution)/shard_map/ppermute | solution.py:354
  6.3 2.2 %collective-permute-start.1 = (bf16[4,128,256]{2,1,0:T(8,128)(2,1)}, bf16[4,128,256]{2,1,0:T(8,128)(2,1)S(1)}, u32[]{:S(2)}, u32[]{:S(2)}) collective-permute-start(bf16[4,128,256]{2,1,0:T(8,128)(2,1)} %mask_strip.1.strip.own), channel_id=1, source_target_pairs={{0,12},{4,0},{8,4},{12,8},{1,13},{5,1},{9,5},{13,9},{2,14},{6,2},{... | collective-permute-start | bytes 786440 | tf_op jit(solution)/shard_map/ppermute | solution.py:356
  8.5 3.0 %local_part.1 = (bf16[8,256,256]{2,1,0:T(8,128)(2,1)}, f32[2,128,256]{2,1,0:T(8,128)}) custom-call(s32[4,8]{1,0:T(4,128)} %bitcast.3, s32[4,8]{1,0:T(4,128)} %bitcast.5, s32[16]{0:T(128)} %atoms_ref.1, s32[4,4]{1,0:T(4,128)} %classes_ref.1, f32[4]{0:T(128)} %rates_ref.1, bf16[2,512,256]{2,1,0:T(8,128)(2,1)} %k_ref.1, bf16[2,512,256]{2,1,0:T(8,128)(2,1)} %p_ref.1, ...), custom_call_target="tpu_custom_call" | custom-call | flops 1048576 | bytes 2621440 | tf_op jit(solution)/shard_map/local_part/pallas_call | solution.py:176
  11.6 0.0 copy-start
  11.6 0.0 copy-start.1
  11.6 0.0 collective-permute-done.2.refs_0_
  11.6 1.6 %collective-permute-start.4 = (bf16[4,128,256]{2,1,0:T(8,128)(2,1)S(1)}, bf16[4,128,256]{2,1,0:T(8,128)(2,1)S(1)}, u32[]{:S(2)}, u32[]{:S(2)}) collective-permute-start(bf16[4,128,256]{2,1,0:T(8,128)(2,1)S(1)} %collective-permute-done.2.refs_0_), channel_id=1, source_target_pairs={{0,2},{1,3},{2,0},{3,1},{4,6},{5,7},{6,4},{7,5},{8,10},{9,11},{10,... | collective-permute-start | bytes 786440 | tf_op jit(solution)/shard_map/ppermute | solution.py:368
  13.2 2.8 %collective-permute-done.refs_0_.block = bf16[4,128,256]{2,1,0:T(8,128)(2,1)S(1)} collective-permute-done((bf16[4,128,256]{2,1,0:T(8,128)(2,1)}, bf16[4,128,256]{2,1,0:T(8,128)(2,1)S(1)}, u32[]{:S(2)}, u32[]{:S(2)}) %collective-permute-start) | collective-permute-done | bytes 262176 | tf_op jit(solution)/shard_map/ppermute | solution.py:354
  16.0 0.1 collective-permute-start.6
  16.1 0.1 collective-permute-start.3
  16.1 2.8 %collective-permute-done.4.refs_2_ = bf16[4,128,256]{2,1,0:T(8,128)(2,1)S(1)} collective-permute-done((bf16[4,128,256]{2,1,0:T(8,128)(2,1)S(1)}, bf16[4,128,256]{2,1,0:T(8,128)(2,1)S(1)}, u32[]{:S(2)}, u32[]{:S(2)}) %collective-permute-start.4) | collective-permute-done | bytes 262176 | tf_op jit(solution)/shard_map/ppermute | solution.py:368
  18.9 0.0 collective-permute-start.5
  18.9 1.4 %collective-permute-done.1.refs_1_ = bf16[4,128,256]{2,1,0:T(8,128)(2,1)S(1)} collective-permute-done((bf16[4,128,256]{2,1,0:T(8,128)(2,1)}, bf16[4,128,256]{2,1,0:T(8,128)(2,1)S(1)}, u32[]{:S(2)}, u32[]{:S(2)}) %collective-permute-start.1) | collective-permute-done | bytes 262176 | tf_op jit(solution)/shard_map/ppermute | solution.py:356
  20.3 0.0 copy-done
  20.3 0.0 copy-done.1
  20.3 0.7 %early_product.1 = (bf16[256,4096]{1,0:T(8,128)(2,1)S(1)}, f32[256,256]{1,0:T(8,128)S(1)}) custom-call(bf16[8,256,256]{2,1,0:T(8,128)(2,1)S(1)} %copy-done, bf16[4,128,256]{2,1,0:T(8,128)(2,1)S(1)} %copy-done.1, bf16[4,128,256]{2,1,0:T(8,128)(2,1)S(1)} %collective-permute-done.refs_0_.block, bf16[4,128,256]{2,1,0:T(8,128)(2,1)S(1)} %collective-permute-done.1.refs_1_), custom_call_target="tpu_custom_call" | custom-call | flops 10737418240 | bytes 4194304 | tf_op jit(solution)/shard_map/early_product/pallas_call | solution.py:270
  21.0 0.0 copy-start.2
  21.0 0.0 collective-permute-done.3.refs_1_
  21.0 0.0 collective-permute-done.5.refs_3_
  21.0 0.5 %shares_product.1 = (f32[256,256]{1,0:T(8,128)S(1)}, bf16[8,256,256]{2,1,0:T(8,128)(2,1)S(1)}) custom-call(bf16[256,4096]{1,0:T(8,128)(2,1)S(1)} %get-tuple-element.13.left, f32[256,256]{1,0:T(8,128)S(1)} %get-tuple-element.14.early, bf16[4,128,256]{2,1,0:T(8,128)(2,1)S(1)} %collective-permute-done.2.refs_0_, ...), custom_call_target="tpu_custom_call" | custom-call | flops 1000000 | bytes 1000000 | tf_op jit(solution)/shard_map/shares_product/pallas_call | solution.py:310
  21.6 4.3 %collective-permute-done.6.last = bf16[4,128,256]{2,1,0:T(8,128)(2,1)S(1)} collective-permute-done((bf16[4,128,256]{2,1,0:T(8,128)(2,1)S(1)}, bf16[4,128,256]{2,1,0:T(8,128)(2,1)S(1)}, u32[]{:S(2)}, u32[]{:S(2)}) %collective-permute-start.6) | collective-permute-done | bytes 262176 | tf_op jit(solution)/shard_map/ppermute | solution.py:354
  25.8 0.0 copy-done.2
  25.9 1.1 %commutator.1 = f32[2,128,256]{2,1,0:T(8,128)} custom-call(f32[2,128,256]{2,1,0:T(8,128)S(1)} %copy-done.2, bf16[8,256,256]{2,1,0:T(8,128)(2,1)S(1)} %copy-done, bf16[8,256,256]{2,1,0:T(8,128)(2,1)S(1)} %get-tuple-element.15.far, f32[256,256]{1,0:T(8,128)S(1)} %get-tuple-element.16.middle, bf16[4,128,256]{2,1,0:T(8,128)(2,1)S(1)} %collective-permute-done.6.last), custom_call_target="tpu_custom_call" | custom-call | tf_op jit(solution)/shard_map/commutator/pallas_call | solution.py:376
  (1 shorter events, 0.0 us)
Async XLA Ops:
  1.7 9.9 %collective-permute-start.2 = (bf16[4,128,256]{2,1,0:T(8,128)(2,1)}, bf16[4,128,256]{2,1,0:T(8,128)(2,1)S(1)}, u32[]{:S(2)}, u32[]{:S(2)}) collective-permute-start(bf16[4,128,256]{2,1,0:T(8,128)(2,1)} %mask_strip.1.strip.own), channel_id=1, source_target_pairs={{0,16},{16,0},{1,17},{17,1},{2,18},{18,2},{3,19},{19,3},{4,20},{20... | collective-permute-start | bytes 786440 | tf_op jit(solution)/shard_map/ppermute | solution.py:363
  4.7 11.3 %collective-permute-start = (bf16[4,128,256]{2,1,0:T(8,128)(2,1)}, bf16[4,128,256]{2,1,0:T(8,128)(2,1)S(1)}, u32[]{:S(2)}, u32[]{:S(2)}) collective-permute-start(bf16[4,128,256]{2,1,0:T(8,128)(2,1)} %mask_strip.1.strip.own), channel_id=1, source_target_pairs={{0,4},{4,8},{8,12},{12,0},{1,5},{5,9},{9,13},{13,1},{2,6},{6,10},{... | collective-permute-start | bytes 786440 | tf_op jit(solution)/shard_map/ppermute | solution.py:354
  6.3 14.0 %collective-permute-start.1 = (bf16[4,128,256]{2,1,0:T(8,128)(2,1)}, bf16[4,128,256]{2,1,0:T(8,128)(2,1)S(1)}, u32[]{:S(2)}, u32[]{:S(2)}) collective-permute-start(bf16[4,128,256]{2,1,0:T(8,128)(2,1)} %mask_strip.1.strip.own), channel_id=1, source_target_pairs={{0,12},{4,0},{8,4},{12,8},{1,13},{5,1},{9,5},{13,9},{2,14},{6,2},{... | collective-permute-start | bytes 786440 | tf_op jit(solution)/shard_map/ppermute | solution.py:356
  11.6 8.8 %copy-start = (bf16[8,256,256]{2,1,0:T(8,128)(2,1)S(1)}, bf16[8,256,256]{2,1,0:T(8,128)(2,1)}, u32[]{:S(2)}) copy-start(bf16[8,256,256]{2,1,0:T(8,128)(2,1)} %get-tuple-element.12.near) | copy-start | bytes 3145732
  11.6 8.8 %copy-start.1 = (bf16[4,128,256]{2,1,0:T(8,128)(2,1)S(1)}, bf16[4,128,256]{2,1,0:T(8,128)(2,1)}, u32[]{:S(2)}) copy-start(bf16[4,128,256]{2,1,0:T(8,128)(2,1)} %mask_strip.1.strip.own) | copy-start | bytes 786436
  11.6 7.3 %collective-permute-start.4 = (bf16[4,128,256]{2,1,0:T(8,128)(2,1)S(1)}, bf16[4,128,256]{2,1,0:T(8,128)(2,1)S(1)}, u32[]{:S(2)}, u32[]{:S(2)}) collective-permute-start(bf16[4,128,256]{2,1,0:T(8,128)(2,1)S(1)} %collective-permute-done.2.refs_0_), channel_id=1, source_target_pairs={{0,2},{1,3},{2,0},{3,1},{4,6},{5,7},{6,4},{7,5},{8,10},{9,11},{10,... | collective-permute-start | bytes 786440 | tf_op jit(solution)/shard_map/ppermute | solution.py:368
  16.0 9.8 %collective-permute-start.6 = (bf16[4,128,256]{2,1,0:T(8,128)(2,1)S(1)}, bf16[4,128,256]{2,1,0:T(8,128)(2,1)S(1)}, u32[]{:S(2)}, u32[]{:S(2)}) collective-permute-start(bf16[4,128,256]{2,1,0:T(8,128)(2,1)S(1)} %relay.1), channel_id=1, source_target_pairs={{0,4},{4,8},{8,12},{12,0},{1,5},{5,9},{9,13},{13,1},{2,6},{6,10},{... | collective-permute-start | bytes 786440 | tf_op jit(solution)/shard_map/ppermute | solution.py:354
  16.1 4.9 %collective-permute-start.3 = (bf16[4,128,256]{2,1,0:T(8,128)(2,1)S(1)}, bf16[4,128,256]{2,1,0:T(8,128)(2,1)S(1)}, u32[]{:S(2)}, u32[]{:S(2)}) collective-permute-start(bf16[4,128,256]{2,1,0:T(8,128)(2,1)S(1)} %collective-permute-done.2.refs_0_), channel_id=1, source_target_pairs={{0,1},{1,0},{2,3},{3,2},{4,5},{5,4},{6,7},{7,6},{8,9},{9,8},{10,11... | collective-permute-start | bytes 786440 | tf_op jit(solution)/shard_map/ppermute | solution.py:368
  18.9 2.1 %collective-permute-start.5 = (bf16[4,128,256]{2,1,0:T(8,128)(2,1)S(1)}, bf16[4,128,256]{2,1,0:T(8,128)(2,1)S(1)}, u32[]{:S(2)}, u32[]{:S(2)}) collective-permute-start(bf16[4,128,256]{2,1,0:T(8,128)(2,1)S(1)} %collective-permute-done.4.refs_2_), channel_id=1, source_target_pairs={{0,1},{1,0},{2,3},{3,2},{4,5},{5,4},{6,7},{7,6},{8,9},{9,8},{10,11... | collective-permute-start | bytes 786440 | tf_op jit(solution)/shard_map/ppermute | solution.py:368
  21.0 4.9 %copy-start.2 = (f32[2,128,256]{2,1,0:T(8,128)S(1)}, f32[2,128,256]{2,1,0:T(8,128)}, u32[]{:S(2)}) copy-start(f32[2,128,256]{2,1,0:T(8,128)} %get-tuple-element.11.damp) | copy-start | bytes 786436

commit v6 on v2

--- a/solution.py
+++ b/solution.py
@@ -351,6 +351,7 @@
     for step in range(1, cols_n // 2 + 1):
         block = ups[-1] if step == 1 else relay(ups[-1])
         ups.append(lax.ppermute(block, "col", [(i, (i + 1) % cols_n) for i in range(cols_n)]))
+    downs[0] = lax.optimization_barrier((strip, ups[1]))[0]
     for step in range(1, cols_n - cols_n // 2):
         downs.append(lax.ppermute(downs[-1], "col", [(i, (i - 1) % cols_n) for i in range(cols_n)]))
     near, damp = local_part(

time: 25.9 us -> 28.2 us (1.089)
  waiting for transfers between devices: 8.27 us -> 10.6 us
    ppermute x2, waiting for transfers between devices: 2.12 us -> 6.93 us  [body(): lax.ppermute(block, 'col', [(i, (i + 1) % cols_n) for i in range(cols_n)])]
    ppermute x2, waiting for transfers between devices: 6.14 us -> 1.82 us  [body(): got = [lax.ppermute(part, 'row', perm) for part in share]]
    ppermute x1, waiting for transfers between devices: 0.01 us -> 1.85 us  [body(): lax.ppermute(downs[-1], 'col', [(i, (i - 1) % cols_n) for i in range(cols...]
    ppermute x1, starting transfers between devices: 2.05 us -> 1.73 us  [body(): lax.ppermute(downs[-1], 'col', [(i, (i - 1) % cols_n) for i in range(cols...]
    ppermute x2, starting transfers between devices: 3.13 us -> 3.42 us  [body(): lax.ppermute(block, 'col', [(i, (i + 1) % cols_n) for i in range(cols_n)])]
  transfers between devices with their start and end apart: 7 -> 7, of which waited for: 4 -> 4; matrix products, arithmetic and copies ran while one was open for 0% -> 0% of each run, Pallas kernels for 23% -> 21%
where the time goes in v6:
time: 28.2 us; the launch traced here: 28 us
  waiting for transfers between devices  10.6 us (38%)
  Pallas kernels  8.76 us (31%)
  starting transfers between devices  7.25 us (26%)
  local copies, waits for them, and re-layouts  1.24 us (4%)
    ppermute x2, waiting for transfers between devices, body(): lax.ppermute(block, 'col', [(i, (i + 1) % cols_n) for i in range(cols_n)])  6.93 us
    pallas_call x2, Pallas kernels, mask_rows(): pl.pallas_call(functools.partial(rows_kernel, places), in_specs=[HBM] * 4...  3.53 us
    ppermute x2, starting transfers between devices, body(): lax.ppermute(block, 'col', [(i, (i + 1) % cols_n) for i in range(cols_n)])  3.42 us
    pallas_call x1, Pallas kernels, local_part(): pl.pallas_call(local_kernel, in_specs=[HBM] * 8, out_specs=[HBM, VMEM], o...  3.02 us
    ppermute x2, starting transfers between devices, body(): got = [lax.ppermute(part, 'row', perm) for part in share]  2.09 us
    ppermute x1, waiting for transfers between devices, body(): lax.ppermute(downs[-1], 'col', [(i, (i - 1) % cols_n) for i in range(cols...  1.85 us
    ppermute x2, waiting for transfers between devices, body(): got = [lax.ppermute(part, 'row', perm) for part in share]  1.82 us
    ppermute x1, starting transfers between devices, body(): lax.ppermute(downs[-1], 'col', [(i, (i - 1) % cols_n) for i in range(cols...  1.73 us
  transfers between devices with their start and end apart: 7, of which 4 were waited for; matrix products, arithmetic and copies ran while one was open for 0% of the time, Pallas kernels for 21%

profile of v6, /device:TPU:0, one launch (start us, length us, event | category | flops | bytes accessed | tf_op | source)
XLA Modules:
  0.0 28.0 jit_solution(14268539793029909069)
XLA Ops:
  0.0 1.7 %mask_strip.1.strip.own = bf16[4,128,256]{2,1,0:T(8,128)(2,1)} custom-call(s32[4,8]{1,0:T(4,128)} %bitcast.2, s32[4,8]{1,0:T(4,128)} %bitcast.5, bf16[2,512,256]{2,1,0:T(8,128)(2,1)} %second_ref.3, bf16[2,512,256]{2,1,0:T(8,128)(2,1)} %first_ref.3), custom_call_target="tpu_custom_call" | custom-call | tf_op jit(solution)/shard_map/mask_strip/pallas_call | solution.py:81
  1.7 0.0 copy-start.2
  1.7 3.1 %collective-permute-start = (bf16[4,128,256]{2,1,0:T(8,128)(2,1)}, bf16[4,128,256]{2,1,0:T(8,128)(2,1)S(1)}, u32[]{:S(2)}, u32[]{:S(2)}) collective-permute-start(bf16[4,128,256]{2,1,0:T(8,128)(2,1)} %mask_strip.1.strip.own), channel_id=1, source_target_pairs={{0,4},{4,8},{8,12},{12,0},{1,5},{5,9},{9,13},{13,1},{2,6},{6,10},{... | collective-permute-start | bytes 786440 | tf_op jit(solution)/shard_map/ppermute | solution.py:353
  4.8 1.8 %mask_share.1 = (bf16[2,256,256]{2,1,0:T(8,128)(2,1)}, bf16[2,256,256]{2,1,0:T(8,128)(2,1)}) custom-call(s32[4,8]{1,0:T(4,128)} %bitcast.6, s32[4,8]{1,0:T(4,128)} %bitcast.3, bf16[2,512,256]{2,1,0:T(8,128)(2,1)} %first_ref.3, bf16[2,512,256]{2,1,0:T(8,128)(2,1)} %second_ref.3), custom_call_target="tpu_custom_call" | custom-call | tf_op jit(solution)/shard_map/mask_share/pallas_call | solution.py:81
  6.6 1.6 %collective-permute-start.2 = (bf16[2,256,256]{2,1,0:T(8,128)(2,1)}, bf16[2,256,256]{2,1,0:T(8,128)(2,1)S(1)}, u32[]{:S(2)}, u32[]{:S(2)}) collective-permute-start(bf16[2,256,256]{2,1,0:T(8,128)(2,1)} %get-tuple-element.17), channel_id=1, source_target_pairs={{0,16},{16,0},{1,17},{17,1},{2,18},{18,2},{3,19},{19,3},{4,20},{20... | collective-permute-start | bytes 786440 | tf_op jit(solution)/shard_map/ppermute | solution.py:363
  8.2 0.5 %collective-permute-start.3 = (bf16[2,256,256]{2,1,0:T(8,128)(2,1)}, bf16[2,256,256]{2,1,0:T(8,128)(2,1)S(1)}, u32[]{:S(2)}, u32[]{:S(2)}) collective-permute-start(bf16[2,256,256]{2,1,0:T(8,128)(2,1)} %get-tuple-element.18), channel_id=1, source_target_pairs={{0,16},{16,0},{1,17},{17,1},{2,18},{18,2},{3,19},{19,3},{4,20},{20... | collective-permute-start | bytes 786440 | tf_op jit(solution)/shard_map/ppermute | solution.py:363
  8.7 4.6 %collective-permute-done.refs_0_.block = bf16[4,128,256]{2,1,0:T(8,128)(2,1)S(1)} collective-permute-done((bf16[4,128,256]{2,1,0:T(8,128)(2,1)}, bf16[4,128,256]{2,1,0:T(8,128)(2,1)S(1)}, u32[]{:S(2)}, u32[]{:S(2)}) %collective-permute-start) | collective-permute-done | bytes 262176 | tf_op jit(solution)/shard_map/ppermute | solution.py:353
  13.3 1.7 %collective-permute-start.1 = (bf16[4,128,256]{2,1,0:T(8,128)(2,1)}, bf16[4,128,256]{2,1,0:T(8,128)(2,1)S(1)}, u32[]{:S(2)}, u32[]{:S(2)}) collective-permute-start(bf16[4,128,256]{2,1,0:T(8,128)(2,1)} %mask_strip.1.strip.own), channel_id=1, source_target_pairs={{0,12},{4,0},{8,4},{12,8},{1,13},{5,1},{9,5},{13,9},{2,14},{6,2},{... | collective-permute-start | bytes 786440 | tf_op jit(solution)/shard_map/ppermute | solution.py:356
  15.1 3.0 %local_part.1 = (bf16[8,256,256]{2,1,0:T(8,128)(2,1)}, f32[2,128,256]{2,1,0:T(8,128)}) custom-call(s32[4,8]{1,0:T(4,128)} %bitcast.4, s32[4,8]{1,0:T(4,128)} %bitcast.7, s32[16]{0:T(128)} %atoms_ref.1, s32[4,4]{1,0:T(4,128)} %classes_ref.1, f32[4]{0:T(128)} %rates_ref.1, bf16[2,512,256]{2,1,0:T(8,128)(2,1)} %second_ref.3, bf16[2,512,256]{2,1,0:T(8,128)(2,1)} %first_ref.3, ...), custom_call_target="tpu_custom_call" | custom-call | flops 1048576 | bytes 2621440 | tf_op jit(solution)/shard_map/local_part/pallas_call | solution.py:176
  18.1 0.3 %collective-permute-start.6 = (bf16[4,128,256]{2,1,0:T(8,128)(2,1)S(1)}, bf16[4,128,256]{2,1,0:T(8,128)(2,1)S(1)}, u32[]{:S(2)}, u32[]{:S(2)}) collective-permute-start(bf16[4,128,256]{2,1,0:T(8,128)(2,1)S(1)} %relay.1), channel_id=1, source_target_pairs={{0,4},{4,8},{8,12},{12,0},{1,5},{5,9},{9,13},{13,1},{2,6},{6,10},{... | collective-permute-start | bytes 786440 | tf_op jit(solution)/shard_map/ppermute | solution.py:353
  18.5 0.0 collective-permute-done.2.refs_0_
  18.5 0.0 collective-permute-start.4
  18.5 1.8 %collective-permute-done.3.refs_1_ = bf16[2,256,256]{2,1,0:T(8,128)(2,1)S(1)} collective-permute-done((bf16[2,256,256]{2,1,0:T(8,128)(2,1)}, bf16[2,256,256]{2,1,0:T(8,128)(2,1)S(1)}, u32[]{:S(2)}, u32[]{:S(2)}) %collective-permute-start.3) | collective-permute-done | bytes 262176 | tf_op jit(solution)/shard_map/ppermute | solution.py:363
  20.3 0.0 collective-permute-start.5
  20.3 1.9 %collective-permute-done.1.refs_1_ = bf16[4,128,256]{2,1,0:T(8,128)(2,1)S(1)} collective-permute-done((bf16[4,128,256]{2,1,0:T(8,128)(2,1)}, bf16[4,128,256]{2,1,0:T(8,128)(2,1)S(1)}, u32[]{:S(2)}, u32[]{:S(2)}) %collective-permute-start.1) | collective-permute-done | bytes 262176 | tf_op jit(solution)/shard_map/ppermute | solution.py:356
  22.1 0.0 copy-done.2
  22.1 0.0 copy-start
  22.2 1.2 %copy-done = bf16[8,256,256]{2,1,0:T(8,128)(2,1)S(1)} copy-done((bf16[8,256,256]{2,1,0:T(8,128)(2,1)S(1)}, bf16[8,256,256]{2,1,0:T(8,128)(2,1)}, u32[]{:S(2)}) %copy-start) | copy-done | bytes 1048600
  23.4 0.7 %early_product.1 = (bf16[256,4096]{1,0:T(8,128)(2,1)S(1)}, f32[256,256]{1,0:T(8,128)S(1)}) custom-call(bf16[8,256,256]{2,1,0:T(8,128)(2,1)S(1)} %copy-done, bf16[4,128,256]{2,1,0:T(8,128)(2,1)S(1)} %copy-done.2, bf16[4,128,256]{2,1,0:T(8,128)(2,1)S(1)} %collective-permute-done.refs_0_.block, bf16[4,128,256]{2,1,0:T(8,128)(2,1)S(1)} %collective-permute-done.1.refs_1_), custom_call_target="tpu_custom_call" | custom-call | flops 10737418240 | bytes 4194304 | tf_op jit(solution)/shard_map/early_product/pallas_call | solution.py:275
  24.0 0.0 copy-start.1
  24.1 0.0 copy-start.3
  24.1 0.0 collective-permute-done.4.refs_2_
  24.1 0.0 collective-permute-done.5.refs_3_
  24.1 0.5 %shares_product.1.middle = f32[256,256]{1,0:T(8,128)S(1)} custom-call(bf16[256,4096]{1,0:T(8,128)(2,1)S(1)} %get-tuple-element.15.left, f32[256,256]{1,0:T(8,128)S(1)} %get-tuple-element.16.early, bf16[2,256,256]{2,1,0:T(8,128)(2,1)S(1)} %collective-permute-done.2.refs_0_, bf16[2,256,256]{2,1,0:T(8,128)(2,1)S(1)} %collective-permute-done.3.refs_1_, ...), custom_call_target="tpu_custom_call" | custom-call | flops 1000000 | bytes 1000000 | tf_op jit(solution)/shard_map/shares_product/pallas_call | solution.py:307
  24.5 2.3 %collective-permute-done.6.last = bf16[4,128,256]{2,1,0:T(8,128)(2,1)S(1)} collective-permute-done((bf16[4,128,256]{2,1,0:T(8,128)(2,1)S(1)}, bf16[4,128,256]{2,1,0:T(8,128)(2,1)S(1)}, u32[]{:S(2)}, u32[]{:S(2)}) %collective-permute-start.6) | collective-permute-done | bytes 262176 | tf_op jit(solution)/shard_map/ppermute | solution.py:353
  26.9 0.0 copy-done.1
  26.9 0.0 copy-done.3
  26.9 1.1 %commutator.1 = f32[2,128,256]{2,1,0:T(8,128)} custom-call(f32[2,128,256]{2,1,0:T(8,128)S(1)} %copy-done.3, bf16[8,256,256]{2,1,0:T(8,128)(2,1)S(1)} %copy-done.1, f32[256,256]{1,0:T(8,128)S(1)} %shares_product.1.middle, bf16[4,128,256]{2,1,0:T(8,128)(2,1)S(1)} %collective-permute-done.6.last, bf16[2,256,256]{2,1,0:T(8,128)(2,1)S(1)} %collective-permute-done.2.refs_0_, ...), custom_call_target="tpu_custom_call" | custom-call | tf_op jit(solution)/shard_map/commutator/pallas_call | solution.py:373
  (1 shorter events, 0.0 us)
Async XLA Ops:
  1.7 20.5 %copy-start.2 = (bf16[4,128,256]{2,1,0:T(8,128)(2,1)S(1)}, bf16[4,128,256]{2,1,0:T(8,128)(2,1)}, u32[]{:S(2)}) copy-start(bf16[4,128,256]{2,1,0:T(8,128)(2,1)} %mask_strip.1.strip.own) | copy-start | bytes 786436
  1.7 11.6 %collective-permute-start = (bf16[4,128,256]{2,1,0:T(8,128)(2,1)}, bf16[4,128,256]{2,1,0:T(8,128)(2,1)S(1)}, u32[]{:S(2)}, u32[]{:S(2)}) collective-permute-start(bf16[4,128,256]{2,1,0:T(8,128)(2,1)} %mask_strip.1.strip.own), channel_id=1, source_target_pairs={{0,4},{4,8},{8,12},{12,0},{1,5},{5,9},{9,13},{13,1},{2,6},{6,10},{... | collective-permute-start | bytes 786440 | tf_op jit(solution)/shard_map/ppermute | solution.py:353
  6.6 11.8 %collective-permute-start.2 = (bf16[2,256,256]{2,1,0:T(8,128)(2,1)}, bf16[2,256,256]{2,1,0:T(8,128)(2,1)S(1)}, u32[]{:S(2)}, u32[]{:S(2)}) collective-permute-start(bf16[2,256,256]{2,1,0:T(8,128)(2,1)} %get-tuple-element.17), channel_id=1, source_target_pairs={{0,16},{16,0},{1,17},{17,1},{2,18},{18,2},{3,19},{19,3},{4,20},{20... | collective-permute-start | bytes 786440 | tf_op jit(solution)/shard_map/ppermute | solution.py:363
  8.2 12.1 %collective-permute-start.3 = (bf16[2,256,256]{2,1,0:T(8,128)(2,1)}, bf16[2,256,256]{2,1,0:T(8,128)(2,1)S(1)}, u32[]{:S(2)}, u32[]{:S(2)}) collective-permute-start(bf16[2,256,256]{2,1,0:T(8,128)(2,1)} %get-tuple-element.18), channel_id=1, source_target_pairs={{0,16},{16,0},{1,17},{17,1},{2,18},{18,2},{3,19},{19,3},{4,20},{20... | collective-permute-start | bytes 786440 | tf_op jit(solution)/shard_map/ppermute | solution.py:363
  13.3 8.8 %collective-permute-start.1 = (bf16[4,128,256]{2,1,0:T(8,128)(2,1)}, bf16[4,128,256]{2,1,0:T(8,128)(2,1)S(1)}, u32[]{:S(2)}, u32[]{:S(2)}) collective-permute-start(bf16[4,128,256]{2,1,0:T(8,128)(2,1)} %mask_strip.1.strip.own), channel_id=1, source_target_pairs={{0,12},{4,0},{8,4},{12,8},{1,13},{5,1},{9,5},{13,9},{2,14},{6,2},{... | collective-permute-start | bytes 786440 | tf_op jit(solution)/shard_map/ppermute | solution.py:356
  18.1 8.7 %collective-permute-start.6 = (bf16[4,128,256]{2,1,0:T(8,128)(2,1)S(1)}, bf16[4,128,256]{2,1,0:T(8,128)(2,1)S(1)}, u32[]{:S(2)}, u32[]{:S(2)}) collective-permute-start(bf16[4,128,256]{2,1,0:T(8,128)(2,1)S(1)} %relay.1), channel_id=1, source_target_pairs={{0,4},{4,8},{8,12},{12,0},{1,5},{5,9},{9,13},{13,1},{2,6},{6,10},{... | collective-permute-start | bytes 786440 | tf_op jit(solution)/shard_map/ppermute | solution.py:353
  18.5 5.6 %collective-permute-start.4 = (bf16[2,256,256]{2,1,0:T(8,128)(2,1)S(1)}, bf16[2,256,256]{2,1,0:T(8,128)(2,1)S(1)}, u32[]{:S(2)}, u32[]{:S(2)}) collective-permute-start(bf16[2,256,256]{2,1,0:T(8,128)(2,1)S(1)} %collective-permute-done.2.refs_0_), channel_id=1, source_target_pairs={{0,1},{1,0},{2,3},{3,2},{4,5},{5,4},{6,7},{7,6},{8,9},{9,8},{10,11... | collective-permute-start | bytes 786440 | tf_op jit(solution)/shard_map/ppermute | solution.py:367
  20.3 3.8 %collective-permute-start.5 = (bf16[2,256,256]{2,1,0:T(8,128)(2,1)S(1)}, bf16[2,256,256]{2,1,0:T(8,128)(2,1)S(1)}, u32[]{:S(2)}, u32[]{:S(2)}) collective-permute-start(bf16[2,256,256]{2,1,0:T(8,128)(2,1)S(1)} %collective-permute-done.3.refs_1_), channel_id=1, source_target_pairs={{0,1},{1,0},{2,3},{3,2},{4,5},{5,4},{6,7},{7,6},{8,9},{9,8},{10,11... | collective-permute-start | bytes 786440 | tf_op jit(solution)/shard_map/ppermute | solution.py:367
  22.1 1.2 %copy-start = (bf16[8,256,256]{2,1,0:T(8,128)(2,1)S(1)}, bf16[8,256,256]{2,1,0:T(8,128)(2,1)}, u32[]{:S(2)}) copy-start(bf16[8,256,256]{2,1,0:T(8,128)(2,1)} %get-tuple-element.13.near) | copy-start | bytes 3145732
  24.0 2.8 %copy-start.1 = (bf16[8,256,256]{2,1,0:T(8,128)(2,1)S(1)}, bf16[8,256,256]{2,1,0:T(8,128)(2,1)}, u32[]{:S(2)}) copy-start(bf16[8,256,256]{2,1,0:T(8,128)(2,1)} %get-tuple-element.13.near) | copy-start | bytes 3145732
  24.1 2.8 %copy-start.3 = (f32[2,128,256]{2,1,0:T(8,128)S(1)}, f32[2,128,256]{2,1,0:T(8,128)}, u32[]{:S(2)}) copy-start(f32[2,128,256]{2,1,0:T(8,128)} %get-tuple-element.12.damp) | copy-start | bytes 786436

commit v7 on v2

--- a/solution.py
+++ b/solution.py
@@ -201,24 +201,26 @@
 
 
 def place_left(left, ref, block):
-    rows, width = ref.shape[1:]
-    k_re, k_im, p_re, p_im = ref[0], ref[1], ref[2], ref[3]
+    k_ref, p_ref = ref if isinstance(ref, tuple) else (ref.at[pl.ds(0, 2)], ref.at[pl.ds(2, 2)])
+    rows, width = k_ref.shape[1:]
+    k_re, k_im, p_re, p_im = k_ref[0], k_ref[1], p_ref[0], p_ref[1]
     for half, parts in enumerate(((k_re, -k_im, -p_re, p_im), (k_im, k_re, -p_im, -p_re))):
         for slot, part in enumerate(parts):
             at = pl.multiple_of((4 * block + slot) * width, width)
             left[pl.ds(half * rows, rows), pl.ds(at, width)] = part
 
 
-def relay_kernel(block, out):
-    out[...] = block[...]
+def relay_kernel(block, k_out, p_out):
+    k_out[...] = block[:2]
+    p_out[...] = block[2:]
 
 
 def relay(block):
     return pl.pallas_call(
         relay_kernel,
         in_specs=[VMEM],
-        out_specs=VMEM,
-        out_shape=jax.ShapeDtypeStruct(block.shape, block.dtype),
+        out_specs=[VMEM] * 2,
+        out_shape=[jax.ShapeDtypeStruct((2,) + block.shape[1:], block.dtype)] * 2,
         compiler_params=params((block.shape, 4)),
         cost_estimate=pl.CostEstimate(
             flops=100000000, bytes_accessed=4 * block.size, transcendentals=0
@@ -315,12 +317,12 @@
     )(*operands)
 
 
-def product_kernel(rows_n, cols_n, split, damp, near, middle, last, *refs):
+def product_kernel(rows_n, cols_n, split, damp, near, middle, last_k, last_p, *refs):
     shares = refs[:-3]
     out_ref, left_last, total = refs[-3:]
-    out_rows = last.shape[1]
+    out_rows = last_k.shape[1]
     row, layer = lax.axis_index("row"), lax.axis_index("depth")
-    place_left(left_last, last, 0)
+    place_left(left_last, (last_k, last_p), 0)
     here = near.shape[0] // 4
     rights = [(row * here, here, [near])]
     for index in range(len(shares) // 2):
@@ -348,9 +350,11 @@
     (strip,) = mask_rows(k_mask, p_mask, k_parts, p_parts, depth, 1, "mask_strip")
     share = mask_rows(p_mask, k_mask, p_parts, k_parts, split, 2, "mask_share")
     ups, downs = [strip], [strip]
-    for step in range(1, cols_n // 2 + 1):
-        block = ups[-1] if step == 1 else relay(ups[-1])
-        ups.append(lax.ppermute(block, "col", [(i, (i + 1) % cols_n) for i in range(cols_n)]))
+    up = [(i, (i + 1) % cols_n) for i in range(cols_n)]
+    for step in range(1, cols_n // 2):
+        block = ups[-1] if step == 1 else jnp.concatenate(relay(ups[-1]))
+        ups.append(lax.ppermute(block, "col", up))
+    last = [lax.ppermute(half, "col", up) for half in relay(ups[-1])]
     for step in range(1, cols_n - cols_n // 2):
         downs.append(lax.ppermute(downs[-1], "col", [(i, (i - 1) % cols_n) for i in range(cols_n)]))
     near, damp = local_part(
@@ -364,10 +368,10 @@
         if split == 2:
             swap = [(i, i ^ 1) for i in range(depth)]
             shares += [lax.ppermute(part, "depth", swap) for part in got]
-    blocks = ups[1:-1] + downs[1:]
+    blocks = ups[1:] + downs[1:]
     left, early = early_product(near, strip, blocks, cols_n)
     middle = shares_product(left, early, shares, rows_n, split, here // width)
-    operands = [damp, near, middle, ups[-1]] + shares
+    operands = [damp, near, middle] + last + shares
     block, total = (2 * out_rows, 4 * width), (2 * out_rows, width)
     return pl.pallas_call(
         functools.partial(product_kernel, rows_n, cols_n, split),

time: 25.9 us -> 25.9 us (level)
  starting transfers between devices: 7.29 us -> 12 us
  waiting for transfers between devices: 8.27 us -> 3.56 us
    ppermute x2 -> x3, starting transfers between devices: 3.13 us -> 7.83 us  [the longest x2 4.75 us: body(): last = [lax.ppermute(half, 'col', up) for half in relay(ups[-1])]]
    ppermute x2, waiting for transfers between devices: 6.14 us -> 1.46 us  [body(): got = [lax.ppermute(part, 'row', perm) for part in share]]
    ppermute x2 -> x3, waiting for transfers between devices: 2.12 us -> 2.09 us  [the longest x2 1.86 us: body(): last = [lax.ppermute(half, 'col', up) for half in relay(ups[-1])]]
  transfers between devices with their start and end apart: 7 -> 8, of which waited for: 4 -> 4; matrix products, arithmetic and copies ran while one was open for 0% -> 0% of each run, Pallas kernels for 23% -> 23%
where the time goes in v7:
time: 25.9 us; the launch traced here: 25.7 us
  starting transfers between devices  12 us (46%)
  Pallas kernels  8.78 us (34%)
  waiting for transfers between devices  3.56 us (14%)
  local copies, waits for them, and re-layouts  1.23 us (5%)
    ppermute x2, starting transfers between devices, body(): last = [lax.ppermute(half, 'col', up) for half in relay(ups[-1])]  4.75 us
    pallas_call x2, Pallas kernels, mask_rows(): pl.pallas_call(functools.partial(rows_kernel, places), in_specs=[HBM] * 4...  3.53 us
    ppermute x1, starting transfers between devices, body(): ups.append(lax.ppermute(block, 'col', up))  3.08 us
    pallas_call x1, Pallas kernels, local_part(): pl.pallas_call(local_kernel, in_specs=[HBM] * 8, out_specs=[HBM, VMEM], o...  3.02 us
    ppermute x2, starting transfers between devices, body(): got = [lax.ppermute(part, 'row', perm) for part in share]  2.09 us
    ppermute x1, starting transfers between devices, body(): lax.ppermute(downs[-1], 'col', [(i, (i - 1) % cols_n) for i in range(cols...  2.05 us
    ppermute x2, waiting for transfers between devices, body(): last = [lax.ppermute(half, 'col', up) for half in relay(ups[-1])]  1.86 us
    ppermute x2, waiting for transfers between devices, body(): got = [lax.ppermute(part, 'row', perm) for part in share]  1.46 us
  transfers between devices with their start and end apart: 8, of which 4 were waited for; matrix products, arithmetic and copies ran while one was open for 0% of the time, Pallas kernels for 23%

profile of v7, /device:TPU:0, one launch (start us, length us, event | category | flops | bytes accessed | tf_op | source)
XLA Modules:
  0.0 25.7 jit_solution(11501548817812667523)
XLA Ops:
  0.0 1.7 %mask_strip.1.strip.own = bf16[4,128,256]{2,1,0:T(8,128)(2,1)} custom-call(s32[4,8]{1,0:T(4,128)} %bitcast.2, s32[4,8]{1,0:T(4,128)} %bitcast.5, bf16[2,512,256]{2,1,0:T(8,128)(2,1)} %second_ref.3, bf16[2,512,256]{2,1,0:T(8,128)(2,1)} %first_ref.3), custom_call_target="tpu_custom_call" | custom-call | tf_op jit(solution)/shard_map/mask_strip/pallas_call | solution.py:81
  1.7 0.0 copy-start.2
  1.7 3.1 %collective-permute-start = (bf16[4,128,256]{2,1,0:T(8,128)(2,1)}, bf16[4,128,256]{2,1,0:T(8,128)(2,1)S(1)}, u32[]{:S(2)}, u32[]{:S(2)}) collective-permute-start(bf16[4,128,256]{2,1,0:T(8,128)(2,1)} %mask_strip.1.strip.own), channel_id=1, source_target_pairs={{0,4},{4,8},{8,12},{12,0},{1,5},{5,9},{9,13},{13,1},{2,6},{6,10},{... | collective-permute-start | bytes 786440 | tf_op jit(solution)/shard_map/ppermute | solution.py:356
  4.8 1.8 %mask_share.1 = (bf16[2,256,256]{2,1,0:T(8,128)(2,1)}, bf16[2,256,256]{2,1,0:T(8,128)(2,1)}) custom-call(s32[4,8]{1,0:T(4,128)} %bitcast.6, s32[4,8]{1,0:T(4,128)} %bitcast.3, bf16[2,512,256]{2,1,0:T(8,128)(2,1)} %first_ref.3, bf16[2,512,256]{2,1,0:T(8,128)(2,1)} %second_ref.3), custom_call_target="tpu_custom_call" | custom-call | tf_op jit(solution)/shard_map/mask_share/pallas_call | solution.py:81
  6.6 1.6 %collective-permute-start.2 = (bf16[2,256,256]{2,1,0:T(8,128)(2,1)}, bf16[2,256,256]{2,1,0:T(8,128)(2,1)S(1)}, u32[]{:S(2)}, u32[]{:S(2)}) collective-permute-start(bf16[2,256,256]{2,1,0:T(8,128)(2,1)} %get-tuple-element.17), channel_id=1, source_target_pairs={{0,16},{16,0},{1,17},{17,1},{2,18},{18,2},{3,19},{19,3},{4,20},{20... | collective-permute-start | bytes 786440 | tf_op jit(solution)/shard_map/ppermute | solution.py:366
  8.2 0.5 %collective-permute-start.3 = (bf16[2,256,256]{2,1,0:T(8,128)(2,1)}, bf16[2,256,256]{2,1,0:T(8,128)(2,1)S(1)}, u32[]{:S(2)}, u32[]{:S(2)}) collective-permute-start(bf16[2,256,256]{2,1,0:T(8,128)(2,1)} %get-tuple-element.18), channel_id=1, source_target_pairs={{0,16},{16,0},{1,17},{17,1},{2,18},{18,2},{3,19},{19,3},{4,20},{20... | collective-permute-start | bytes 786440 | tf_op jit(solution)/shard_map/ppermute | solution.py:366
  8.7 2.1 %collective-permute-start.1 = (bf16[4,128,256]{2,1,0:T(8,128)(2,1)}, bf16[4,128,256]{2,1,0:T(8,128)(2,1)S(1)}, u32[]{:S(2)}, u32[]{:S(2)}) collective-permute-start(bf16[4,128,256]{2,1,0:T(8,128)(2,1)} %mask_strip.1.strip.own), channel_id=1, source_target_pairs={{0,12},{4,0},{8,4},{12,8},{1,13},{5,1},{9,5},{13,9},{2,14},{6,2},{... | collective-permute-start | bytes 786440 | tf_op jit(solution)/shard_map/ppermute | solution.py:359
  10.8 3.0 %local_part.1 = (bf16[8,256,256]{2,1,0:T(8,128)(2,1)}, f32[2,128,256]{2,1,0:T(8,128)}) custom-call(s32[4,8]{1,0:T(4,128)} %bitcast.4, s32[4,8]{1,0:T(4,128)} %bitcast.7, s32[16]{0:T(128)} %atoms_ref.1, s32[4,4]{1,0:T(4,128)} %classes_ref.1, f32[4]{0:T(128)} %rates_ref.1, bf16[2,512,256]{2,1,0:T(8,128)(2,1)} %second_ref.3, bf16[2,512,256]{2,1,0:T(8,128)(2,1)} %first_ref.3, ...), custom_call_target="tpu_custom_call" | custom-call | flops 1048576 | bytes 2621440 | tf_op jit(solution)/shard_map/local_part/pallas_call | solution.py:176
  13.8 0.2 collective-permute-done.refs_0_.block
  14.1 0.1 collective-permute-start.6
  14.1 4.7 %collective-permute-start.7 = (bf16[2,128,256]{2,1,0:T(8,128)(2,1)S(1)}, bf16[2,128,256]{2,1,0:T(8,128)(2,1)S(1)}, u32[]{:S(2)}, u32[]{:S(2)}) collective-permute-start(bf16[2,128,256]{2,1,0:T(8,128)(2,1)S(1)} %get-tuple-element.20), channel_id=1, source_target_pairs={{0,4},{4,8},{8,12},{12,0},{1,5},{5,9},{9,13},{13,1},{2,6},{6,10},{... | collective-permute-start | bytes 393224 | tf_op jit(solution)/shard_map/ppermute | solution.py:357
  18.8 0.0 collective-permute-done.2.refs_0_
  18.8 0.0 collective-permute-start.4
  18.8 1.5 %collective-permute-done.3.refs_1_ = bf16[2,256,256]{2,1,0:T(8,128)(2,1)S(1)} collective-permute-done((bf16[2,256,256]{2,1,0:T(8,128)(2,1)}, bf16[2,256,256]{2,1,0:T(8,128)(2,1)S(1)}, u32[]{:S(2)}, u32[]{:S(2)}) %collective-permute-start.3) | collective-permute-done | bytes 262176 | tf_op jit(solution)/shard_map/ppermute | solution.py:366
  20.3 0.0 collective-permute-start.5
  20.3 0.0 collective-permute-done.1.refs_1_
  20.3 0.0 copy-done.2
  20.3 0.0 copy-start
  20.3 1.2 %copy-done = bf16[8,256,256]{2,1,0:T(8,128)(2,1)S(1)} copy-done((bf16[8,256,256]{2,1,0:T(8,128)(2,1)S(1)}, bf16[8,256,256]{2,1,0:T(8,128)(2,1)}, u32[]{:S(2)}) %copy-start) | copy-done | bytes 1048600
  21.5 0.7 %early_product.1 = (bf16[256,4096]{1,0:T(8,128)(2,1)S(1)}, f32[256,256]{1,0:T(8,128)S(1)}) custom-call(bf16[8,256,256]{2,1,0:T(8,128)(2,1)S(1)} %copy-done, bf16[4,128,256]{2,1,0:T(8,128)(2,1)S(1)} %copy-done.2, bf16[4,128,256]{2,1,0:T(8,128)(2,1)S(1)} %collective-permute-done.refs_0_.block, bf16[4,128,256]{2,1,0:T(8,128)(2,1)S(1)} %collective-permute-done.1.refs_1_), custom_call_target="tpu_custom_call" | custom-call | flops 10737418240 | bytes 4194304 | tf_op jit(solution)/shard_map/early_product/pallas_call | solution.py:277
  22.2 0.0 copy-start.1
  22.2 0.0 copy-start.3
  22.2 0.0 collective-permute-done.4.refs_2_
  22.2 0.0 collective-permute-done.5.refs_3_
  22.3 0.5 %shares_product.1.middle = f32[256,256]{1,0:T(8,128)S(1)} custom-call(bf16[256,4096]{1,0:T(8,128)(2,1)S(1)} %get-tuple-element.15.left, f32[256,256]{1,0:T(8,128)S(1)} %get-tuple-element.16.early, bf16[2,256,256]{2,1,0:T(8,128)(2,1)S(1)} %collective-permute-done.2.refs_0_, bf16[2,256,256]{2,1,0:T(8,128)(2,1)S(1)} %collective-permute-done.3.refs_1_, ...), custom_call_target="tpu_custom_call" | custom-call | flops 1000000 | bytes 1000000 | tf_op jit(solution)/shard_map/shares_product/pallas_call | solution.py:309
  22.7 0.5 %collective-permute-done.6.last_k = bf16[2,128,256]{2,1,0:T(8,128)(2,1)S(1)} collective-permute-done((bf16[2,128,256]{2,1,0:T(8,128)(2,1)S(1)}, bf16[2,128,256]{2,1,0:T(8,128)(2,1)S(1)}, u32[]{:S(2)}, u32[]{:S(2)}) %collective-permute-start.6) | collective-permute-done | bytes 131104 | tf_op jit(solution)/shard_map/ppermute | solution.py:357
  23.2 1.4 %collective-permute-done.7.last_p = bf16[2,128,256]{2,1,0:T(8,128)(2,1)S(1)} collective-permute-done((bf16[2,128,256]{2,1,0:T(8,128)(2,1)S(1)}, bf16[2,128,256]{2,1,0:T(8,128)(2,1)S(1)}, u32[]{:S(2)}, u32[]{:S(2)}) %collective-permute-start.7) | collective-permute-done | bytes 131104 | tf_op jit(solution)/shard_map/ppermute | solution.py:357
  24.6 0.0 copy-done.1
  24.6 0.0 copy-done.3
  24.6 1.1 %commutator.1 = f32[2,128,256]{2,1,0:T(8,128)} custom-call(f32[2,128,256]{2,1,0:T(8,128)S(1)} %copy-done.3, bf16[8,256,256]{2,1,0:T(8,128)(2,1)S(1)} %copy-done.1, f32[256,256]{1,0:T(8,128)S(1)} %shares_product.1.middle, bf16[2,128,256]{2,1,0:T(8,128)(2,1)S(1)} %collective-permute-done.6.last_k, bf16[2,128,256]{2,1,0:T(8,128)(2,1)S(1)} %collective-permute-done.7.last_p, ...), custom_call_target="tpu_custom_call" | custom-call | tf_op jit(solution)/shard_map/commutator/pallas_call | solution.py:376
  (1 shorter events, 0.0 us)
Async XLA Ops:
  1.7 18.6 %copy-start.2 = (bf16[4,128,256]{2,1,0:T(8,128)(2,1)S(1)}, bf16[4,128,256]{2,1,0:T(8,128)(2,1)}, u32[]{:S(2)}) copy-start(bf16[4,128,256]{2,1,0:T(8,128)(2,1)} %mask_strip.1.strip.own) | copy-start | bytes 786436
  1.7 12.3 %collective-permute-start = (bf16[4,128,256]{2,1,0:T(8,128)(2,1)}, bf16[4,128,256]{2,1,0:T(8,128)(2,1)S(1)}, u32[]{:S(2)}, u32[]{:S(2)}) collective-permute-start(bf16[4,128,256]{2,1,0:T(8,128)(2,1)} %mask_strip.1.strip.own), channel_id=1, source_target_pairs={{0,4},{4,8},{8,12},{12,0},{1,5},{5,9},{9,13},{13,1},{2,6},{6,10},{... | collective-permute-start | bytes 786440 | tf_op jit(solution)/shard_map/ppermute | solution.py:356
  6.6 12.2 %collective-permute-start.2 = (bf16[2,256,256]{2,1,0:T(8,128)(2,1)}, bf16[2,256,256]{2,1,0:T(8,128)(2,1)S(1)}, u32[]{:S(2)}, u32[]{:S(2)}) collective-permute-start(bf16[2,256,256]{2,1,0:T(8,128)(2,1)} %get-tuple-element.17), channel_id=1, source_target_pairs={{0,16},{16,0},{1,17},{17,1},{2,18},{18,2},{3,19},{19,3},{4,20},{20... | collective-permute-start | bytes 786440 | tf_op jit(solution)/shard_map/ppermute | solution.py:366
  8.2 12.1 %collective-permute-start.3 = (bf16[2,256,256]{2,1,0:T(8,128)(2,1)}, bf16[2,256,256]{2,1,0:T(8,128)(2,1)S(1)}, u32[]{:S(2)}, u32[]{:S(2)}) collective-permute-start(bf16[2,256,256]{2,1,0:T(8,128)(2,1)} %get-tuple-element.18), channel_id=1, source_target_pairs={{0,16},{16,0},{1,17},{17,1},{2,18},{18,2},{3,19},{19,3},{4,20},{20... | collective-permute-start | bytes 786440 | tf_op jit(solution)/shard_map/ppermute | solution.py:366
  8.7 11.6 %collective-permute-start.1 = (bf16[4,128,256]{2,1,0:T(8,128)(2,1)}, bf16[4,128,256]{2,1,0:T(8,128)(2,1)S(1)}, u32[]{:S(2)}, u32[]{:S(2)}) collective-permute-start(bf16[4,128,256]{2,1,0:T(8,128)(2,1)} %mask_strip.1.strip.own), channel_id=1, source_target_pairs={{0,12},{4,0},{8,4},{12,8},{1,13},{5,1},{9,5},{13,9},{2,14},{6,2},{... | collective-permute-start | bytes 786440 | tf_op jit(solution)/shard_map/ppermute | solution.py:359
  14.1 9.1 %collective-permute-start.6 = (bf16[2,128,256]{2,1,0:T(8,128)(2,1)S(1)}, bf16[2,128,256]{2,1,0:T(8,128)(2,1)S(1)}, u32[]{:S(2)}, u32[]{:S(2)}) collective-permute-start(bf16[2,128,256]{2,1,0:T(8,128)(2,1)S(1)} %get-tuple-element.19), channel_id=1, source_target_pairs={{0,4},{4,8},{8,12},{12,0},{1,5},{5,9},{9,13},{13,1},{2,6},{6,10},{... | collective-permute-start | bytes 393224 | tf_op jit(solution)/shard_map/ppermute | solution.py:357
  14.1 10.4 %collective-permute-start.7 = (bf16[2,128,256]{2,1,0:T(8,128)(2,1)S(1)}, bf16[2,128,256]{2,1,0:T(8,128)(2,1)S(1)}, u32[]{:S(2)}, u32[]{:S(2)}) collective-permute-start(bf16[2,128,256]{2,1,0:T(8,128)(2,1)S(1)} %get-tuple-element.20), channel_id=1, source_target_pairs={{0,4},{4,8},{8,12},{12,0},{1,5},{5,9},{9,13},{13,1},{2,6},{6,10},{... | collective-permute-start | bytes 393224 | tf_op jit(solution)/shard_map/ppermute | solution.py:357
  18.8 3.4 %collective-permute-start.4 = (bf16[2,256,256]{2,1,0:T(8,128)(2,1)S(1)}, bf16[2,256,256]{2,1,0:T(8,128)(2,1)S(1)}, u32[]{:S(2)}, u32[]{:S(2)}) collective-permute-start(bf16[2,256,256]{2,1,0:T(8,128)(2,1)S(1)} %collective-permute-done.2.refs_0_), channel_id=1, source_target_pairs={{0,1},{1,0},{2,3},{3,2},{4,5},{5,4},{6,7},{7,6},{8,9},{9,8},{10,11... | collective-permute-start | bytes 786440 | tf_op jit(solution)/shard_map/ppermute | solution.py:370
  20.3 1.9 %collective-permute-start.5 = (bf16[2,256,256]{2,1,0:T(8,128)(2,1)S(1)}, bf16[2,256,256]{2,1,0:T(8,128)(2,1)S(1)}, u32[]{:S(2)}, u32[]{:S(2)}) collective-permute-start(bf16[2,256,256]{2,1,0:T(8,128)(2,1)S(1)} %collective-permute-done.3.refs_1_), channel_id=1, source_target_pairs={{0,1},{1,0},{2,3},{3,2},{4,5},{5,4},{6,7},{7,6},{8,9},{9,8},{10,11... | collective-permute-start | bytes 786440 | tf_op jit(solution)/shard_map/ppermute | solution.py:370
  20.3 1.2 %copy-start = (bf16[8,256,256]{2,1,0:T(8,128)(2,1)S(1)}, bf16[8,256,256]{2,1,0:T(8,128)(2,1)}, u32[]{:S(2)}) copy-start(bf16[8,256,256]{2,1,0:T(8,128)(2,1)} %get-tuple-element.14.near) | copy-start | bytes 3145732
  22.2 2.4 %copy-start.1 = (bf16[8,256,256]{2,1,0:T(8,128)(2,1)S(1)}, bf16[8,256,256]{2,1,0:T(8,128)(2,1)}, u32[]{:S(2)}) copy-start(bf16[8,256,256]{2,1,0:T(8,128)(2,1)} %get-tuple-element.14.near) | copy-start | bytes 3145732
  22.2 2.4 %copy-start.3 = (f32[2,128,256]{2,1,0:T(8,128)S(1)}, f32[2,128,256]{2,1,0:T(8,128)}, u32[]{:S(2)}) copy-start(f32[2,128,256]{2,1,0:T(8,128)} %get-tuple-element.13.damp) | copy-start | bytes 786436

commit v8 on v7

--- a/solution.py
+++ b/solution.py
@@ -223,7 +223,7 @@
         out_shape=[jax.ShapeDtypeStruct((2,) + block.shape[1:], block.dtype)] * 2,
         compiler_params=params((block.shape, 4)),
         cost_estimate=pl.CostEstimate(
-            flops=100000000, bytes_accessed=4 * block.size, transcendentals=0
+            flops=10000000000, bytes_accessed=4 * block.size, transcendentals=0
         ),
         name="relay",
     )(block)

time: 25.9 us -> 25.9 us (level)
  local copies, waits for them, and re-layouts: 1.23 us -> 0.01 us
  waiting for transfers between devices: 3.56 us -> 4.51 us
    ppermute x2, waiting for transfers between devices: 1.46 us -> 3.18 us  [body(): got = [lax.ppermute(part, 'row', perm) for part in share]]
    ppermute x2, waiting for transfers between devices: 1.86 us -> 0.2 us  [body(): last = [lax.ppermute(half, 'col', up) for half in relay(ups[-1])]]
    unnamed x8 -> x6, local copies, waits for them, and re-layouts: 1.23 us -> 0.01 us
    ppermute x2, waiting for transfers between devices: 0.01 us -> 0.82 us  [body(): shares += [lax.ppermute(part, 'depth', swap) for part in got]]
where the time goes in v8:
time: 25.9 us; the launch traced here: 25.7 us
  starting transfers between devices  12.2 us (47%)
  Pallas kernels  8.8 us (34%)
  waiting for transfers between devices  4.51 us (17%)
    ppermute x2, starting transfers between devices, body(): last = [lax.ppermute(half, 'col', up) for half in relay(ups[-1])]  4.98 us
    pallas_call x2, Pallas kernels, mask_rows(): pl.pallas_call(functools.partial(rows_kernel, places), in_specs=[HBM] * 4...  3.54 us
    ppermute x2, waiting for transfers between devices, body(): got = [lax.ppermute(part, 'row', perm) for part in share]  3.18 us
    ppermute x1, starting transfers between devices, body(): ups.append(lax.ppermute(block, 'col', up))  3.08 us
    pallas_call x1, Pallas kernels, local_part(): pl.pallas_call(local_kernel, in_specs=[HBM] * 8, out_specs=[HBM, VMEM], o...  3.03 us
    ppermute x2, starting transfers between devices, body(): got = [lax.ppermute(part, 'row', perm) for part in share]  2.09 us
    ppermute x1, starting transfers between devices, body(): lax.ppermute(downs[-1], 'col', [(i, (i - 1) % cols_n) for i in range(cols...  2.09 us
    pallas_call x1, Pallas kernels, body(): pl.pallas_call(functools.partial(product_kernel, rows_n, cols_n, split),...  1.08 us
  transfers between devices with their start and end apart: 8, of which 4 were waited for; matrix products, arithmetic and copies ran while one was open for 0% of the time, Pallas kernels for 23%

profile of v8, /device:TPU:0, one launch (start us, length us, event | category | flops | bytes accessed | tf_op | source)
XLA Modules:
  0.0 25.7 jit_solution(17157400501937491330)
XLA Ops:
  0.0 1.7 %mask_strip.1.strip.own = bf16[4,128,256]{2,1,0:T(8,128)(2,1)} custom-call(s32[4,8]{1,0:T(4,128)} %bitcast.2, s32[4,8]{1,0:T(4,128)} %bitcast.5, bf16[2,512,256]{2,1,0:T(8,128)(2,1)} %second_ref.3, bf16[2,512,256]{2,1,0:T(8,128)(2,1)} %first_ref.3), custom_call_target="tpu_custom_call" | custom-call | tf_op jit(solution)/shard_map/mask_strip/pallas_call | solution.py:81
  1.7 3.1 %collective-permute-start = (bf16[4,128,256]{2,1,0:T(8,128)(2,1)}, bf16[4,128,256]{2,1,0:T(8,128)(2,1)S(1)}, u32[]{:S(2)}, u32[]{:S(2)}) collective-permute-start(bf16[4,128,256]{2,1,0:T(8,128)(2,1)} %mask_strip.1.strip.own), channel_id=1, source_target_pairs={{0,4},{4,8},{8,12},{12,0},{1,5},{5,9},{9,13},{13,1},{2,6},{6,10},{... | collective-permute-start | bytes 786440 | tf_op jit(solution)/shard_map/ppermute | solution.py:356
  4.8 2.1 %collective-permute-start.1 = (bf16[4,128,256]{2,1,0:T(8,128)(2,1)}, bf16[4,128,256]{2,1,0:T(8,128)(2,1)S(1)}, u32[]{:S(2)}, u32[]{:S(2)}) collective-permute-start(bf16[4,128,256]{2,1,0:T(8,128)(2,1)} %mask_strip.1.strip.own), channel_id=1, source_target_pairs={{0,12},{4,0},{8,4},{12,8},{1,13},{5,1},{9,5},{13,9},{2,14},{6,2},{... | collective-permute-start | bytes 786440 | tf_op jit(solution)/shard_map/ppermute | solution.py:359
  6.9 1.9 %mask_share.1 = (bf16[2,256,256]{2,1,0:T(8,128)(2,1)}, bf16[2,256,256]{2,1,0:T(8,128)(2,1)}) custom-call(s32[4,8]{1,0:T(4,128)} %bitcast.6, s32[4,8]{1,0:T(4,128)} %bitcast.3, bf16[2,512,256]{2,1,0:T(8,128)(2,1)} %first_ref.3, bf16[2,512,256]{2,1,0:T(8,128)(2,1)} %second_ref.3), custom_call_target="tpu_custom_call" | custom-call | tf_op jit(solution)/shard_map/mask_share/pallas_call | solution.py:81
  8.7 1.7 %collective-permute-start.2 = (bf16[2,256,256]{2,1,0:T(8,128)(2,1)}, bf16[2,256,256]{2,1,0:T(8,128)(2,1)S(1)}, u32[]{:S(2)}, u32[]{:S(2)}) collective-permute-start(bf16[2,256,256]{2,1,0:T(8,128)(2,1)} %get-tuple-element.17), channel_id=1, source_target_pairs={{0,16},{16,0},{1,17},{17,1},{2,18},{18,2},{3,19},{19,3},{4,20},{20... | collective-permute-start | bytes 786440 | tf_op jit(solution)/shard_map/ppermute | solution.py:366
  10.4 0.4 %collective-permute-start.3 = (bf16[2,256,256]{2,1,0:T(8,128)(2,1)}, bf16[2,256,256]{2,1,0:T(8,128)(2,1)S(1)}, u32[]{:S(2)}, u32[]{:S(2)}) collective-permute-start(bf16[2,256,256]{2,1,0:T(8,128)(2,1)} %get-tuple-element.18), channel_id=1, source_target_pairs={{0,16},{16,0},{1,17},{17,1},{2,18},{18,2},{3,19},{19,3},{4,20},{20... | collective-permute-start | bytes 786440 | tf_op jit(solution)/shard_map/ppermute | solution.py:366
  10.8 3.0 %local_part.1 = (bf16[8,256,256]{2,1,0:T(8,128)(2,1)}, f32[2,128,256]{2,1,0:T(8,128)}) custom-call(s32[4,8]{1,0:T(4,128)} %bitcast.4, s32[4,8]{1,0:T(4,128)} %bitcast.7, s32[16]{0:T(128)} %atoms_ref.1, s32[4,4]{1,0:T(4,128)} %classes_ref.1, f32[4]{0:T(128)} %rates_ref.1, bf16[2,512,256]{2,1,0:T(8,128)(2,1)} %second_ref.3, bf16[2,512,256]{2,1,0:T(8,128)(2,1)} %first_ref.3, ...), custom_call_target="tpu_custom_call" | custom-call | flops 1048576 | bytes 2621440 | tf_op jit(solution)/shard_map/local_part/pallas_call | solution.py:176
  13.9 0.0 copy-start
  13.9 0.0 copy-start.1
  13.9 0.3 %collective-permute-done.refs_0_.block = bf16[4,128,256]{2,1,0:T(8,128)(2,1)S(1)} collective-permute-done((bf16[4,128,256]{2,1,0:T(8,128)(2,1)}, bf16[4,128,256]{2,1,0:T(8,128)(2,1)S(1)}, u32[]{:S(2)}, u32[]{:S(2)}) %collective-permute-start) | collective-permute-done | bytes 262176 | tf_op jit(solution)/shard_map/ppermute | solution.py:356
  14.2 0.1 collective-permute-start.6
  14.3 4.9 %collective-permute-start.7 = (bf16[2,128,256]{2,1,0:T(8,128)(2,1)S(1)}, bf16[2,128,256]{2,1,0:T(8,128)(2,1)S(1)}, u32[]{:S(2)}, u32[]{:S(2)}) collective-permute-start(bf16[2,128,256]{2,1,0:T(8,128)(2,1)S(1)} %get-tuple-element.20), channel_id=1, source_target_pairs={{0,4},{4,8},{8,12},{12,0},{1,5},{5,9},{9,13},{13,1},{2,6},{6,10},{... | collective-permute-start | bytes 393224 | tf_op jit(solution)/shard_map/ppermute | solution.py:357
  19.2 0.0 collective-permute-done.2.refs_0_
  19.2 0.0 collective-permute-start.4
  19.2 3.2 %collective-permute-done.3.refs_1_ = bf16[2,256,256]{2,1,0:T(8,128)(2,1)S(1)} collective-permute-done((bf16[2,256,256]{2,1,0:T(8,128)(2,1)}, bf16[2,256,256]{2,1,0:T(8,128)(2,1)S(1)}, u32[]{:S(2)}, u32[]{:S(2)}) %collective-permute-start.3) | collective-permute-done | bytes 262176 | tf_op jit(solution)/shard_map/ppermute | solution.py:366
  22.4 0.0 collective-permute-start.5
  22.4 0.0 collective-permute-done.1.refs_1_
  22.4 0.0 copy-done
  22.4 0.0 copy-done.1
  22.4 0.7 %early_product.1 = (bf16[256,4096]{1,0:T(8,128)(2,1)S(1)}, f32[256,256]{1,0:T(8,128)S(1)}) custom-call(bf16[8,256,256]{2,1,0:T(8,128)(2,1)S(1)} %copy-done, bf16[4,128,256]{2,1,0:T(8,128)(2,1)S(1)} %copy-done.1, bf16[4,128,256]{2,1,0:T(8,128)(2,1)S(1)} %collective-permute-done.refs_0_.block, bf16[4,128,256]{2,1,0:T(8,128)(2,1)S(1)} %collective-permute-done.1.refs_1_), custom_call_target="tpu_custom_call" | custom-call | flops 10737418240 | bytes 4194304 | tf_op jit(solution)/shard_map/early_product/pallas_call | solution.py:277
  23.1 0.0 copy-start.2
  23.1 0.0 collective-permute-done.4.refs_2_
  23.1 0.8 %collective-permute-done.5.refs_3_ = bf16[2,256,256]{2,1,0:T(8,128)(2,1)S(1)} collective-permute-done((bf16[2,256,256]{2,1,0:T(8,128)(2,1)S(1)}, bf16[2,256,256]{2,1,0:T(8,128)(2,1)S(1)}, u32[]{:S(2)}, u32[]{:S(2)}) %collective-permute-start.5) | collective-permute-done | bytes 262176 | tf_op jit(solution)/shard_map/ppermute | solution.py:370
  23.9 0.5 %shares_product.1.middle = f32[256,256]{1,0:T(8,128)S(1)} custom-call(bf16[256,4096]{1,0:T(8,128)(2,1)S(1)} %get-tuple-element.15.left, f32[256,256]{1,0:T(8,128)S(1)} %get-tuple-element.16.early, bf16[2,256,256]{2,1,0:T(8,128)(2,1)S(1)} %collective-permute-done.2.refs_0_, bf16[2,256,256]{2,1,0:T(8,128)(2,1)S(1)} %collective-permute-done.3.refs_1_, ...), custom_call_target="tpu_custom_call" | custom-call | flops 1000000 | bytes 1000000 | tf_op jit(solution)/shard_map/shares_product/pallas_call | solution.py:309
  24.4 0.0 collective-permute-done.6.last_k
  24.4 0.2 collective-permute-done.7.last_p
  24.6 0.0 copy-done.2
  24.6 1.1 %commutator.1 = f32[2,128,256]{2,1,0:T(8,128)} custom-call(f32[2,128,256]{2,1,0:T(8,128)S(1)} %copy-done.2, bf16[8,256,256]{2,1,0:T(8,128)(2,1)S(1)} %copy-done, f32[256,256]{1,0:T(8,128)S(1)} %shares_product.1.middle, bf16[2,128,256]{2,1,0:T(8,128)(2,1)S(1)} %collective-permute-done.6.last_k, bf16[2,128,256]{2,1,0:T(8,128)(2,1)S(1)} %collective-permute-done.7.last_p, ...), custom_call_target="tpu_custom_call" | custom-call | tf_op jit(solution)/shard_map/commutator/pallas_call | solution.py:376
  (1 shorter events, 0.0 us)
Async XLA Ops:
  1.7 12.5 %collective-permute-start = (bf16[4,128,256]{2,1,0:T(8,128)(2,1)}, bf16[4,128,256]{2,1,0:T(8,128)(2,1)S(1)}, u32[]{:S(2)}, u32[]{:S(2)}) collective-permute-start(bf16[4,128,256]{2,1,0:T(8,128)(2,1)} %mask_strip.1.strip.own), channel_id=1, source_target_pairs={{0,4},{4,8},{8,12},{12,0},{1,5},{5,9},{9,13},{13,1},{2,6},{6,10},{... | collective-permute-start | bytes 786440 | tf_op jit(solution)/shard_map/ppermute | solution.py:356
  4.8 17.6 %collective-permute-start.1 = (bf16[4,128,256]{2,1,0:T(8,128)(2,1)}, bf16[4,128,256]{2,1,0:T(8,128)(2,1)S(1)}, u32[]{:S(2)}, u32[]{:S(2)}) collective-permute-start(bf16[4,128,256]{2,1,0:T(8,128)(2,1)} %mask_strip.1.strip.own), channel_id=1, source_target_pairs={{0,12},{4,0},{8,4},{12,8},{1,13},{5,1},{9,5},{13,9},{2,14},{6,2},{... | collective-permute-start | bytes 786440 | tf_op jit(solution)/shard_map/ppermute | solution.py:359
  8.7 10.5 %collective-permute-start.2 = (bf16[2,256,256]{2,1,0:T(8,128)(2,1)}, bf16[2,256,256]{2,1,0:T(8,128)(2,1)S(1)}, u32[]{:S(2)}, u32[]{:S(2)}) collective-permute-start(bf16[2,256,256]{2,1,0:T(8,128)(2,1)} %get-tuple-element.17), channel_id=1, source_target_pairs={{0,16},{16,0},{1,17},{17,1},{2,18},{18,2},{3,19},{19,3},{4,20},{20... | collective-permute-start | bytes 786440 | tf_op jit(solution)/shard_map/ppermute | solution.py:366
  10.4 11.9 %collective-permute-start.3 = (bf16[2,256,256]{2,1,0:T(8,128)(2,1)}, bf16[2,256,256]{2,1,0:T(8,128)(2,1)S(1)}, u32[]{:S(2)}, u32[]{:S(2)}) collective-permute-start(bf16[2,256,256]{2,1,0:T(8,128)(2,1)} %get-tuple-element.18), channel_id=1, source_target_pairs={{0,16},{16,0},{1,17},{17,1},{2,18},{18,2},{3,19},{19,3},{4,20},{20... | collective-permute-start | bytes 786440 | tf_op jit(solution)/shard_map/ppermute | solution.py:366
  13.9 8.5 %copy-start = (bf16[8,256,256]{2,1,0:T(8,128)(2,1)S(1)}, bf16[8,256,256]{2,1,0:T(8,128)(2,1)}, u32[]{:S(2)}) copy-start(bf16[8,256,256]{2,1,0:T(8,128)(2,1)} %get-tuple-element.14.near) | copy-start | bytes 3145732
  13.9 8.5 %copy-start.1 = (bf16[4,128,256]{2,1,0:T(8,128)(2,1)S(1)}, bf16[4,128,256]{2,1,0:T(8,128)(2,1)}, u32[]{:S(2)}) copy-start(bf16[4,128,256]{2,1,0:T(8,128)(2,1)} %mask_strip.1.strip.own) | copy-start | bytes 786436
  14.2 10.2 %collective-permute-start.6 = (bf16[2,128,256]{2,1,0:T(8,128)(2,1)S(1)}, bf16[2,128,256]{2,1,0:T(8,128)(2,1)S(1)}, u32[]{:S(2)}, u32[]{:S(2)}) collective-permute-start(bf16[2,128,256]{2,1,0:T(8,128)(2,1)S(1)} %get-tuple-element.19), channel_id=1, source_target_pairs={{0,4},{4,8},{8,12},{12,0},{1,5},{5,9},{9,13},{13,1},{2,6},{6,10},{... | collective-permute-start | bytes 393224 | tf_op jit(solution)/shard_map/ppermute | solution.py:357
  14.3 10.3 %collective-permute-start.7 = (bf16[2,128,256]{2,1,0:T(8,128)(2,1)S(1)}, bf16[2,128,256]{2,1,0:T(8,128)(2,1)S(1)}, u32[]{:S(2)}, u32[]{:S(2)}) collective-permute-start(bf16[2,128,256]{2,1,0:T(8,128)(2,1)S(1)} %get-tuple-element.20), channel_id=1, source_target_pairs={{0,4},{4,8},{8,12},{12,0},{1,5},{5,9},{9,13},{13,1},{2,6},{6,10},{... | collective-permute-start | bytes 393224 | tf_op jit(solution)/shard_map/ppermute | solution.py:357
  19.2 3.9 %collective-permute-start.4 = (bf16[2,256,256]{2,1,0:T(8,128)(2,1)S(1)}, bf16[2,256,256]{2,1,0:T(8,128)(2,1)S(1)}, u32[]{:S(2)}, u32[]{:S(2)}) collective-permute-start(bf16[2,256,256]{2,1,0:T(8,128)(2,1)S(1)} %collective-permute-done.2.refs_0_), channel_id=1, source_target_pairs={{0,1},{1,0},{2,3},{3,2},{4,5},{5,4},{6,7},{7,6},{8,9},{9,8},{10,11... | collective-permute-start | bytes 786440 | tf_op jit(solution)/shard_map/ppermute | solution.py:370
  22.4 1.5 %collective-permute-start.5 = (bf16[2,256,256]{2,1,0:T(8,128)(2,1)S(1)}, bf16[2,256,256]{2,1,0:T(8,128)(2,1)S(1)}, u32[]{:S(2)}, u32[]{:S(2)}) collective-permute-start(bf16[2,256,256]{2,1,0:T(8,128)(2,1)S(1)} %collective-permute-done.3.refs_1_), channel_id=1, source_target_pairs={{0,1},{1,0},{2,3},{3,2},{4,5},{5,4},{6,7},{7,6},{8,9},{9,8},{10,11... | collective-permute-start | bytes 786440 | tf_op jit(solution)/shard_map/ppermute | solution.py:370
  23.1 1.5 %copy-start.2 = (f32[2,128,256]{2,1,0:T(8,128)S(1)}, f32[2,128,256]{2,1,0:T(8,128)}, u32[]{:S(2)}) copy-start(f32[2,128,256]{2,1,0:T(8,128)} %get-tuple-element.13.damp) | copy-start | bytes 786436

commit v9 on v7

--- a/solution.py
+++ b/solution.py
@@ -44,13 +44,13 @@
     unit = masked.shape[1]
     first = lax.rem(lax.axis_index("depth"), places) * rows
     span = pl.ds(pl.multiple_of(first, rows), rows)
-    mask_copies = fetch_masks((first_mask, second_mask), masks, mask_sems)
     copies = [
         pltpu.make_async_copy(ref.at[:, span, :], held.at[pl.ds(2 * i, 2)], sems.at[i])
         for i, ref in enumerate((first_ref, second_ref))
     ]
     for copy in copies:
         copy.start()
+    mask_copies = fetch_masks((first_mask, second_mask), masks, mask_sems)
     for copy in mask_copies:
         copy.wait()
     out_copies = []

time: 25.9 us -> 25.9 us (level)
  no operation moved by 1% of the time
where the time goes in v9:
time: 25.9 us; the launch traced here: 25.7 us
  starting transfers between devices  12 us (46%)
  Pallas kernels  8.78 us (34%)
  waiting for transfers between devices  3.56 us (14%)
  local copies, waits for them, and re-layouts  1.23 us (5%)
    ppermute x2, starting transfers between devices, body(): last = [lax.ppermute(half, 'col', up) for half in relay(ups[-1])]  4.75 us
    pallas_call x2, Pallas kernels, mask_rows(): pl.pallas_call(functools.partial(rows_kernel, places), in_specs=[HBM] * 4...  3.53 us
    ppermute x1, starting transfers between devices, body(): ups.append(lax.ppermute(block, 'col', up))  3.08 us
    pallas_call x1, Pallas kernels, local_part(): pl.pallas_call(local_kernel, in_specs=[HBM] * 8, out_specs=[HBM, VMEM], o...  3.02 us
    ppermute x2, starting transfers between devices, body(): got = [lax.ppermute(part, 'row', perm) for part in share]  2.09 us
    ppermute x1, starting transfers between devices, body(): lax.ppermute(downs[-1], 'col', [(i, (i - 1) % cols_n) for i in range(cols...  2.05 us
    ppermute x2, waiting for transfers between devices, body(): last = [lax.ppermute(half, 'col', up) for half in relay(ups[-1])]  1.86 us
    ppermute x2, waiting for transfers between devices, body(): got = [lax.ppermute(part, 'row', perm) for part in share]  1.46 us
  transfers between devices with their start and end apart: 8, of which 4 were waited for; matrix products, arithmetic and copies ran while one was open for 0% of the time, Pallas kernels for 23%

profile of v9, /device:TPU:0, one launch (start us, length us, event | category | flops | bytes accessed | tf_op | source)
XLA Modules:
  0.0 25.7 jit_solution(12936463139967552015)
XLA Ops:
  0.0 1.7 %mask_strip.1.strip.own = bf16[4,128,256]{2,1,0:T(8,128)(2,1)} custom-call(s32[4,8]{1,0:T(4,128)} %bitcast.2, s32[4,8]{1,0:T(4,128)} %bitcast.5, bf16[2,512,256]{2,1,0:T(8,128)(2,1)} %second_ref.3, bf16[2,512,256]{2,1,0:T(8,128)(2,1)} %first_ref.3), custom_call_target="tpu_custom_call" | custom-call | tf_op jit(solution)/shard_map/mask_strip/pallas_call | solution.py:81
  1.7 0.0 copy-start.2
  1.7 3.1 %collective-permute-start = (bf16[4,128,256]{2,1,0:T(8,128)(2,1)}, bf16[4,128,256]{2,1,0:T(8,128)(2,1)S(1)}, u32[]{:S(2)}, u32[]{:S(2)}) collective-permute-start(bf16[4,128,256]{2,1,0:T(8,128)(2,1)} %mask_strip.1.strip.own), channel_id=1, source_target_pairs={{0,4},{4,8},{8,12},{12,0},{1,5},{5,9},{9,13},{13,1},{2,6},{6,10},{... | collective-permute-start | bytes 786440 | tf_op jit(solution)/shard_map/ppermute | solution.py:356
  4.8 1.8 %mask_share.1 = (bf16[2,256,256]{2,1,0:T(8,128)(2,1)}, bf16[2,256,256]{2,1,0:T(8,128)(2,1)}) custom-call(s32[4,8]{1,0:T(4,128)} %bitcast.6, s32[4,8]{1,0:T(4,128)} %bitcast.3, bf16[2,512,256]{2,1,0:T(8,128)(2,1)} %first_ref.3, bf16[2,512,256]{2,1,0:T(8,128)(2,1)} %second_ref.3), custom_call_target="tpu_custom_call" | custom-call | tf_op jit(solution)/shard_map/mask_share/pallas_call | solution.py:81
  6.6 1.6 %collective-permute-start.2 = (bf16[2,256,256]{2,1,0:T(8,128)(2,1)}, bf16[2,256,256]{2,1,0:T(8,128)(2,1)S(1)}, u32[]{:S(2)}, u32[]{:S(2)}) collective-permute-start(bf16[2,256,256]{2,1,0:T(8,128)(2,1)} %get-tuple-element.17), channel_id=1, source_target_pairs={{0,16},{16,0},{1,17},{17,1},{2,18},{18,2},{3,19},{19,3},{4,20},{20... | collective-permute-start | bytes 786440 | tf_op jit(solution)/shard_map/ppermute | solution.py:366
  8.2 0.5 %collective-permute-start.3 = (bf16[2,256,256]{2,1,0:T(8,128)(2,1)}, bf16[2,256,256]{2,1,0:T(8,128)(2,1)S(1)}, u32[]{:S(2)}, u32[]{:S(2)}) collective-permute-start(bf16[2,256,256]{2,1,0:T(8,128)(2,1)} %get-tuple-element.18), channel_id=1, source_target_pairs={{0,16},{16,0},{1,17},{17,1},{2,18},{18,2},{3,19},{19,3},{4,20},{20... | collective-permute-start | bytes 786440 | tf_op jit(solution)/shard_map/ppermute | solution.py:366
  8.7 2.1 %collective-permute-start.1 = (bf16[4,128,256]{2,1,0:T(8,128)(2,1)}, bf16[4,128,256]{2,1,0:T(8,128)(2,1)S(1)}, u32[]{:S(2)}, u32[]{:S(2)}) collective-permute-start(bf16[4,128,256]{2,1,0:T(8,128)(2,1)} %mask_strip.1.strip.own), channel_id=1, source_target_pairs={{0,12},{4,0},{8,4},{12,8},{1,13},{5,1},{9,5},{13,9},{2,14},{6,2},{... | collective-permute-start | bytes 786440 | tf_op jit(solution)/shard_map/ppermute | solution.py:359
  10.8 3.0 %local_part.1 = (bf16[8,256,256]{2,1,0:T(8,128)(2,1)}, f32[2,128,256]{2,1,0:T(8,128)}) custom-call(s32[4,8]{1,0:T(4,128)} %bitcast.4, s32[4,8]{1,0:T(4,128)} %bitcast.7, s32[16]{0:T(128)} %atoms_ref.1, s32[4,4]{1,0:T(4,128)} %classes_ref.1, f32[4]{0:T(128)} %rates_ref.1, bf16[2,512,256]{2,1,0:T(8,128)(2,1)} %second_ref.3, bf16[2,512,256]{2,1,0:T(8,128)(2,1)} %first_ref.3, ...), custom_call_target="tpu_custom_call" | custom-call | flops 1048576 | bytes 2621440 | tf_op jit(solution)/shard_map/local_part/pallas_call | solution.py:176
  13.8 0.2 collective-permute-done.refs_0_.block
  14.1 0.1 collective-permute-start.6
  14.1 4.7 %collective-permute-start.7 = (bf16[2,128,256]{2,1,0:T(8,128)(2,1)S(1)}, bf16[2,128,256]{2,1,0:T(8,128)(2,1)S(1)}, u32[]{:S(2)}, u32[]{:S(2)}) collective-permute-start(bf16[2,128,256]{2,1,0:T(8,128)(2,1)S(1)} %get-tuple-element.20), channel_id=1, source_target_pairs={{0,4},{4,8},{8,12},{12,0},{1,5},{5,9},{9,13},{13,1},{2,6},{6,10},{... | collective-permute-start | bytes 393224 | tf_op jit(solution)/shard_map/ppermute | solution.py:357
  18.8 0.0 collective-permute-done.2.refs_0_
  18.8 0.0 collective-permute-start.4
  18.8 1.5 %collective-permute-done.3.refs_1_ = bf16[2,256,256]{2,1,0:T(8,128)(2,1)S(1)} collective-permute-done((bf16[2,256,256]{2,1,0:T(8,128)(2,1)}, bf16[2,256,256]{2,1,0:T(8,128)(2,1)S(1)}, u32[]{:S(2)}, u32[]{:S(2)}) %collective-permute-start.3) | collective-permute-done | bytes 262176 | tf_op jit(solution)/shard_map/ppermute | solution.py:366
  20.3 0.0 collective-permute-start.5
  20.3 0.0 collective-permute-done.1.refs_1_
  20.3 0.0 copy-done.2
  20.3 0.0 copy-start
  20.3 1.2 %copy-done = bf16[8,256,256]{2,1,0:T(8,128)(2,1)S(1)} copy-done((bf16[8,256,256]{2,1,0:T(8,128)(2,1)S(1)}, bf16[8,256,256]{2,1,0:T(8,128)(2,1)}, u32[]{:S(2)}) %copy-start) | copy-done | bytes 1048600
  21.5 0.7 %early_product.1 = (bf16[256,4096]{1,0:T(8,128)(2,1)S(1)}, f32[256,256]{1,0:T(8,128)S(1)}) custom-call(bf16[8,256,256]{2,1,0:T(8,128)(2,1)S(1)} %copy-done, bf16[4,128,256]{2,1,0:T(8,128)(2,1)S(1)} %copy-done.2, bf16[4,128,256]{2,1,0:T(8,128)(2,1)S(1)} %collective-permute-done.refs_0_.block, bf16[4,128,256]{2,1,0:T(8,128)(2,1)S(1)} %collective-permute-done.1.refs_1_), custom_call_target="tpu_custom_call" | custom-call | flops 10737418240 | bytes 4194304 | tf_op jit(solution)/shard_map/early_product/pallas_call | solution.py:277
  22.2 0.0 copy-start.1
  22.2 0.0 copy-start.3
  22.2 0.0 collective-permute-done.4.refs_2_
  22.2 0.0 collective-permute-done.5.refs_3_
  22.3 0.5 %shares_product.1.middle = f32[256,256]{1,0:T(8,128)S(1)} custom-call(bf16[256,4096]{1,0:T(8,128)(2,1)S(1)} %get-tuple-element.15.left, f32[256,256]{1,0:T(8,128)S(1)} %get-tuple-element.16.early, bf16[2,256,256]{2,1,0:T(8,128)(2,1)S(1)} %collective-permute-done.2.refs_0_, bf16[2,256,256]{2,1,0:T(8,128)(2,1)S(1)} %collective-permute-done.3.refs_1_, ...), custom_call_target="tpu_custom_call" | custom-call | flops 1000000 | bytes 1000000 | tf_op jit(solution)/shard_map/shares_product/pallas_call | solution.py:309
  22.7 0.5 %collective-permute-done.6.last_k = bf16[2,128,256]{2,1,0:T(8,128)(2,1)S(1)} collective-permute-done((bf16[2,128,256]{2,1,0:T(8,128)(2,1)S(1)}, bf16[2,128,256]{2,1,0:T(8,128)(2,1)S(1)}, u32[]{:S(2)}, u32[]{:S(2)}) %collective-permute-start.6) | collective-permute-done | bytes 131104 | tf_op jit(solution)/shard_map/ppermute | solution.py:357
  23.2 1.4 %collective-permute-done.7.last_p = bf16[2,128,256]{2,1,0:T(8,128)(2,1)S(1)} collective-permute-done((bf16[2,128,256]{2,1,0:T(8,128)(2,1)S(1)}, bf16[2,128,256]{2,1,0:T(8,128)(2,1)S(1)}, u32[]{:S(2)}, u32[]{:S(2)}) %collective-permute-start.7) | collective-permute-done | bytes 131104 | tf_op jit(solution)/shard_map/ppermute | solution.py:357
  24.6 0.0 copy-done.1
  24.6 0.0 copy-done.3
  24.6 1.1 %commutator.1 = f32[2,128,256]{2,1,0:T(8,128)} custom-call(f32[2,128,256]{2,1,0:T(8,128)S(1)} %copy-done.3, bf16[8,256,256]{2,1,0:T(8,128)(2,1)S(1)} %copy-done.1, f32[256,256]{1,0:T(8,128)S(1)} %shares_product.1.middle, bf16[2,128,256]{2,1,0:T(8,128)(2,1)S(1)} %collective-permute-done.6.last_k, bf16[2,128,256]{2,1,0:T(8,128)(2,1)S(1)} %collective-permute-done.7.last_p, ...), custom_call_target="tpu_custom_call" | custom-call | tf_op jit(solution)/shard_map/commutator/pallas_call | solution.py:376
  (1 shorter events, 0.0 us)
Async XLA Ops:
  1.7 18.6 %copy-start.2 = (bf16[4,128,256]{2,1,0:T(8,128)(2,1)S(1)}, bf16[4,128,256]{2,1,0:T(8,128)(2,1)}, u32[]{:S(2)}) copy-start(bf16[4,128,256]{2,1,0:T(8,128)(2,1)} %mask_strip.1.strip.own) | copy-start | bytes 786436
  1.7 12.3 %collective-permute-start = (bf16[4,128,256]{2,1,0:T(8,128)(2,1)}, bf16[4,128,256]{2,1,0:T(8,128)(2,1)S(1)}, u32[]{:S(2)}, u32[]{:S(2)}) collective-permute-start(bf16[4,128,256]{2,1,0:T(8,128)(2,1)} %mask_strip.1.strip.own), channel_id=1, source_target_pairs={{0,4},{4,8},{8,12},{12,0},{1,5},{5,9},{9,13},{13,1},{2,6},{6,10},{... | collective-permute-start | bytes 786440 | tf_op jit(solution)/shard_map/ppermute | solution.py:356
  6.6 12.2 %collective-permute-start.2 = (bf16[2,256,256]{2,1,0:T(8,128)(2,1)}, bf16[2,256,256]{2,1,0:T(8,128)(2,1)S(1)}, u32[]{:S(2)}, u32[]{:S(2)}) collective-permute-start(bf16[2,256,256]{2,1,0:T(8,128)(2,1)} %get-tuple-element.17), channel_id=1, source_target_pairs={{0,16},{16,0},{1,17},{17,1},{2,18},{18,2},{3,19},{19,3},{4,20},{20... | collective-permute-start | bytes 786440 | tf_op jit(solution)/shard_map/ppermute | solution.py:366
  8.2 12.1 %collective-permute-start.3 = (bf16[2,256,256]{2,1,0:T(8,128)(2,1)}, bf16[2,256,256]{2,1,0:T(8,128)(2,1)S(1)}, u32[]{:S(2)}, u32[]{:S(2)}) collective-permute-start(bf16[2,256,256]{2,1,0:T(8,128)(2,1)} %get-tuple-element.18), channel_id=1, source_target_pairs={{0,16},{16,0},{1,17},{17,1},{2,18},{18,2},{3,19},{19,3},{4,20},{20... | collective-permute-start | bytes 786440 | tf_op jit(solution)/shard_map/ppermute | solution.py:366
  8.7 11.6 %collective-permute-start.1 = (bf16[4,128,256]{2,1,0:T(8,128)(2,1)}, bf16[4,128,256]{2,1,0:T(8,128)(2,1)S(1)}, u32[]{:S(2)}, u32[]{:S(2)}) collective-permute-start(bf16[4,128,256]{2,1,0:T(8,128)(2,1)} %mask_strip.1.strip.own), channel_id=1, source_target_pairs={{0,12},{4,0},{8,4},{12,8},{1,13},{5,1},{9,5},{13,9},{2,14},{6,2},{... | collective-permute-start | bytes 786440 | tf_op jit(solution)/shard_map/ppermute | solution.py:359
  14.1 9.1 %collective-permute-start.6 = (bf16[2,128,256]{2,1,0:T(8,128)(2,1)S(1)}, bf16[2,128,256]{2,1,0:T(8,128)(2,1)S(1)}, u32[]{:S(2)}, u32[]{:S(2)}) collective-permute-start(bf16[2,128,256]{2,1,0:T(8,128)(2,1)S(1)} %get-tuple-element.19), channel_id=1, source_target_pairs={{0,4},{4,8},{8,12},{12,0},{1,5},{5,9},{9,13},{13,1},{2,6},{6,10},{... | collective-permute-start | bytes 393224 | tf_op jit(solution)/shard_map/ppermute | solution.py:357
  14.1 10.4 %collective-permute-start.7 = (bf16[2,128,256]{2,1,0:T(8,128)(2,1)S(1)}, bf16[2,128,256]{2,1,0:T(8,128)(2,1)S(1)}, u32[]{:S(2)}, u32[]{:S(2)}) collective-permute-start(bf16[2,128,256]{2,1,0:T(8,128)(2,1)S(1)} %get-tuple-element.20), channel_id=1, source_target_pairs={{0,4},{4,8},{8,12},{12,0},{1,5},{5,9},{9,13},{13,1},{2,6},{6,10},{... | collective-permute-start | bytes 393224 | tf_op jit(solution)/shard_map/ppermute | solution.py:357
  18.8 3.4 %collective-permute-start.4 = (bf16[2,256,256]{2,1,0:T(8,128)(2,1)S(1)}, bf16[2,256,256]{2,1,0:T(8,128)(2,1)S(1)}, u32[]{:S(2)}, u32[]{:S(2)}) collective-permute-start(bf16[2,256,256]{2,1,0:T(8,128)(2,1)S(1)} %collective-permute-done.2.refs_0_), channel_id=1, source_target_pairs={{0,1},{1,0},{2,3},{3,2},{4,5},{5,4},{6,7},{7,6},{8,9},{9,8},{10,11... | collective-permute-start | bytes 786440 | tf_op jit(solution)/shard_map/ppermute | solution.py:370
  20.3 1.9 %collective-permute-start.5 = (bf16[2,256,256]{2,1,0:T(8,128)(2,1)S(1)}, bf16[2,256,256]{2,1,0:T(8,128)(2,1)S(1)}, u32[]{:S(2)}, u32[]{:S(2)}) collective-permute-start(bf16[2,256,256]{2,1,0:T(8,128)(2,1)S(1)} %collective-permute-done.3.refs_1_), channel_id=1, source_target_pairs={{0,1},{1,0},{2,3},{3,2},{4,5},{5,4},{6,7},{7,6},{8,9},{9,8},{10,11... | collective-permute-start | bytes 786440 | tf_op jit(solution)/shard_map/ppermute | solution.py:370
  20.3 1.2 %copy-start = (bf16[8,256,256]{2,1,0:T(8,128)(2,1)S(1)}, bf16[8,256,256]{2,1,0:T(8,128)(2,1)}, u32[]{:S(2)}) copy-start(bf16[8,256,256]{2,1,0:T(8,128)(2,1)} %get-tuple-element.14.near) | copy-start | bytes 3145732
  22.2 2.4 %copy-start.1 = (bf16[8,256,256]{2,1,0:T(8,128)(2,1)S(1)}, bf16[8,256,256]{2,1,0:T(8,128)(2,1)}, u32[]{:S(2)}) copy-start(bf16[8,256,256]{2,1,0:T(8,128)(2,1)} %get-tuple-element.14.near) | copy-start | bytes 3145732
  22.2 2.4 %copy-start.3 = (f32[2,128,256]{2,1,0:T(8,128)S(1)}, f32[2,128,256]{2,1,0:T(8,128)}, u32[]{:S(2)}) copy-start(f32[2,128,256]{2,1,0:T(8,128)} %get-tuple-element.13.damp) | copy-start | bytes 786436

commit v10 on v9

--- a/solution.py
+++ b/solution.py
@@ -120,7 +120,6 @@
     here, width = held.shape[1:]
     out_rows = damp.shape[1]
     row, col, layer = (lax.axis_index(a) for a in ("row", "col", "depth"))
-    small = fetch_masks((k_mask, p_mask), masks, small_sems)
     copies = [
         pltpu.make_async_copy(ref, held.at[pl.ds(2 * i, 2)], sems.at[i])
         for i, ref in enumerate((p_ref, k_ref))
@@ -134,6 +133,7 @@
     ]
     for copy in copies + [own_copy] + tables:
         copy.start()
+    small = fetch_masks((k_mask, p_mask), masks, small_sems)
     for copy in small + copies:
         copy.wait()
     out_copies = []

time: 25.9 us -> 25.9 us (level)
  no operation moved by 1% of the time
where the time goes in v10:
time: 25.9 us; the launch traced here: 25.7 us
  starting transfers between devices  12 us (46%)
  Pallas kernels  8.78 us (34%)
  waiting for transfers between devices  3.56 us (14%)
  local copies, waits for them, and re-layouts  1.23 us (5%)
    ppermute x2, starting transfers between devices, body(): last = [lax.ppermute(half, 'col', up) for half in relay(ups[-1])]  4.75 us
    pallas_call x2, Pallas kernels, mask_rows(): pl.pallas_call(functools.partial(rows_kernel, places), in_specs=[HBM] * 4...  3.53 us
    ppermute x1, starting transfers between devices, body(): ups.append(lax.ppermute(block, 'col', up))  3.08 us
    pallas_call x1, Pallas kernels, local_part(): pl.pallas_call(local_kernel, in_specs=[HBM] * 8, out_specs=[HBM, VMEM], o...  3.02 us
    ppermute x2, starting transfers between devices, body(): got = [lax.ppermute(part, 'row', perm) for part in share]  2.09 us
    ppermute x1, starting transfers between devices, body(): lax.ppermute(downs[-1], 'col', [(i, (i - 1) % cols_n) for i in range(cols...  2.05 us
    ppermute x2, waiting for transfers between devices, body(): last = [lax.ppermute(half, 'col', up) for half in relay(ups[-1])]  1.86 us
    ppermute x2, waiting for transfers between devices, body(): got = [lax.ppermute(part, 'row', perm) for part in share]  1.46 us
  transfers between devices with their start and end apart: 8, of which 4 were waited for; matrix products, arithmetic and copies ran while one was open for 0% of the time, Pallas kernels for 23%

profile of v10, /device:TPU:0, one launch (start us, length us, event | category | flops | bytes accessed | tf_op | source)
XLA Modules:
  0.0 25.7 jit_solution(15215838253093293729)
XLA Ops:
  0.0 1.7 %mask_strip.1.strip.own = bf16[4,128,256]{2,1,0:T(8,128)(2,1)} custom-call(s32[4,8]{1,0:T(4,128)} %bitcast.2, s32[4,8]{1,0:T(4,128)} %bitcast.5, bf16[2,512,256]{2,1,0:T(8,128)(2,1)} %second_ref.3, bf16[2,512,256]{2,1,0:T(8,128)(2,1)} %first_ref.3), custom_call_target="tpu_custom_call" | custom-call | tf_op jit(solution)/shard_map/mask_strip/pallas_call | solution.py:81
  1.7 0.0 copy-start.2
  1.7 3.1 %collective-permute-start = (bf16[4,128,256]{2,1,0:T(8,128)(2,1)}, bf16[4,128,256]{2,1,0:T(8,128)(2,1)S(1)}, u32[]{:S(2)}, u32[]{:S(2)}) collective-permute-start(bf16[4,128,256]{2,1,0:T(8,128)(2,1)} %mask_strip.1.strip.own), channel_id=1, source_target_pairs={{0,4},{4,8},{8,12},{12,0},{1,5},{5,9},{9,13},{13,1},{2,6},{6,10},{... | collective-permute-start | bytes 786440 | tf_op jit(solution)/shard_map/ppermute | solution.py:356
  4.8 1.8 %mask_share.1 = (bf16[2,256,256]{2,1,0:T(8,128)(2,1)}, bf16[2,256,256]{2,1,0:T(8,128)(2,1)}) custom-call(s32[4,8]{1,0:T(4,128)} %bitcast.6, s32[4,8]{1,0:T(4,128)} %bitcast.3, bf16[2,512,256]{2,1,0:T(8,128)(2,1)} %first_ref.3, bf16[2,512,256]{2,1,0:T(8,128)(2,1)} %second_ref.3), custom_call_target="tpu_custom_call" | custom-call | tf_op jit(solution)/shard_map/mask_share/pallas_call | solution.py:81
  6.6 1.6 %collective-permute-start.2 = (bf16[2,256,256]{2,1,0:T(8,128)(2,1)}, bf16[2,256,256]{2,1,0:T(8,128)(2,1)S(1)}, u32[]{:S(2)}, u32[]{:S(2)}) collective-permute-start(bf16[2,256,256]{2,1,0:T(8,128)(2,1)} %get-tuple-element.17), channel_id=1, source_target_pairs={{0,16},{16,0},{1,17},{17,1},{2,18},{18,2},{3,19},{19,3},{4,20},{20... | collective-permute-start | bytes 786440 | tf_op jit(solution)/shard_map/ppermute | solution.py:366
  8.2 0.5 %collective-permute-start.3 = (bf16[2,256,256]{2,1,0:T(8,128)(2,1)}, bf16[2,256,256]{2,1,0:T(8,128)(2,1)S(1)}, u32[]{:S(2)}, u32[]{:S(2)}) collective-permute-start(bf16[2,256,256]{2,1,0:T(8,128)(2,1)} %get-tuple-element.18), channel_id=1, source_target_pairs={{0,16},{16,0},{1,17},{17,1},{2,18},{18,2},{3,19},{19,3},{4,20},{20... | collective-permute-start | bytes 786440 | tf_op jit(solution)/shard_map/ppermute | solution.py:366
  8.7 2.1 %collective-permute-start.1 = (bf16[4,128,256]{2,1,0:T(8,128)(2,1)}, bf16[4,128,256]{2,1,0:T(8,128)(2,1)S(1)}, u32[]{:S(2)}, u32[]{:S(2)}) collective-permute-start(bf16[4,128,256]{2,1,0:T(8,128)(2,1)} %mask_strip.1.strip.own), channel_id=1, source_target_pairs={{0,12},{4,0},{8,4},{12,8},{1,13},{5,1},{9,5},{13,9},{2,14},{6,2},{... | collective-permute-start | bytes 786440 | tf_op jit(solution)/shard_map/ppermute | solution.py:359
  10.8 3.0 %local_part.1 = (bf16[8,256,256]{2,1,0:T(8,128)(2,1)}, f32[2,128,256]{2,1,0:T(8,128)}) custom-call(s32[4,8]{1,0:T(4,128)} %bitcast.4, s32[4,8]{1,0:T(4,128)} %bitcast.7, s32[16]{0:T(128)} %atoms_ref.1, s32[4,4]{1,0:T(4,128)} %classes_ref.1, f32[4]{0:T(128)} %rates_ref.1, bf16[2,512,256]{2,1,0:T(8,128)(2,1)} %second_ref.3, bf16[2,512,256]{2,1,0:T(8,128)(2,1)} %first_ref.3, ...), custom_call_target="tpu_custom_call" | custom-call | flops 1048576 | bytes 2621440 | tf_op jit(solution)/shard_map/local_part/pallas_call | solution.py:176
  13.8 0.2 collective-permute-done.refs_0_.block
  14.1 0.1 collective-permute-start.6
  14.1 4.7 %collective-permute-start.7 = (bf16[2,128,256]{2,1,0:T(8,128)(2,1)S(1)}, bf16[2,128,256]{2,1,0:T(8,128)(2,1)S(1)}, u32[]{:S(2)}, u32[]{:S(2)}) collective-permute-start(bf16[2,128,256]{2,1,0:T(8,128)(2,1)S(1)} %get-tuple-element.20), channel_id=1, source_target_pairs={{0,4},{4,8},{8,12},{12,0},{1,5},{5,9},{9,13},{13,1},{2,6},{6,10},{... | collective-permute-start | bytes 393224 | tf_op jit(solution)/shard_map/ppermute | solution.py:357
  18.8 0.0 collective-permute-done.2.refs_0_
  18.8 0.0 collective-permute-start.4
  18.8 1.5 %collective-permute-done.3.refs_1_ = bf16[2,256,256]{2,1,0:T(8,128)(2,1)S(1)} collective-permute-done((bf16[2,256,256]{2,1,0:T(8,128)(2,1)}, bf16[2,256,256]{2,1,0:T(8,128)(2,1)S(1)}, u32[]{:S(2)}, u32[]{:S(2)}) %collective-permute-start.3) | collective-permute-done | bytes 262176 | tf_op jit(solution)/shard_map/ppermute | solution.py:366
  20.3 0.0 collective-permute-start.5
  20.3 0.0 collective-permute-done.1.refs_1_
  20.3 0.0 copy-done.2
  20.3 0.0 copy-start
  20.3 1.2 %copy-done = bf16[8,256,256]{2,1,0:T(8,128)(2,1)S(1)} copy-done((bf16[8,256,256]{2,1,0:T(8,128)(2,1)S(1)}, bf16[8,256,256]{2,1,0:T(8,128)(2,1)}, u32[]{:S(2)}) %copy-start) | copy-done | bytes 1048600
  21.5 0.7 %early_product.1 = (bf16[256,4096]{1,0:T(8,128)(2,1)S(1)}, f32[256,256]{1,0:T(8,128)S(1)}) custom-call(bf16[8,256,256]{2,1,0:T(8,128)(2,1)S(1)} %copy-done, bf16[4,128,256]{2,1,0:T(8,128)(2,1)S(1)} %copy-done.2, bf16[4,128,256]{2,1,0:T(8,128)(2,1)S(1)} %collective-permute-done.refs_0_.block, bf16[4,128,256]{2,1,0:T(8,128)(2,1)S(1)} %collective-permute-done.1.refs_1_), custom_call_target="tpu_custom_call" | custom-call | flops 10737418240 | bytes 4194304 | tf_op jit(solution)/shard_map/early_product/pallas_call | solution.py:277
  22.2 0.0 copy-start.1
  22.2 0.0 copy-start.3
  22.2 0.0 collective-permute-done.4.refs_2_
  22.2 0.0 collective-permute-done.5.refs_3_
  22.3 0.5 %shares_product.1.middle = f32[256,256]{1,0:T(8,128)S(1)} custom-call(bf16[256,4096]{1,0:T(8,128)(2,1)S(1)} %get-tuple-element.15.left, f32[256,256]{1,0:T(8,128)S(1)} %get-tuple-element.16.early, bf16[2,256,256]{2,1,0:T(8,128)(2,1)S(1)} %collective-permute-done.2.refs_0_, bf16[2,256,256]{2,1,0:T(8,128)(2,1)S(1)} %collective-permute-done.3.refs_1_, ...), custom_call_target="tpu_custom_call" | custom-call | flops 1000000 | bytes 1000000 | tf_op jit(solution)/shard_map/shares_product/pallas_call | solution.py:309
  22.7 0.5 %collective-permute-done.6.last_k = bf16[2,128,256]{2,1,0:T(8,128)(2,1)S(1)} collective-permute-done((bf16[2,128,256]{2,1,0:T(8,128)(2,1)S(1)}, bf16[2,128,256]{2,1,0:T(8,128)(2,1)S(1)}, u32[]{:S(2)}, u32[]{:S(2)}) %collective-permute-start.6) | collective-permute-done | bytes 131104 | tf_op jit(solution)/shard_map/ppermute | solution.py:357
  23.2 1.4 %collective-permute-done.7.last_p = bf16[2,128,256]{2,1,0:T(8,128)(2,1)S(1)} collective-permute-done((bf16[2,128,256]{2,1,0:T(8,128)(2,1)S(1)}, bf16[2,128,256]{2,1,0:T(8,128)(2,1)S(1)}, u32[]{:S(2)}, u32[]{:S(2)}) %collective-permute-start.7) | collective-permute-done | bytes 131104 | tf_op jit(solution)/shard_map/ppermute | solution.py:357
  24.6 0.0 copy-done.1
  24.6 0.0 copy-done.3
  24.6 1.1 %commutator.1 = f32[2,128,256]{2,1,0:T(8,128)} custom-call(f32[2,128,256]{2,1,0:T(8,128)S(1)} %copy-done.3, bf16[8,256,256]{2,1,0:T(8,128)(2,1)S(1)} %copy-done.1, f32[256,256]{1,0:T(8,128)S(1)} %shares_product.1.middle, bf16[2,128,256]{2,1,0:T(8,128)(2,1)S(1)} %collective-permute-done.6.last_k, bf16[2,128,256]{2,1,0:T(8,128)(2,1)S(1)} %collective-permute-done.7.last_p, ...), custom_call_target="tpu_custom_call" | custom-call | tf_op jit(solution)/shard_map/commutator/pallas_call | solution.py:376
  (1 shorter events, 0.0 us)
Async XLA Ops:
  1.7 18.6 %copy-start.2 = (bf16[4,128,256]{2,1,0:T(8,128)(2,1)S(1)}, bf16[4,128,256]{2,1,0:T(8,128)(2,1)}, u32[]{:S(2)}) copy-start(bf16[4,128,256]{2,1,0:T(8,128)(2,1)} %mask_strip.1.strip.own) | copy-start | bytes 786436
  1.7 12.3 %collective-permute-start = (bf16[4,128,256]{2,1,0:T(8,128)(2,1)}, bf16[4,128,256]{2,1,0:T(8,128)(2,1)S(1)}, u32[]{:S(2)}, u32[]{:S(2)}) collective-permute-start(bf16[4,128,256]{2,1,0:T(8,128)(2,1)} %mask_strip.1.strip.own), channel_id=1, source_target_pairs={{0,4},{4,8},{8,12},{12,0},{1,5},{5,9},{9,13},{13,1},{2,6},{6,10},{... | collective-permute-start | bytes 786440 | tf_op jit(solution)/shard_map/ppermute | solution.py:356
  6.6 12.2 %collective-permute-start.2 = (bf16[2,256,256]{2,1,0:T(8,128)(2,1)}, bf16[2,256,256]{2,1,0:T(8,128)(2,1)S(1)}, u32[]{:S(2)}, u32[]{:S(2)}) collective-permute-start(bf16[2,256,256]{2,1,0:T(8,128)(2,1)} %get-tuple-element.17), channel_id=1, source_target_pairs={{0,16},{16,0},{1,17},{17,1},{2,18},{18,2},{3,19},{19,3},{4,20},{20... | collective-permute-start | bytes 786440 | tf_op jit(solution)/shard_map/ppermute | solution.py:366
  8.2 12.1 %collective-permute-start.3 = (bf16[2,256,256]{2,1,0:T(8,128)(2,1)}, bf16[2,256,256]{2,1,0:T(8,128)(2,1)S(1)}, u32[]{:S(2)}, u32[]{:S(2)}) collective-permute-start(bf16[2,256,256]{2,1,0:T(8,128)(2,1)} %get-tuple-element.18), channel_id=1, source_target_pairs={{0,16},{16,0},{1,17},{17,1},{2,18},{18,2},{3,19},{19,3},{4,20},{20... | collective-permute-start | bytes 786440 | tf_op jit(solution)/shard_map/ppermute | solution.py:366
  8.7 11.6 %collective-permute-start.1 = (bf16[4,128,256]{2,1,0:T(8,128)(2,1)}, bf16[4,128,256]{2,1,0:T(8,128)(2,1)S(1)}, u32[]{:S(2)}, u32[]{:S(2)}) collective-permute-start(bf16[4,128,256]{2,1,0:T(8,128)(2,1)} %mask_strip.1.strip.own), channel_id=1, source_target_pairs={{0,12},{4,0},{8,4},{12,8},{1,13},{5,1},{9,5},{13,9},{2,14},{6,2},{... | collective-permute-start | bytes 786440 | tf_op jit(solution)/shard_map/ppermute | solution.py:359
  14.1 9.1 %collective-permute-start.6 = (bf16[2,128,256]{2,1,0:T(8,128)(2,1)S(1)}, bf16[2,128,256]{2,1,0:T(8,128)(2,1)S(1)}, u32[]{:S(2)}, u32[]{:S(2)}) collective-permute-start(bf16[2,128,256]{2,1,0:T(8,128)(2,1)S(1)} %get-tuple-element.19), channel_id=1, source_target_pairs={{0,4},{4,8},{8,12},{12,0},{1,5},{5,9},{9,13},{13,1},{2,6},{6,10},{... | collective-permute-start | bytes 393224 | tf_op jit(solution)/shard_map/ppermute | solution.py:357
  14.1 10.4 %collective-permute-start.7 = (bf16[2,128,256]{2,1,0:T(8,128)(2,1)S(1)}, bf16[2,128,256]{2,1,0:T(8,128)(2,1)S(1)}, u32[]{:S(2)}, u32[]{:S(2)}) collective-permute-start(bf16[2,128,256]{2,1,0:T(8,128)(2,1)S(1)} %get-tuple-element.20), channel_id=1, source_target_pairs={{0,4},{4,8},{8,12},{12,0},{1,5},{5,9},{9,13},{13,1},{2,6},{6,10},{... | collective-permute-start | bytes 393224 | tf_op jit(solution)/shard_map/ppermute | solution.py:357
  18.8 3.4 %collective-permute-start.4 = (bf16[2,256,256]{2,1,0:T(8,128)(2,1)S(1)}, bf16[2,256,256]{2,1,0:T(8,128)(2,1)S(1)}, u32[]{:S(2)}, u32[]{:S(2)}) collective-permute-start(bf16[2,256,256]{2,1,0:T(8,128)(2,1)S(1)} %collective-permute-done.2.refs_0_), channel_id=1, source_target_pairs={{0,1},{1,0},{2,3},{3,2},{4,5},{5,4},{6,7},{7,6},{8,9},{9,8},{10,11... | collective-permute-start | bytes 786440 | tf_op jit(solution)/shard_map/ppermute | solution.py:370
  20.3 1.9 %collective-permute-start.5 = (bf16[2,256,256]{2,1,0:T(8,128)(2,1)S(1)}, bf16[2,256,256]{2,1,0:T(8,128)(2,1)S(1)}, u32[]{:S(2)}, u32[]{:S(2)}) collective-permute-start(bf16[2,256,256]{2,1,0:T(8,128)(2,1)S(1)} %collective-permute-done.3.refs_1_), channel_id=1, source_target_pairs={{0,1},{1,0},{2,3},{3,2},{4,5},{5,4},{6,7},{7,6},{8,9},{9,8},{10,11... | collective-permute-start | bytes 786440 | tf_op jit(solution)/shard_map/ppermute | solution.py:370
  20.3 1.2 %copy-start = (bf16[8,256,256]{2,1,0:T(8,128)(2,1)S(1)}, bf16[8,256,256]{2,1,0:T(8,128)(2,1)}, u32[]{:S(2)}) copy-start(bf16[8,256,256]{2,1,0:T(8,128)(2,1)} %get-tuple-element.14.near) | copy-start | bytes 3145732
  22.2 2.4 %copy-start.1 = (bf16[8,256,256]{2,1,0:T(8,128)(2,1)S(1)}, bf16[8,256,256]{2,1,0:T(8,128)(2,1)}, u32[]{:S(2)}) copy-start(bf16[8,256,256]{2,1,0:T(8,128)(2,1)} %get-tuple-element.14.near) | copy-start | bytes 3145732
  22.2 2.4 %copy-start.3 = (f32[2,128,256]{2,1,0:T(8,128)S(1)}, f32[2,128,256]{2,1,0:T(8,128)}, u32[]{:S(2)}) copy-start(f32[2,128,256]{2,1,0:T(8,128)} %get-tuple-element.13.damp) | copy-start | bytes 786436
